TPU v7x, 512 devices: a whole 4x4x16 slice. The times are simulated.
512 devices in a mesh: seq: 64 (over z, y), head: 8 (over x, core).
Axes of the slice: x: 4, y: 4, z: 16, core: 2. Of those that a mesh axis runs over, the one named last changes fastest.
Arguments:
- queries: bfloat16 [49152, 2048], P('seq', 'head'), may hold values from -20 to 20
- keys: bfloat16 [49152, 2048], P('seq', 'head'), may hold values from -45 to 45
- values: bfloat16 [49152, 2048], P('seq', 'head'), may hold values from -6 to 6
- cluster_ids: int32 [16, 49152], P('head', 'seq'), may hold values from 0 to 511, as said below
- out_weight: bfloat16 [2048, 2048], P('head'), may hold values from -0.125 to 0.125
Outputs:
- attended: bfloat16 [49152, 2048], P(('seq', 'head'))
- key_sums: float32 [512, 2048], P('seq', 'head')
Inputs may be any that keep to these rules, and one draw needn't show every extreme that they name: `cluster_ids`: in each head, the 768 tokens of one index of seq name any cluster at most 5 times, and in each head one cluster is named exactly 5 times by the tokens of every index of seq.
All inputs are finite; a program needn't handle non-finite values.
Results may differ from a plain program's by a relative error of at most 0.017.
Values may be sent and summed in bfloat16 or wider, within the bound.
No kernel may reach another device: no remote copies, remote signals or barrier semaphores. Data moves between devices by JAX's collectives and lax.ppermute only.
A program may use at most 64 MiB of HBM per device.

v0:
```python
import math

import jax
import jax.numpy as jnp
from jax import lax
from jax.sharding import PartitionSpec as P

CLUSTERS = 512
MOST = 5


def place_rows(rows, target, lanes, fill_value, lead_shape):
    buffer = jnp.full((CLUSTERS * MOST, rows.shape[1], rows.shape[2]), fill_value, rows.dtype)
    buffer = buffer.at[target, lanes].set(rows)
    return buffer.reshape(lead_shape + (rows.shape[1] * rows.shape[2],))


def unit_rows(key_float):
    return key_float * lax.rsqrt(jnp.sum(key_float * key_float, axis=-1, keepdims=True) + 1e-06)


def body(queries, keys, values, cluster_ids, out_weight):
    heads_local = cluster_ids.shape[0]
    tok_count = cluster_ids.shape[1]
    width = queries.shape[1]
    head_dim = width // heads_local
    seq_count = lax.axis_size("seq")
    owned = CLUSTERS // seq_count
    factor = 1.0 / math.sqrt(head_dim)
    earlier = jnp.arange(tok_count)[:, None] < jnp.arange(tok_count)[None, :]
    same_cluster = cluster_ids[:, :, None] == cluster_ids[:, None, :]
    ranking = jnp.sum(same_cluster & earlier[None], axis=1)
    target = (cluster_ids * MOST + ranking).T
    lanes = jnp.broadcast_to(jnp.arange(heads_local, dtype=jnp.int32)[None, :], target.shape)
    lead_shape = (seq_count, owned, MOST)
    query_send = place_rows(
        queries.reshape(tok_count, heads_local, head_dim), target, lanes, 0.0, lead_shape
    )
    key_send = place_rows(
        keys.reshape(tok_count, heads_local, head_dim), target, lanes, 0.0, lead_shape
    )
    value_send = place_rows(
        values.reshape(tok_count, heads_local, head_dim), target, lanes, 0.0, lead_shape
    )
    local_index = jnp.arange(tok_count, dtype=jnp.int32)
    marks = jnp.stack([local_index // 64, local_index % 64], axis=-1).astype(jnp.bfloat16)
    marks = jnp.broadcast_to(marks[:, None, :], (tok_count, heads_local, 2))
    mark_send = place_rows(marks, target, lanes, -1.0, lead_shape)
    query_part = lax.all_to_all(query_send, "seq", split_axis=0, concat_axis=0, tiled=True)
    key_part = lax.all_to_all(key_send, "seq", split_axis=0, concat_axis=0, tiled=True)
    value_part = lax.all_to_all(value_send, "seq", split_axis=0, concat_axis=0, tiled=True)
    mark_part = lax.all_to_all(mark_send, "seq", split_axis=0, concat_axis=0, tiled=True)
    sources = query_part.shape[0]
    count_items = query_part.shape[1]
    rows_all = sources * MOST
    query_six = query_part.reshape(sources, count_items, MOST, heads_local, head_dim)
    key_six = key_part.reshape(sources, count_items, MOST, heads_local, head_dim)
    value_six = value_part.reshape(sources, count_items, MOST, heads_local, head_dim)
    mark_int = mark_part.reshape(sources, count_items, MOST, heads_local, 2).astype(jnp.int32)
    anchor = jnp.arange(sources, dtype=jnp.int32)[:, None, None, None]
    places = jnp.where(
        mark_int[..., 0] >= 0, anchor * tok_count + mark_int[..., 0] * 64 + mark_int[..., 1], -1
    )

    def one_item(item):
        query_item, key_item, value_item, place_item = item
        place_flat = place_item.transpose(2, 0, 1).reshape(heads_local, rows_all)
        scores = jnp.einsum(
            "smhd,tnhd->hsmtn", query_item, key_item, preferred_element_type=jnp.float32
        )
        scores = scores.reshape(heads_local, rows_all, rows_all) * factor
        allowed = (place_flat[:, None, :] >= 0) & (place_flat[:, None, :] <= place_flat[:, :, None])
        scores = jnp.where(allowed, scores, -1e30)
        highest = jnp.max(scores, axis=-1, keepdims=True)
        raised = jnp.exp(scores - highest)
        weights = (raised / jnp.sum(raised, axis=-1, keepdims=True)).astype(jnp.bfloat16)
        weights = weights.reshape(heads_local, sources, MOST, sources, MOST)
        result = jnp.einsum(
            "hsmtn,tnhd->smhd", weights, value_item, preferred_element_type=jnp.float32
        )
        return result.astype(jnp.bfloat16).reshape(sources, MOST, heads_local * head_dim)

    items = (
        jnp.moveaxis(query_six, 1, 0),
        jnp.moveaxis(key_six, 1, 0),
        jnp.moveaxis(value_six, 1, 0),
        jnp.moveaxis(places, 1, 0),
    )
    outputs = jnp.moveaxis(lax.map(one_item, items), 0, 1)
    returned = lax.all_to_all(outputs, "seq", split_axis=0, concat_axis=0, tiled=True)
    routed = returned
    returned = routed
    unit_keys = unit_rows(keys.reshape(tok_count, heads_local, head_dim).astype(jnp.float32))
    member = (
        cluster_ids[:, :, None] == jnp.arange(CLUSTERS, dtype=jnp.int32)[None, None, :]
    ).astype(jnp.float32)
    partial_value = jnp.einsum("htc,thd->chd", member, unit_keys, precision=lax.Precision.HIGHEST)
    key_sums = lax.psum_scatter(
        partial_value.reshape(CLUSTERS, heads_local * head_dim),
        "seq",
        scatter_dimension=0,
        tiled=True,
    )
    returned_rows = returned.reshape(CLUSTERS * MOST, heads_local, head_dim)
    head_outputs = returned_rows[target, lanes].reshape(tok_count, width)
    attended = lax.psum_scatter(
        jnp.dot(head_outputs, out_weight, preferred_element_type=jnp.float32).astype(jnp.bfloat16),
        "head",
        scatter_dimension=0,
        tiled=True,
    )
    return (attended, key_sums)


def solution(mesh):
    placed = (
        P("seq", "head"),
        P("seq", "head"),
        P("seq", "head"),
        P("head", "seq"),
        P("head", None),
    )
    return jax.shard_map(
        body,
        mesh=mesh,
        in_specs=placed,
        out_specs=(P(("seq", "head"), None), P("seq", "head")),
        check_vma=False,
    )
```

profile of v0, /device:TPU:1, one launch (start us, length us, event | category | flops | bytes accessed | tf_op | source)
XLA Modules:
  0.0 1076.7 jit_solution(14441516404602621945)
XLA Ops:
  7.4 1.7 convert_reduce_fusion
  12.1 4.9 scatter_custom_fusion.1
  18.0 2.8 copy.68
  20.8 19.3 %all-to-all-start.1 = ((bf16[64,8,5,4]{1,3,2,0:T(4,128)(2,1)}), bf16[64,8,5,4]{1,3,2,0:T(4,128)(2,1)S(1)}, u32[]{:S(2)}, u32[]{:S(2)}) async-start(bf16[64,8,5,4]{1,3,2,0:T(4,128)(2,1)} %copy.68), calls=%async_computation.1 | async-start | bytes 655360 | tf_op jit(solution)/shard_map/all_to_all | solution.py:52
  40.2 5.7 scatter_custom_fusion
  45.9 2.5 reshape.195
  48.4 1.5 copy.66
  50.0 12.2 %all-to-all-done.1 = bf16[64,8,5,4]{1,3,2,0:T(4,128)(2,1)S(1)} async-done(((bf16[64,8,5,4]{1,3,2,0:T(4,128)(2,1)}), bf16[64,8,5,4]{1,3,2,0:T(4,128)(2,1)S(1)}, u32[]{:S(2)}, u32[]{:S(2)}) %all-to-all-start.1) | async-done | bytes 20512 | tf_op jit(solution)/shard_map/all_to_all | solution.py:52
  62.9 7.5 all-to-all-start
  70.5 5.7 scatter_custom_fusion.2
  76.2 2.5 reshape.199
  78.8 1.5 copy.71
  80.3 51.3 %all-to-all-done = bf16[64,8,5,256]{3,1,2,0:T(8,128)(2,1)} async-done(((bf16[64,8,5,256]{3,1,2,0:T(8,128)(2,1)}), bf16[64,8,5,256]{3,1,2,0:T(8,128)(2,1)}, u32[]{:S(2)}, u32[]{:S(2)}) %all-to-all-start) | async-done | bytes 1310752 | tf_op jit(solution)/shard_map/all_to_all | solution.py:51
  131.5 9.7 all-to-all-start.2
  141.3 5.7 scatter_custom_fusion.3
  147.1 2.5 reshape.202
  149.6 1.5 copy.72
  151.1 51.2 %all-to-all-done.2 = bf16[64,8,5,256]{3,1,2,0:T(8,128)(2,1)} async-done(((bf16[64,8,5,256]{3,1,2,0:T(8,128)(2,1)}), bf16[64,8,5,256]{3,1,2,0:T(8,128)(2,1)}, u32[]{:S(2)}, u32[]{:S(2)}) %all-to-all-start.2) | async-done | bytes 1310752 | tf_op jit(solution)/shard_map/all_to_all | solution.py:49
  202.3 9.2 all-to-all-start.3
  211.8 2.7 copy.73
  214.5 2.7 copy.75
  217.2 55.7 %all-to-all-done.3 = bf16[64,8,5,256]{3,1,2,0:T(8,128)(2,1)S(1)} async-done(((bf16[64,8,5,256]{3,1,2,0:T(8,128)(2,1)}), bf16[64,8,5,256]{3,1,2,0:T(8,128)(2,1)S(1)}, u32[]{:S(2)}, u32[]{:S(2)}) %all-to-all-start.3) | async-done | bytes 1310752 | tf_op jit(solution)/shard_map/all_to_all | solution.py:50
  273.0 1.4 copy.76
  274.4 34.5 %while.10 = (s32[]{:T(128)}, bf16[8,64,5,256]{3,1,2,0:T(8,128)(2,1)}, bf16[8,64,5,2,128]{4,1,2,3,0:T(8,128)(2,1)}, s32[8,64,5,2]{1,0,3,2:T(8,128)S(1)}, bf16[8,6...) while((s32[]{:T(128)}, bf16[8,64,5,256]{3,1,2,0:T(8,128)(2,1)}, ...), condition=%wide.region_8.9_spmd, body=%wide.region_5.8_spmd.sunk | while | flops 106986880 | bytes 4142801 | solution.py:89
  274.4 1.6 fusion.37
  276.3 1.4 fusion.39
  278.7 1.6 fusion.37
  280.6 1.4 fusion.39
  283.0 1.6 fusion.37
  284.9 1.4 fusion.39
  287.3 1.6 fusion.37
  289.2 1.4 fusion.39
  291.6 1.6 fusion.37
  295.9 1.6 fusion.37
  300.2 1.6 fusion.37
  302.2 1.4 fusion.39
  304.6 1.6 fusion.37
  306.5 1.4 fusion.39
  308.8 3.1 copy.96
  311.9 8.5 all-to-all-start.4
  323.1 1.6 fusion.11
  326.2 56.1 %all-to-all-done.4 = bf16[64,8,5,256]{3,1,2,0:T(8,128)(2,1)S(1)} async-done(((bf16[64,8,5,256]{3,1,2,0:T(8,128)(2,1)}), bf16[64,8,5,256]{3,1,2,0:T(8,128)(2,1)S(1)}, u32[]{:S(2)}, u32[]{:S(2)}) %all-to-all-start.4) | async-done | bytes 1310752 | tf_op jit(solution)/shard_map/all_to_all | solution.py:90
  382.3 1.9 copy.78
  384.2 3.6 reshape.204
  387.8 7.2 gather_fusion
  395.2 2.7 convolution_convert_fusion
  397.8 618.3 %reduce-scatter.5.cloned.1.call-done = f32[8,256]{1,0:T(8,128)} async-done(((f32[512,256]{1,0:T(8,128)}), f32[8,256]{1,0:T(8,128)}) %reduce-scatter.5.cloned.1.call-update) | async-done | bytes 8208 | tf_op jit(solution)/shard_map/reduce_scatter | solution.py:98
  1016.1 53.7 %reduce-scatter.3.cloned.1.call-done = bf16[96,2048]{1,0:T(8,128)(2,1)} async-done(((bf16[768,2048]{1,0:T(8,128)(2,1)}), bf16[96,2048]{1,0:T(8,128)(2,1)}) %reduce-scatter.3.cloned.1.call-update) | async-done | bytes 393232 | tf_op jit(solution)/shard_map/reduce_scatter | solution.py:106
  (105 shorter events, 22.5 us)
Async XLA Ops:
  7.2 388.0 %copy-start = (bf16[256,2048]{1,0:T(8,128)(2,1)S(1)}, bf16[256,2048]{1,0:T(8,128)(2,1)}, u32[]{:S(2)}) copy-start(bf16[256,2048]{1,0:T(8,128)(2,1)} %param.11) | copy-start | bytes 3145732
  18.0 22.1 %copy-start.4 = (bf16[768,256]{1,0:T(8,128)(2,1)S(1)}, bf16[768,256]{1,0:T(8,128)(2,1)}, u32[]{:S(2)}) copy-start(bf16[768,256]{1,0:T(8,128)(2,1)} %param.9) | copy-start | bytes 1179652
  20.8 41.4 %all-to-all-start.1 = ((bf16[64,8,5,4]{1,3,2,0:T(4,128)(2,1)}), bf16[64,8,5,4]{1,3,2,0:T(4,128)(2,1)S(1)}, u32[]{:S(2)}, u32[]{:S(2)}) async-start(bf16[64,8,5,4]{1,3,2,0:T(4,128)(2,1)} %copy.68), calls=%async_computation.1 | async-start | bytes 655360 | tf_op jit(solution)/shard_map/all_to_all | solution.py:52
  50.0 20.4 %copy-start.5 = (bf16[768,256]{1,0:T(8,128)(2,1)S(1)}, bf16[768,256]{1,0:T(8,128)(2,1)}, u32[]{:S(2)}) copy-start(bf16[768,256]{1,0:T(8,128)(2,1)} %param.7) | copy-start | bytes 1179652
  62.1 0.7 copy-start.2
  62.9 68.6 %all-to-all-start = ((bf16[64,8,5,256]{3,1,2,0:T(8,128)(2,1)}), bf16[64,8,5,256]{3,1,2,0:T(8,128)(2,1)}, u32[]{:S(2)}, u32[]{:S(2)}) async-start(bf16[64,8,5,256]{3,1,2,0:T(8,128)(2,1)} %copy.66), calls=%async_computation | async-start | bytes 2621440 | tf_op jit(solution)/shard_map/all_to_all | solution.py:51
  80.3 60.9 %copy-start.1 = (bf16[768,256]{1,0:T(8,128)(2,1)S(1)}, bf16[768,256]{1,0:T(8,128)(2,1)}, u32[]{:S(2)}) copy-start(bf16[768,256]{1,0:T(8,128)(2,1)} %param.8) | copy-start | bytes 1179652
  131.5 70.8 %all-to-all-start.2 = ((bf16[64,8,5,256]{3,1,2,0:T(8,128)(2,1)}), bf16[64,8,5,256]{3,1,2,0:T(8,128)(2,1)}, u32[]{:S(2)}, u32[]{:S(2)}) async-start(bf16[64,8,5,256]{3,1,2,0:T(8,128)(2,1)} %copy.71), calls=%async_computation.2 | async-start | bytes 2621440 | tf_op jit(solution)/shard_map/all_to_all | solution.py:49
  151.1 60.4 %copy-start.3 = (bf16[64,8,5,4]{1,3,2,0:T(4,128)(2,1)S(1)}, bf16[64,8,5,4]{1,3,2,0:T(4,128)(2,1)}, u32[]{:S(2)}) copy-start(bf16[64,8,5,4]{1,3,2,0:T(4,128)(2,1)} %copy-done.2) | copy-start | bytes 61444
  202.3 70.7 %all-to-all-start.3 = ((bf16[64,8,5,256]{3,1,2,0:T(8,128)(2,1)}), bf16[64,8,5,256]{3,1,2,0:T(8,128)(2,1)S(1)}, u32[]{:S(2)}, u32[]{:S(2)}) async-start(bf16[64,8,5,256]{3,1,2,0:T(8,128)(2,1)} %copy.72), calls=%async_computation.3 | async-start | bytes 2621440 | tf_op jit(solution)/shard_map/all_to_all | solution.py:50
  311.9 70.4 %all-to-all-start.4 = ((bf16[64,8,5,256]{3,1,2,0:T(8,128)(2,1)}), bf16[64,8,5,256]{3,1,2,0:T(8,128)(2,1)S(1)}, u32[]{:S(2)}, u32[]{:S(2)}) async-start(bf16[64,8,5,256]{3,1,2,0:T(8,128)(2,1)} %bitcast.102), calls=%async_computation.4 | async-start | bytes 2621440 | tf_op jit(solution)/shard_map/all_to_all | solution.py:90
  320.5 695.6 %reduce-scatter.5.cloned.1.call-start = ((), (), s32[]{:S(2)}) async-start(), calls=%async_computation.8 | async-start | bytes 532480 | tf_op jit(solution)/shard_map/reduce_scatter | solution.py:98
  322.0 1.1 copy-start.6
  325.8 744.1 %reduce-scatter.3.cloned.1.call-start = ((), (), s32[]{:S(2)}) async-start(), calls=%async_computation.7 | async-start | bytes 3538944 | tf_op jit(solution)/shard_map/reduce_scatter | solution.py:106
Sparse Core Ops, SparseCore 0:
  326.3 689.8 reduce-scatter.4
  1019.8 50.0 reduce-scatter.2
where the time goes:
time: 1080 us
  waiting for transfers between devices  898 us (83%)
  local copies, waits for them, and re-layouts  72.3 us (7%)
  starting transfers between devices  54.5 us (5%)
  matrix products  28.3 us (3%)
  between operations  14.4 us (1%)
    reduce_scatter x1, waiting for transfers between devices, body(): lax.psum_scatter(partial_value.reshape(CLUSTERS, heads_local * head_dim),...  618 us
    all_to_all x1, waiting for transfers between devices, body(): lax.all_to_all(outputs, 'seq', split_axis=0, concat_axis=0, tiled=True)  56.1 us
    all_to_all x1, waiting for transfers between devices, body(): lax.all_to_all(key_send, 'seq', split_axis=0, concat_axis=0, tiled=True)  55.7 us
    reduce_scatter x1, waiting for transfers between devices, body(): lax.psum_scatter(jnp.dot(head_outputs, out_weight, preferred_element_type...  53.7 us
    all_to_all x1, waiting for transfers between devices, body(): lax.all_to_all(value_send, 'seq', split_axis=0, concat_axis=0, tiled=True)  51.3 us
    all_to_all x1, waiting for transfers between devices, body(): lax.all_to_all(query_send, 'seq', split_axis=0, concat_axis=0, tiled=True)  51.2 us
    unnamed x20, local copies, waits for them, and re-layouts  23.2 us
  transfers between devices with their start and end apart: 7, of which 7 were waited for; matrix products, arithmetic and copies ran while one was open for 5% of the time, Pallas kernels for 0%

commit v1 on v0

v1 whole, which is shorter than its diff:
```python
import functools
import math

import jax
import jax.numpy as jnp
from jax import lax
from jax.experimental import pallas as pl
from jax.experimental.pallas import tpu as pltpu
from jax.sharding import PartitionSpec as P

CLUSTERS = 512
MOST = 5
TILE = 256
VMEM = 48 * 1024 * 1024


def pack_kernel(place_ref, q_ref, k_ref, v_ref, out_ref):
    rows, toks = out_ref.shape[0], q_ref.shape[0]
    base = pl.program_id(0) * rows
    wanted = lax.broadcasted_iota(jnp.int32, (rows, toks), 0) + base
    pick = jnp.where(wanted == place_ref[0:1, :], 1.0, 0.0).astype(jnp.bfloat16)
    for part, ref in enumerate((q_ref, k_ref, v_ref)):
        width = ref.shape[1]
        moved = jnp.dot(pick, ref[...], preferred_element_type=jnp.float32)
        out_ref[:, part * width : (part + 1) * width] = moved.astype(out_ref.dtype)


def pack(place, queries, keys, values, head, head_dim, rows_all):
    toks = queries.shape[0]
    tile = 512
    column = pl.BlockSpec((toks, head_dim), lambda i: (0, head))
    return pl.pallas_call(
        pack_kernel,
        grid=(rows_all // tile,),
        in_specs=[pl.BlockSpec((1, toks), lambda i: (0, 0)), column, column, column],
        out_specs=pl.BlockSpec((tile, 3 * head_dim), lambda i: (i, 0)),
        out_shape=jax.ShapeDtypeStruct((rows_all, 3 * head_dim), queries.dtype),
        compiler_params=pltpu.CompilerParams(vmem_limit_bytes=VMEM),
        cost_estimate=pl.CostEstimate(
            flops=6 * rows_all * toks * head_dim,
            bytes_accessed=rows_all * head_dim * 6,
            transcendentals=0,
        ),
    )(place[None, :], queries, keys, values)


def attend_kernel(room, ends_ref, ends_t_ref, x_ref, out_ref, sums_ref):
    rows, width = out_ref.shape
    sources, owned = ends_ref.shape
    factor = 1.0 / math.sqrt(width)
    spread = jnp.where(
        lax.broadcasted_iota(jnp.int32, (sources, rows), 1) // room
        == lax.broadcasted_iota(jnp.int32, (sources, rows), 0),
        1.0,
        0.0,
    ).astype(jnp.bfloat16)
    ends_row = jnp.dot(
        ends_t_ref[...].astype(jnp.bfloat16), spread, preferred_element_type=jnp.float32
    )
    slot_row = (lax.broadcasted_iota(jnp.int32, (owned, rows), 1) % room).astype(jnp.float32)
    id_row = jnp.sum(jnp.where(ends_row <= slot_row, 1.0, 0.0), axis=0, keepdims=True)
    spread_col = jnp.where(
        lax.broadcasted_iota(jnp.int32, (rows, sources), 0) // room
        == lax.broadcasted_iota(jnp.int32, (rows, sources), 1),
        1.0,
        0.0,
    ).astype(jnp.bfloat16)
    ends_col = jnp.dot(
        spread_col, ends_ref[...].astype(jnp.bfloat16), preferred_element_type=jnp.float32
    )
    slot_col = (lax.broadcasted_iota(jnp.int32, (rows, owned), 0) % room).astype(jnp.float32)
    id_col = jnp.sum(jnp.where(ends_col <= slot_col, 1.0, 0.0), axis=1, keepdims=True)

    key_float = x_ref[:, width : 2 * width].astype(jnp.float32)
    unit = key_float * lax.rsqrt(jnp.sum(key_float * key_float, axis=1, keepdims=True) + 1e-06)
    high = unit.astype(jnp.bfloat16)
    low = (unit - high.astype(jnp.float32)).astype(jnp.bfloat16)
    member = jnp.where(
        lax.broadcasted_iota(jnp.int32, (owned, rows), 0).astype(jnp.float32) == id_row, 1.0, 0.0
    ).astype(jnp.bfloat16)
    sums_ref[...] = jnp.dot(member, high, preferred_element_type=jnp.float32) + jnp.dot(
        member, low, preferred_element_type=jnp.float32
    )

    for begin in range(0, rows, TILE):
        end = begin + TILE
        query = x_ref[begin:end, 0:width]
        scores = lax.dot_general(
            query,
            x_ref[0:end, width : 2 * width],
            (((1,), (1,)), ((), ())),
            preferred_element_type=jnp.float32,
        )
        allowed = (id_col[begin:end] == id_row[:, 0:end]) & (
            lax.broadcasted_iota(jnp.int32, (TILE, end), 1)
            <= lax.broadcasted_iota(jnp.int32, (TILE, end), 0) + begin
        )
        scores = jnp.where(allowed, scores * factor, -1e30)
        highest = jnp.max(scores, axis=1, keepdims=True)
        raised = jnp.exp(scores - highest)
        total = jnp.sum(raised, axis=1, keepdims=True)
        result = jnp.dot(
            raised.astype(jnp.bfloat16),
            x_ref[0:end, 2 * width : 3 * width],
            preferred_element_type=jnp.float32,
        )
        out_ref[begin:end] = (result / total).astype(out_ref.dtype)


def attend(ends, received, room, head_dim):
    rows = received.shape[0]
    owned = ends.shape[1]
    return pl.pallas_call(
        functools.partial(attend_kernel, room),
        out_shape=(
            jax.ShapeDtypeStruct((rows, head_dim), received.dtype),
            jax.ShapeDtypeStruct((owned, head_dim), jnp.float32),
        ),
        compiler_params=pltpu.CompilerParams(vmem_limit_bytes=VMEM),
        cost_estimate=pl.CostEstimate(
            flops=2 * rows * rows * head_dim,
            bytes_accessed=rows * head_dim * 8,
            transcendentals=rows * rows // 2,
        ),
    )(ends, ends.T, received)


def unpack_kernel(place_ref, back_ref, out_ref):
    toks, rows = out_ref.shape[0], back_ref.shape[0]
    pick = jnp.where(
        lax.broadcasted_iota(jnp.int32, (toks, rows), 1) == place_ref[...], 1.0, 0.0
    ).astype(jnp.bfloat16)
    out_ref[...] = jnp.dot(pick, back_ref[...], preferred_element_type=jnp.float32).astype(
        out_ref.dtype
    )


def unpack(place, back):
    toks, (rows, width) = place.shape[0], back.shape
    tile = 256
    return pl.pallas_call(
        unpack_kernel,
        grid=(toks // tile,),
        in_specs=[
            pl.BlockSpec((tile, 1), lambda i: (i, 0)),
            pl.BlockSpec((rows, width), lambda i: (0, 0)),
        ],
        out_specs=pl.BlockSpec((tile, width), lambda i: (i, 0)),
        out_shape=jax.ShapeDtypeStruct((toks, width), back.dtype),
        compiler_params=pltpu.CompilerParams(vmem_limit_bytes=VMEM),
        cost_estimate=pl.CostEstimate(
            flops=2 * rows * toks * width,
            bytes_accessed=rows * width * 2,
            transcendentals=0,
        ),
    )(place[:, None], back)


def exchange(rows, axis):
    return lax.all_to_all(rows, axis, split_axis=0, concat_axis=0, tiled=True)


def body(queries, keys, values, cluster_ids, out_weight):
    heads, toks = cluster_ids.shape
    head_dim = queries.shape[1] // heads
    sources = lax.axis_size("seq")
    groups = lax.axis_size("head")
    owned = CLUSTERS // sources
    room = owned * MOST
    full_weight = lax.all_gather(out_weight, "head", axis=0, tiled=True)

    clusters = jnp.arange(CLUSTERS, dtype=jnp.int32)
    is_in = cluster_ids[:, None, :] == clusters[None, :, None]
    counts = jnp.sum(is_in.astype(jnp.float32), axis=2)
    by_source = lax.all_gather(counts, "seq", axis=0)

    spot = jnp.arange(toks, dtype=jnp.int32)
    same = cluster_ids[:, :, None] == cluster_ids[:, None, :]
    rank = jnp.sum((same & (spot[:, None] < spot[None, :])[None]).astype(jnp.int32), axis=1)
    before = (clusters[:, None] // owned == clusters[None, :] // owned) & (
        clusters[:, None] < clusters[None, :]
    )
    offset = jnp.sum(jnp.where(before[None], counts[:, :, None], 0.0), axis=1).astype(jnp.int32)
    start = clusters[None, :] // owned * room + offset
    place = jnp.sum(jnp.where(is_in, start[:, :, None], 0), axis=1) + rank

    sent = [
        pack(place[h], queries, keys, values, h, head_dim, sources * room) for h in range(heads)
    ]
    received = [exchange(x, "seq") for x in sent]
    mine = lax.dynamic_slice_in_dim(by_source, lax.axis_index("seq") * owned, owned, axis=2)
    ends = jnp.cumsum(mine, axis=2)
    backs, sums = [], []
    for h in range(heads):
        result, partial = attend(ends[:, h], received[h], room, head_dim)
        backs.append(exchange(result, "seq"))
        sums.append(partial)
    key_sums = jnp.concatenate(sums, axis=1)
    head_outputs = jnp.concatenate([unpack(place[h], backs[h]) for h in range(heads)], axis=1)
    parts = exchange(head_outputs, "head").reshape(groups, toks // groups, heads * head_dim)
    weight = full_weight.reshape(groups, heads * head_dim, full_weight.shape[1])
    attended = jnp.einsum("gtd,gdn->tn", parts, weight, preferred_element_type=jnp.float32)
    return attended.astype(jnp.bfloat16), key_sums


def solution(mesh):
    placed = (
        P("seq", "head"),
        P("seq", "head"),
        P("seq", "head"),
        P("head", "seq"),
        P("head", None),
    )
    return jax.shard_map(
        body,
        mesh=mesh,
        in_specs=placed,
        out_specs=(P(("seq", "head"), None), P("seq", "head")),
        check_vma=False,
    )
```

time: 1080 us -> 414 us (0.38)
  waiting for transfers between devices: 898 us -> 131 us
  blocking collectives: 0 us -> 143 us
  local copies, waits for them, and re-layouts: 72.3 us -> 6.29 us
  Pallas kernels: 0 us -> 32.5 us
  matrix products: 28.3 us -> 5.63 us
  starting transfers between devices: 54.5 us -> 75.6 us
    reduce_scatter x2 -> x0, waiting for transfers between devices: 672 us -> none  [the longest x1 618 us: body(): lax.psum_scatter(partial_value.reshape(CLUSTERS, heads_local * head_dim),...]
    all_gather x0 -> x1, blocking collectives: none -> 143 us  [body(): by_source = lax.all_gather(counts, 'seq', axis=0)]
    all_to_all x5, waiting for transfers between devices: 226 us -> 130 us  [exchange(): return lax.all_to_all(rows, axis, split_axis=0, concat_axis=0, tiled=True)]
    pallas_call x0 -> x6, Pallas kernels: none -> 32.5 us  [the longest x2 20.9 us: attend(): pl.pallas_call(functools.partial(attend_kernel, room), out_shape=(jax.Sha...]
    dot_general x18 -> x1, matrix products: 28.3 us -> 5.63 us  [body(): jnp.einsum('gtd,gdn->tn', parts, weight, preferred_element_type=jnp.float32)]
    all_to_all x5, starting transfers between devices: 54.2 us -> 75.5 us  [exchange(): return lax.all_to_all(rows, axis, split_axis=0, concat_axis=0, tiled=True)]
    reshape x14 -> x0, local copies, waits for them, and re-layouts: 20.9 us -> none  [the longest x8 15.8 us: place_rows(): return buffer.reshape(lead_shape + (rows.shape[1] * rows.shape[2],))]
    unnamed x20 -> x17, local copies, waits for them, and re-layouts: 23.2 us -> 5.61 us
  transfers between devices with their start and end apart: 7 -> 6, of which waited for: 7 -> 4; matrix products, arithmetic and copies ran while one was open for 5% -> 1% of each run, Pallas kernels for 0% -> 7%
where the time goes in v1:
time: 414 us
  blocking collectives  143 us (35%)
  waiting for transfers between devices  131 us (32%)
  starting transfers between devices  75.6 us (18%)
  Pallas kernels  32.5 us (8%)
  between operations  14.3 us (3%)
  local copies, waits for them, and re-layouts  6.29 us (2%)
  other arithmetic  6 us (1%)
  matrix products  5.63 us (1%)
    all_gather x1, blocking collectives, body(): by_source = lax.all_gather(counts, 'seq', axis=0)  143 us
    all_to_all x5, waiting for transfers between devices, exchange(): return lax.all_to_all(rows, axis, split_axis=0, concat_axis=0, tiled=True)  130 us
    all_to_all x5, starting transfers between devices, exchange(): return lax.all_to_all(rows, axis, split_axis=0, concat_axis=0, tiled=True)  75.5 us
    pallas_call x2, Pallas kernels, attend(): pl.pallas_call(functools.partial(attend_kernel, room), out_shape=(jax.Sha...  20.9 us
  transfers between devices with their start and end apart: 6, of which 4 were waited for; matrix products, arithmetic and copies ran while one was open for 1% of the time, Pallas kernels for 7%

profile of v1, /device:TPU:1, one launch (start us, length us, event | category | flops | bytes accessed | tf_op | source)
XLA Modules:
  0.0 413.5 jit_solution(10787680234513967878)
XLA Ops:
  7.2 0.2 iota_compare_fusion.1
  7.4 1.1 convert_reduce_fusion.1
  8.5 0.2 fusion.1
  8.7 0.3 select_reduce_fusion.1
  9.0 1.1 select_reduce_fusion
  10.1 1.6 convert_reduce_fusion
  11.8 0.0 copy-start.2
  11.8 1.0 copy-done.2
  12.8 0.0 copy-start.4
  12.8 1.0 copy-done.4
  13.8 0.0 copy-start.6
  13.8 1.0 copy-done.6
  14.8 4.1 shard_map.68
  18.9 0.0 copy-start.1
  18.9 1.3 copy-done.1
  20.2 0.0 copy-start.3
  20.2 19.4 %all-to-all-start = ((bf16[64,40,384]{2,1,0:T(8,128)(2,1)}), bf16[64,40,384]{2,1,0:T(8,128)(2,1)S(1)}, u32[]{:S(2)}, u32[]{:S(2)}) async-start(bf16[64,40,384]{2,1,0:T(8,128)(2,1)} %bitcast.33), calls=%async_computation | async-start | bytes 3932160 | tf_op jit(solution)/shard_map/all_to_all | solution.py:160
  39.7 0.0 all-gather.4.cloned.1.call-start
  39.7 0.7 all-gather.4.cloned.1.call-update
  40.4 0.0 copy-done.3
  40.4 0.0 copy-done.5
  40.4 0.0 copy-done.7
  40.4 4.1 shard_map.71
  44.6 0.0 copy-start
  44.6 1.2 copy-done
  45.8 83.4 %all-to-all-done = bf16[64,40,384]{2,1,0:T(8,128)(2,1)S(1)} async-done(((bf16[64,40,384]{2,1,0:T(8,128)(2,1)}), bf16[64,40,384]{2,1,0:T(8,128)(2,1)S(1)}, u32[]{:S(2)}, u32[]{:S(2)}) %all-to-all-start) | async-done | bytes 1966112 | tf_op jit(solution)/shard_map/all_to_all | solution.py:160
  129.2 10.7 %all-to-all-start.2 = ((bf16[64,40,384]{2,1,0:T(8,128)(2,1)}), bf16[64,40,384]{2,1,0:T(8,128)(2,1)}, u32[]{:S(2)}, u32[]{:S(2)}) async-start(bf16[64,40,384]{2,1,0:T(8,128)(2,1)} %bitcast.32), calls=%async_computation.2 | async-start | bytes 3932160 | tf_op jit(solution)/shard_map/all_to_all | solution.py:160
  139.9 142.6 %all-gather.1 = f32[64,2,512]{2,1,0:T(2,128)S(1)} all-gather(f32[1,2,512]{2,1,0:T(2,128)S(1)} %bitcast.37), channel_id=2, replica_groups=mesh['seq'=64,'head'=8] {'seq'}, dimensions={0}, use_global_device_ids=true | all-gather | bytes 266240 | tf_op jit(solution)/shard_map/all_gather | solution.py:175
  282.4 0.1 constant_dynamic-slice_fusion
  282.6 0.1 copy.24
  282.7 0.1 copy.20.ends_ref
  282.8 9.7 %shard_map.69 = (bf16[2560,128]{1,0:T(8,128)(2,1)}, f32[8,128]{1,0:T(8,128)S(1)}) custom-call(f32[64,8]{1,0:T(8,128)S(1)} %copy.20.ends_ref, f32[8,64]{1,0:T(8,128)S(1)} %get-tuple-element.10.ends_t_ref, bf16[2560,384]{1,0:T(8,128)(2,1)S(1)} %bitcast.31), custom_call_target="tpu_custom_call" | custom-call | flops 1677721600 | bytes 2621440 | tf_op jit(solution)/shard_map/pallas_call | solution.py:113
  292.5 0.0 all-to-all-done.2
  292.5 11.6 %all-to-all-start.1 = ((bf16[64,40,128]{2,1,0:T(8,128)(2,1)}), bf16[64,40,128]{2,1,0:T(8,128)(2,1)S(1)}, u32[]{:S(2)}, u32[]{:S(2)}) async-start(bf16[64,40,128]{2,1,0:T(8,128)(2,1)} %bitcast.6), calls=%async_computation.1 | async-start | bytes 1310720 | tf_op jit(solution)/shard_map/all_to_all | solution.py:160
  304.1 0.1 copy.22.ends_ref
  304.2 11.2 %shard_map.72 = (bf16[2560,128]{1,0:T(8,128)(2,1)}, f32[8,128]{1,0:T(8,128)S(1)}) custom-call(f32[64,8]{1,0:T(8,128)S(1)} %copy.22.ends_ref, f32[8,64]{1,0:T(8,128)S(1)} %get-tuple-element.11.ends_t_ref, bf16[2560,384]{1,0:T(8,128)(2,1)} %bitcast.12.x_ref), custom_call_target="tpu_custom_call" | custom-call | flops 1677721600 | bytes 2621440 | tf_op jit(solution)/shard_map/pallas_call | solution.py:113
  315.4 13.2 %all-to-all-done.1 = bf16[64,40,128]{2,1,0:T(8,128)(2,1)S(1)} async-done(((bf16[64,40,128]{2,1,0:T(8,128)(2,1)}), bf16[64,40,128]{2,1,0:T(8,128)(2,1)S(1)}, u32[]{:S(2)}, u32[]{:S(2)}) %all-to-all-start.1) | async-done | bytes 655392 | tf_op jit(solution)/shard_map/all_to_all | solution.py:160
  328.6 5.5 %all-to-all-start.3 = ((bf16[64,40,128]{2,1,0:T(8,128)(2,1)}), bf16[64,40,128]{2,1,0:T(8,128)(2,1)S(1)}, u32[]{:S(2)}, u32[]{:S(2)}) async-start(bf16[64,40,128]{2,1,0:T(8,128)(2,1)} %bitcast.13), calls=%async_computation.3 | async-start | bytes 1310720 | tf_op jit(solution)/shard_map/all_to_all | solution.py:160
  334.1 0.2 copy.21.place_ref
  334.3 0.2 copy.23.place_ref
  334.5 1.7 shard_map.70
  336.2 25.9 %all-to-all-done.3 = bf16[64,40,128]{2,1,0:T(8,128)(2,1)S(1)} async-done(((bf16[64,40,128]{2,1,0:T(8,128)(2,1)}), bf16[64,40,128]{2,1,0:T(8,128)(2,1)S(1)}, u32[]{:S(2)}, u32[]{:S(2)}) %all-to-all-start.3) | async-done | bytes 655392 | tf_op jit(solution)/shard_map/all_to_all | solution.py:160
  362.1 1.7 shard_map.73
  363.8 0.8 pad_maximum_fusion
  364.6 28.4 %all-to-all-start.4 = ((bf16[8,96,256]{2,1,0:T(8,128)(2,1)}), bf16[8,96,256]{2,1,0:T(8,128)(2,1)S(1)}, u32[]{:S(2)}, u32[]{:S(2)}) async-start(bf16[8,96,256]{2,1,0:T(8,128)(2,1)} %bitcast.15), calls=%async_computation.4 | async-start | bytes 786432 | tf_op jit(solution)/shard_map/all_to_all | solution.py:160
  393.0 0.6 pad_maximum_fusion.1
  393.6 7.5 %all-to-all-done.4 = bf16[8,96,256]{2,1,0:T(8,128)(2,1)S(1)} async-done(((bf16[8,96,256]{2,1,0:T(8,128)(2,1)}), bf16[8,96,256]{2,1,0:T(8,128)(2,1)S(1)}, u32[]{:S(2)}, u32[]{:S(2)}) %all-to-all-start.4) | async-done | bytes 393248 | tf_op jit(solution)/shard_map/all_to_all | solution.py:160
  401.0 5.6 %fusion = bf16[96,2048]{1,0:T(8,128)(2,1)} fusion(bf16[8,96,256]{2,1,0:T(8,128)(2,1)S(1)} %all-to-all-done.4, bf16[8,256,2048]{2,1,0:T(8,128)(2,1)} %bitcast.36), kind=kOutput, calls=%fused_computation.6 | convolution fusion | flops 805502976 | bytes 9175040 | tf_op jit(solution)/shard_map/gtd,gdn->tn/dot_general | solution.py:202
  (10 shorter events, 0.1 us)
Async XLA Ops:
  11.8 1.0 copy-start.2
  12.8 1.0 copy-start.4
  13.8 1.0 copy-start.6
  18.9 1.3 copy-start.1
  20.2 20.2 %copy-start.3 = (bf16[768,256]{1,0:T(8,128)(2,1)S(1)}, bf16[768,256]{1,0:T(8,128)(2,1)}, u32[]{:S(2)}) copy-start(bf16[768,256]{1,0:T(8,128)(2,1)} %q_ref.3) | copy-start | bytes 1179652
  20.2 20.2 %copy-start.5 = (bf16[768,256]{1,0:T(8,128)(2,1)S(1)}, bf16[768,256]{1,0:T(8,128)(2,1)}, u32[]{:S(2)}) copy-start(bf16[768,256]{1,0:T(8,128)(2,1)} %k_ref.3) | copy-start | bytes 1179652
  20.2 20.2 %copy-start.7 = (bf16[768,256]{1,0:T(8,128)(2,1)S(1)}, bf16[768,256]{1,0:T(8,128)(2,1)}, u32[]{:S(2)}) copy-start(bf16[768,256]{1,0:T(8,128)(2,1)} %v_ref.3) | copy-start | bytes 1179652
  20.2 108.9 %all-to-all-start = ((bf16[64,40,384]{2,1,0:T(8,128)(2,1)}), bf16[64,40,384]{2,1,0:T(8,128)(2,1)S(1)}, u32[]{:S(2)}, u32[]{:S(2)}) async-start(bf16[64,40,384]{2,1,0:T(8,128)(2,1)} %bitcast.33), calls=%async_computation | async-start | bytes 3932160 | tf_op jit(solution)/shard_map/all_to_all | solution.py:160
  39.7 361.4 %all-gather.4.cloned.1.call-start = ((), (), s32[]{:S(2)}) async-start(), calls=%async_computation.5 | async-start | bytes 9437184 | tf_op jit(solution)/shard_map/all_gather | solution.py:170
  44.6 1.2 copy-start
  129.2 163.3 %all-to-all-start.2 = ((bf16[64,40,384]{2,1,0:T(8,128)(2,1)}), bf16[64,40,384]{2,1,0:T(8,128)(2,1)}, u32[]{:S(2)}, u32[]{:S(2)}) async-start(bf16[64,40,384]{2,1,0:T(8,128)(2,1)} %bitcast.32), calls=%async_computation.2 | async-start | bytes 3932160 | tf_op jit(solution)/shard_map/all_to_all | solution.py:160
  292.5 36.2 %all-to-all-start.1 = ((bf16[64,40,128]{2,1,0:T(8,128)(2,1)}), bf16[64,40,128]{2,1,0:T(8,128)(2,1)S(1)}, u32[]{:S(2)}, u32[]{:S(2)}) async-start(bf16[64,40,128]{2,1,0:T(8,128)(2,1)} %bitcast.6), calls=%async_computation.1 | async-start | bytes 1310720 | tf_op jit(solution)/shard_map/all_to_all | solution.py:160
  328.6 33.5 %all-to-all-start.3 = ((bf16[64,40,128]{2,1,0:T(8,128)(2,1)}), bf16[64,40,128]{2,1,0:T(8,128)(2,1)S(1)}, u32[]{:S(2)}, u32[]{:S(2)}) async-start(bf16[64,40,128]{2,1,0:T(8,128)(2,1)} %bitcast.13), calls=%async_computation.3 | async-start | bytes 1310720 | tf_op jit(solution)/shard_map/all_to_all | solution.py:160
  364.6 36.4 %all-to-all-start.4 = ((bf16[8,96,256]{2,1,0:T(8,128)(2,1)}), bf16[8,96,256]{2,1,0:T(8,128)(2,1)S(1)}, u32[]{:S(2)}, u32[]{:S(2)}) async-start(bf16[8,96,256]{2,1,0:T(8,128)(2,1)} %bitcast.15), calls=%async_computation.4 | async-start | bytes 786432 | tf_op jit(solution)/shard_map/all_to_all | solution.py:160
Sparse Core Ops, SparseCore 0:
  42.7 58.8 all-gather.3

commit v2 on v0

v2 whole, which is shorter than its diff:
```python
import functools
import math

import jax
import jax.numpy as jnp
from jax import lax
from jax.experimental import pallas as pl
from jax.experimental.pallas import tpu as pltpu
from jax.sharding import PartitionSpec as P

CLUSTERS = 512
MOST = 5
ROOM = 40
DEALS = 3
TILE = 256
LANES = 128
PARAMS = pltpu.CompilerParams(vmem_limit_bytes=48 * 1024 * 1024)
F32 = jnp.float32
BF16 = jnp.bfloat16
I32 = jnp.int32


def iota(shape, dim):
    return lax.broadcasted_iota(I32, shape, dim)


def flags(mask):
    return jnp.where(mask, 1.0, 0.0).astype(BF16)


def dot(a, b):
    return jnp.dot(a, b, preferred_element_type=F32)


def dot_t(a, b):
    return lax.dot_general(a, b, (((1,), (1,)), ((), ())), preferred_element_type=F32)


def to_col(row):
    size = row.shape[1]
    eye = iota((size, size), 0) == iota((size, size), 1)
    return jnp.sum(jnp.where(eye, row, 0.0), axis=1, keepdims=True)


def deal(position, owners, turn):
    bits = owners.bit_length() - 1
    level = position >> bits
    spot = position & (owners - 1)
    spot = jnp.where((level & 1) == 1, owners - 1 - spot, spot)
    return (spot + level * (turn * 11)) & (owners - 1), level


def plan_kernel(
    room,
    me_ref,
    all_ref,
    own_ref,
    ids_ref,
    rank_ref,
    place_ref,
    ends_ref,
    ends_t_ref,
    sums_row_ref,
    sums_col_ref,
    over_ref,
):
    me = me_ref[0]
    owners = all_ref.shape[0]
    owned = CLUSTERS // owners
    heads = ids_ref.shape[0]
    square = (CLUSTERS, CLUSTERS)
    cluster_row = iota((1, CLUSTERS), 1).astype(F32)
    home = flags(iota((owners, CLUSTERS), 1) // owned == iota((owners, CLUSTERS), 0))
    owner_lane = iota((CLUSTERS, LANES), 1)
    counts, spots, loads = [], [], []
    for h in range(heads):
        count = all_ref[:, h * CLUSTERS : (h + 1) * CLUSTERS]
        total = jnp.sum(count.astype(F32), axis=0, keepdims=True)
        order_row = total * CLUSTERS + (CLUSTERS - 1 - cluster_row)
        order_col = to_col(order_row)
        spot_row = jnp.sum(jnp.where(order_col > order_row, 1.0, 0.0), axis=0, keepdims=True)
        spot_col = jnp.sum(jnp.where(order_row > order_col, 1.0, 0.0), axis=1, keepdims=True)
        counts.append(count)
        spots.append((spot_row.astype(I32), spot_col.astype(I32)))
        tries = []
        for turn in range(1 if h == 0 else DEALS):
            at_col, _ = deal(spots[h][1], owners, turn)
            load = dot((count.astype(F32) + home.astype(F32)).astype(BF16), flags(at_col == owner_lane))
            tries.append(load)
        loads.append(tries)
    fits = [
        jnp.max(jnp.max(loads[0][0] + load, axis=1, keepdims=True), axis=0, keepdims=True)
        <= float(room)
        for load in loads[1]
    ]
    over_ref[...] = jnp.broadcast_to(
        jnp.where(fits[0] | fits[1] | fits[2], 0.0, 1.0), over_ref.shape
    )
    at_rows, at_cols, level_rows, level_cols = [], [], [], []
    for h in range(heads):
        for axis, at, level in ((0, at_rows, level_rows), (1, at_cols, level_cols)):
            chosen, lev = deal(spots[h][axis], owners, 0)
            if h == 1:
                second, _ = deal(spots[h][axis], owners, 1)
                third, _ = deal(spots[h][axis], owners, 2)
                chosen = jnp.where(fits[0], chosen, jnp.where(fits[1], second, third))
            at.append(chosen)
            level.append(lev)

    owns = [jnp.broadcast_to(own_ref[h : h + 1, :], (8, CLUSTERS)).astype(BF16) for h in range(heads)]
    for h in range(heads):
        before = flags((at_cols[h] == at_rows[h]) & (level_cols[h] < level_rows[h]))
        offset = dot(owns[h], before)
        if h == 1:
            offset = offset + dot(owns[0], flags(at_cols[0] == at_rows[1]))
        row_id = iota((8, CLUSTERS), 0)
        table = jnp.where(row_id == 0, at_rows[h].astype(F32), offset).astype(BF16)
        toks = ids_ref.shape[1]
        member = flags(iota((CLUSTERS, toks), 0) == ids_ref[h : h + 1, :])
        found = dot(table, member).astype(I32)
        place_ref[h : h + 1, :] = found[0:1] * room + found[1:2] + rank_ref[h : h + 1, :]

    items = heads * owned
    lane = iota((CLUSTERS, LANES), 1)
    item = iota((items, CLUSTERS), 0)
    ends = jnp.zeros((owners, LANES), F32)
    ends_t = jnp.zeros((items, owners), F32)
    id_row = jnp.zeros((1, LANES), F32)
    id_col = jnp.zeros((items, 1), F32)
    for h in range(heads):
        ends += dot(counts[h], flags((at_cols[h] == me) & (level_cols[h] + h * owned <= lane)))
        ends_t += dot_t(flags((at_rows[h] == me) & (level_rows[h] + h * owned <= item)), counts[h])
        hit = (at_cols[h] == me) & (level_cols[h] + h * owned == lane)
        id_row += jnp.sum(jnp.where(hit, iota(lane.shape, 0).astype(F32), 0.0), axis=0, keepdims=True)
        hit = (at_rows[h] == me) & (level_rows[h] + h * owned == item)
        id_col += jnp.sum(jnp.where(hit, cluster_row, 0.0), axis=1, keepdims=True)
    ends_ref[...] = ends
    ends_t_ref[...] = ends_t

    back_row = id_row.astype(I32) // owned
    back_col = id_col.astype(I32) // owned
    earlier = (back_col == back_row) & (iota((items, LANES), 0) < iota((items, LANES), 1))
    queue = jnp.sum(jnp.where(earlier, 1.0, 0.0), axis=0, keepdims=True)
    used = jnp.sum(
        jnp.where(iota((owners, LANES), 0) == back_row, ends[:, items - 1 : items], 0.0),
        axis=0,
        keepdims=True,
    )
    row = back_row * room + (queue + used).astype(I32)
    sums_row_ref[...] = jnp.broadcast_to(jnp.where(iota((1, LANES), 1) < items, row, -1), sums_row_ref.shape)

    at_lane = jnp.zeros((1, LANES), F32)
    turn_lane = jnp.zeros((1, LANES), F32)
    at_item = jnp.zeros((items, 1), F32)
    turn_item = jnp.zeros((items, 1), F32)
    sent = jnp.zeros((8, LANES), F32)
    for h in range(heads):
        low = me * owned - h * owned
        hit = (iota(lane.shape, 0) == lane + low) & (lane >= h * owned) & (lane < (h + 1) * owned)
        at_lane += jnp.sum(jnp.where(hit, at_cols[h].astype(F32), 0.0), axis=0, keepdims=True)
        turn_lane += jnp.sum(
            jnp.where(hit, (level_cols[h] + h * owned).astype(F32), 0.0), axis=0, keepdims=True
        )
        hit = (iota(item.shape, 1) == item + low) & (item >= h * owned) & (item < (h + 1) * owned)
        at_item += jnp.sum(jnp.where(hit, at_rows[h].astype(F32), 0.0), axis=1, keepdims=True)
        turn_item += jnp.sum(
            jnp.where(hit, (level_rows[h] + h * owned).astype(F32), 0.0), axis=1, keepdims=True
        )
        sent += dot(owns[h], flags(at_cols[h] == lane))
    small = iota((items, LANES), 1)
    ahead = (at_lane == at_item) & (turn_lane < turn_item) & (small < items)
    queue = jnp.sum(jnp.where(ahead, 1.0, 0.0), axis=1, keepdims=True)
    used = jnp.sum(
        jnp.where(small == at_item.astype(I32), sent[0:1], 0.0), axis=1, keepdims=True
    )
    sums_col_ref[...] = jnp.broadcast_to(
        at_item.astype(I32) * room + (queue + used).astype(I32), sums_col_ref.shape
    )


def make_plan(me, everyone, own, cluster_ids, rank, room):
    heads, toks = cluster_ids.shape
    owners = everyone.shape[0]
    items = heads * CLUSTERS // owners
    vmem = pl.BlockSpec(memory_space=pltpu.VMEM)
    return pl.pallas_call(
        functools.partial(plan_kernel, room),
        in_specs=[pl.BlockSpec(memory_space=pltpu.SMEM), vmem, vmem, vmem, vmem],
        out_specs=[vmem] * 6,
        out_shape=(
            jax.ShapeDtypeStruct((heads, toks), I32),
            jax.ShapeDtypeStruct((owners, LANES), F32),
            jax.ShapeDtypeStruct((items, owners), F32),
            jax.ShapeDtypeStruct((8, LANES), I32),
            jax.ShapeDtypeStruct((items, LANES), I32),
            jax.ShapeDtypeStruct((8, LANES), F32),
        ),
        compiler_params=PARAMS,
        cost_estimate=pl.CostEstimate(flops=10**9, bytes_accessed=10**6, transcendentals=0),
    )(me, everyone, own, cluster_ids, rank)


def pack_kernel(place_ref, q_ref, k_ref, v_ref, out_ref):
    rows, toks = out_ref.shape[0], q_ref.shape[0]
    heads = place_ref.shape[0]
    width = q_ref.shape[1] // heads
    wanted = iota((rows, toks), 0) + pl.program_id(0) * rows
    picks = [flags(wanted == place_ref[h : h + 1, :]) for h in range(heads)]
    for part, ref in enumerate((q_ref, k_ref, v_ref)):
        moved = jnp.zeros((rows, width), F32)
        for h in range(heads):
            moved += dot(picks[h], ref[:, h * width : (h + 1) * width])
        out_ref[:, part * width : (part + 1) * width] = moved.astype(out_ref.dtype)


def pack(place, queries, keys, values, rows_all):
    toks, width = queries.shape
    heads = place.shape[0]
    tile = 512
    whole = pl.BlockSpec((toks, width), lambda i: (0, 0))
    return pl.pallas_call(
        pack_kernel,
        grid=(rows_all // tile,),
        in_specs=[pl.BlockSpec((heads, toks), lambda i: (0, 0)), whole, whole, whole],
        out_specs=pl.BlockSpec((tile, 3 * width // heads), lambda i: (i, 0)),
        out_shape=jax.ShapeDtypeStruct((rows_all, 3 * width // heads), queries.dtype),
        compiler_params=PARAMS,
        cost_estimate=pl.CostEstimate(
            flops=6 * rows_all * toks * width,
            bytes_accessed=rows_all * width * 3,
            transcendentals=0,
        ),
    )(place, queries, keys, values)


def row_ids(room, rows, ends_ref, ends_t_ref):
    items, sources = ends_t_ref.shape
    spread = flags(iota((sources, rows), 1) // room == iota((sources, rows), 0))
    ends_row = dot(ends_t_ref[...].astype(BF16), spread)
    slot_row = (iota((items, rows), 1) % room).astype(F32)
    id_row = jnp.sum(jnp.where(ends_row <= slot_row, 1.0, 0.0), axis=0, keepdims=True)
    spread = flags(iota((rows, sources), 0) // room == iota((rows, sources), 1))
    ends_col = dot(spread, ends_ref[...].astype(BF16))
    slot_col = (iota((rows, LANES), 0) % room).astype(F32)
    past = (ends_col <= slot_col) & (iota((rows, LANES), 1) < items)
    return id_row, jnp.sum(jnp.where(past, 1.0, 0.0), axis=1, keepdims=True)


def unit_sums(key_rows, id_row, items):
    key_float = key_rows.astype(F32)
    unit = key_float * lax.rsqrt(jnp.sum(key_float * key_float, axis=1, keepdims=True) + 1e-06)
    high = unit.astype(BF16)
    low = (unit - high.astype(F32)).astype(BF16)
    member = flags(iota((items, id_row.shape[1]), 0).astype(F32) == id_row)
    return (dot(member, high) + dot(member, low)).astype(BF16)


def weigh(pieces, values, width):
    scale = math.log2(math.e) / math.sqrt(width)
    highest = jnp.max(pieces[0], axis=1, keepdims=True)
    for scores in pieces[1:]:
        highest = jnp.maximum(highest, jnp.max(scores, axis=1, keepdims=True))
    total = jnp.zeros_like(highest)
    result = jnp.zeros((highest.shape[0], width), F32)
    for scores, value in zip(pieces, values):
        raised = jnp.exp2((scores - highest) * scale)
        total += jnp.sum(raised, axis=1, keepdims=True)
        result += dot(raised.astype(BF16), value)
    return result / total


def homeward(begin, tile, sums_row_ref, sums):
    pick = flags(iota((tile, LANES), 0) + begin == sums_row_ref[0:1, :])
    return dot(pick[:, 0 : sums.shape[0]], sums)


def attend_kernel(room, ends_ref, ends_t_ref, sums_row_ref, x_ref, out_ref):
    rows, width = out_ref.shape
    id_row, id_col = row_ids(room, rows, ends_ref, ends_t_ref)
    sums = unit_sums(x_ref[:, width : 2 * width], id_row, ends_t_ref.shape[0])
    for begin in range(0, rows, TILE):
        end = begin + TILE
        query = x_ref[begin:end, 0:width]
        at = id_col[begin:end]
        pieces, values = [], []
        if begin:
            scores = dot_t(query, x_ref[0:begin, width : 2 * width])
            pieces.append(jnp.where(at == id_row[:, 0:begin], scores, -1e30))
            values.append(x_ref[0:begin, 2 * width : 3 * width])
        scores = dot_t(query, x_ref[begin:end, width : 2 * width])
        allowed = (at == id_row[:, begin:end]) & (iota((TILE, TILE), 1) <= iota((TILE, TILE), 0))
        pieces.append(jnp.where(allowed, scores, -1e30))
        values.append(x_ref[begin:end, 2 * width : 3 * width])
        result = weigh(pieces, values, width) + homeward(begin, TILE, sums_row_ref, sums)
        out_ref[begin:end] = result.astype(out_ref.dtype)


def attend_tile_kernel(
    room, ends_ref, ends_t_ref, sums_row_ref, x_ref, out_ref, row_scr, col_scr, sums_scr
):
    tile, width = out_ref.shape
    rows = x_ref.shape[0]

    @pl.when(pl.program_id(0) == 0)
    def _():
        id_row, id_col = row_ids(room, rows, ends_ref, ends_t_ref)
        row_scr[...] = jnp.broadcast_to(id_row, row_scr.shape)
        col_scr[...] = jnp.broadcast_to(id_col, col_scr.shape)
        sums_scr[...] = unit_sums(x_ref[:, width : 2 * width], id_row, ends_t_ref.shape[0])

    begin = pl.multiple_of(pl.program_id(0) * tile, tile)
    scores = dot_t(x_ref[pl.ds(begin, tile), 0:width], x_ref[:, width : 2 * width])
    allowed = (col_scr[pl.ds(begin, tile), 0:1] == row_scr[0:1, :]) & (
        iota((tile, rows), 1) <= iota((tile, rows), 0) + begin
    )
    result = weigh([jnp.where(allowed, scores, -1e30)], [x_ref[:, 2 * width : 3 * width]], width)
    out_ref[...] = (result + homeward(begin, tile, sums_row_ref, sums_scr[...])).astype(out_ref.dtype)


def attend(ends, ends_t, sums_row, received, room):
    rows, width = received.shape[0], received.shape[1] // 3
    shape = jax.ShapeDtypeStruct((rows, width), received.dtype)
    cost = pl.CostEstimate(
        flops=2 * rows * rows * width,
        bytes_accessed=rows * width * 8,
        transcendentals=rows * rows // 2,
    )
    given = (ends, ends_t, sums_row, received)
    if rows <= 4096:
        return pl.pallas_call(
            functools.partial(attend_kernel, room),
            out_shape=shape,
            compiler_params=PARAMS,
            cost_estimate=cost,
        )(*given)
    tile = 128
    return pl.pallas_call(
        functools.partial(attend_tile_kernel, room),
        grid=(rows // tile,),
        in_specs=[pl.BlockSpec(x.shape, lambda i: (0, 0)) for x in given],
        out_specs=pl.BlockSpec((tile, width), lambda i: (i, 0)),
        out_shape=shape,
        scratch_shapes=[
            pltpu.VMEM((8, rows), F32),
            pltpu.VMEM((rows, LANES), F32),
            pltpu.VMEM((ends_t.shape[0], width), BF16),
        ],
        compiler_params=PARAMS,
        cost_estimate=cost,
    )(*given)


def unpack_kernel(place_ref, sums_col_ref, over_ref, back_ref, out_ref, sums_ref):
    toks, rows = place_ref.shape[0], back_ref.shape[0]
    width = back_ref.shape[1]
    back = back_ref[...]
    for h in range(place_ref.shape[1]):
        pick = flags(iota((toks, rows), 1) == place_ref[:, h : h + 1])
        moved = dot(pick, back)
        out_ref[0, 0:toks, h * width : (h + 1) * width] = moved.astype(out_ref.dtype)
    spare = out_ref.shape[1] - toks
    out_ref[0, toks:, :] = jnp.broadcast_to(over_ref[0:1, 0:1], (spare, out_ref.shape[2])).astype(
        out_ref.dtype
    )
    items = sums_col_ref.shape[0]
    pick = flags(iota((items, rows), 1) == sums_col_ref[:, 0:1])
    sums_ref[...] = dot(pick, back)


def unpack(place, sums_col, over, back, groups):
    (toks, heads), (rows, width) = place.shape, back.shape
    tile = toks // groups
    items = sums_col.shape[0]
    whole = lambda i: (0, 0)
    return pl.pallas_call(
        unpack_kernel,
        grid=(groups,),
        in_specs=[
            pl.BlockSpec((tile, heads), lambda i: (i, 0)),
            pl.BlockSpec(sums_col.shape, whole),
            pl.BlockSpec(over.shape, whole),
            pl.BlockSpec((rows, width), whole),
        ],
        out_specs=(
            pl.BlockSpec((1, tile + 16, heads * width), lambda i: (i, 0, 0)),
            pl.BlockSpec((items, width), whole),
        ),
        out_shape=(
            jax.ShapeDtypeStruct((groups, tile + 16, heads * width), back.dtype),
            jax.ShapeDtypeStruct((items, width), F32),
        ),
        compiler_params=PARAMS,
        cost_estimate=pl.CostEstimate(
            flops=2 * rows * toks * width * heads,
            bytes_accessed=rows * width * 2,
            transcendentals=0,
        ),
    )(place, sums_col, over, back)


def exchange(rows, axis):
    return lax.all_to_all(rows, axis, split_axis=0, concat_axis=0, tiled=True)


def routed(room, queries, keys, values, cluster_ids, rank, own, everyone):
    heads = cluster_ids.shape[0]
    owners = everyone.shape[0]
    me = lax.axis_index("seq").astype(I32)[None]
    place, ends, ends_t, sums_row, sums_col, over = make_plan(
        me, everyone, own, cluster_ids, rank, room
    )
    sent = pack(place, queries, keys, values, owners * room)
    received = exchange(sent, "seq")
    back = exchange(attend(ends, ends_t, sums_row, received, room), "seq")
    share, sums = unpack(place.T, sums_col, over, back, lax.axis_size("head"))
    parts = exchange(share, "head")
    owned = CLUSTERS // owners
    return parts, jnp.concatenate([sums[h * owned : (h + 1) * owned] for h in range(heads)], axis=1)


def project(parts, weight):
    toks = parts.shape[1] - 16
    weight = weight.reshape(parts.shape[0], parts.shape[2], weight.shape[1])
    total = jnp.einsum("gtd,gdn->tn", parts[:, :toks], weight, preferred_element_type=F32)
    return total.astype(BF16)


def body(queries, keys, values, cluster_ids, out_weight):
    heads, toks = cluster_ids.shape
    owners = lax.axis_size("seq")
    clusters = jnp.arange(CLUSTERS, dtype=I32)
    own = jnp.sum((cluster_ids[:, None, :] == clusters[None, :, None]).astype(F32), axis=2)
    told = jnp.broadcast_to(own.astype(BF16).reshape(1, 8, LANES), (owners, 8, LANES))
    everyone = exchange(told, "seq").reshape(owners, heads * CLUSTERS)
    full_weight = lax.all_gather(out_weight, "head", axis=0, tiled=True)

    spot = jnp.arange(toks, dtype=I32)
    same = cluster_ids[:, :, None] == cluster_ids[:, None, :]
    rank = jnp.sum((same & (spot[:, None] < spot[None, :])[None]).astype(I32), axis=1)
    given = (queries, keys, values, cluster_ids, rank, own, everyone)
    parts, key_sums = routed(ROOM, *given)
    full_room = -(-heads * CLUSTERS // owners * (MOST + 1) // 16) * 16

    def again():
        wide, wide_sums = routed(full_room, *given)
        return project(wide, full_weight), wide_sums

    def done():
        return project(parts, full_weight), key_sums

    return lax.cond(jnp.max(parts[:, -1, 0].astype(F32)) > 0.5, again, done)


def solution(mesh):
    placed = (
        P("seq", "head"),
        P("seq", "head"),
        P("seq", "head"),
        P("head", "seq"),
        P("head", None),
    )
    return jax.shard_map(
        body,
        mesh=mesh,
        in_specs=placed,
        out_specs=(P(("seq", "head"), None), P("seq", "head")),
        check_vma=False,
    )
```

time: 1080 us -> 241 us (0.22)
  waiting for transfers between devices: 898 us -> 56.2 us
  blocking collectives: 0 us -> 96 us
  local copies, waits for them, and re-layouts: 72.3 us -> 1.65 us
  Pallas kernels: 0 us -> 24.7 us
  matrix products: 28.3 us -> 4.87 us
  starting transfers between devices: 54.5 us -> 38.9 us
    reduce_scatter x2 -> x0, waiting for transfers between devices: 672 us -> none  [the longest x1 618 us: body(): lax.psum_scatter(partial_value.reshape(CLUSTERS, heads_local * head_dim),...]
    all_to_all x5 -> x3, waiting for transfers between devices: 226 us -> 55.5 us  [exchange(): return lax.all_to_all(rows, axis, split_axis=0, concat_axis=0, tiled=True)]
    all_to_all x0 -> x1, blocking collectives: none -> 96 us  [exchange(): return lax.all_to_all(rows, axis, split_axis=0, concat_axis=0, tiled=True)]
    pallas_call x0 -> x4, Pallas kernels: none -> 24.7 us  [the longest x1 9.59 us: attend(): pl.pallas_call(functools.partial(attend_kernel, room), out_shape=shape, c...]
    dot_general x18 -> x1, matrix products: 28.3 us -> 4.87 us  [project(): jnp.einsum('gtd,gdn->tn', parts[:, :toks], weight, preferred_element_type...]
    unnamed x20 -> x13, local copies, waits for them, and re-layouts: 23.2 us -> 0.77 us
    reshape x14 -> x0, local copies, waits for them, and re-layouts: 20.9 us -> none  [the longest x8 15.8 us: place_rows(): return buffer.reshape(lead_shape + (rows.shape[1] * rows.shape[2],))]
    all_to_all x5 -> x3, starting transfers between devices: 54.2 us -> 38.9 us  [exchange(): return lax.all_to_all(rows, axis, split_axis=0, concat_axis=0, tiled=True)]
  transfers between devices with their start and end apart: 7 -> 4, of which waited for: 7 -> 3; matrix products, arithmetic and copies ran while one was open for 5% -> 2% of each run, Pallas kernels for 0% -> 10%
where the time goes in v2:
time: 241 us
  blocking collectives  96 us (40%)
  waiting for transfers between devices  56.2 us (23%)
  starting transfers between devices  38.9 us (16%)
  Pallas kernels  24.7 us (10%)
  between operations  14.8 us (6%)
  matrix products  4.87 us (2%)
  other arithmetic  3.57 us (1%)
    all_to_all x1, blocking collectives, exchange(): return lax.all_to_all(rows, axis, split_axis=0, concat_axis=0, tiled=True)  96 us
    all_to_all x3, waiting for transfers between devices, exchange(): return lax.all_to_all(rows, axis, split_axis=0, concat_axis=0, tiled=True)  55.5 us
    all_to_all x3, starting transfers between devices, exchange(): return lax.all_to_all(rows, axis, split_axis=0, concat_axis=0, tiled=True)  38.9 us
    pallas_call x1, Pallas kernels, attend(): pl.pallas_call(functools.partial(attend_kernel, room), out_shape=shape, c...  9.59 us
    pallas_call x1, Pallas kernels, pack(): pl.pallas_call(pack_kernel, grid=(rows_all // tile,), in_specs=[pl.BlockS...  7.01 us
    pallas_call x1, Pallas kernels, unpack(): pl.pallas_call(unpack_kernel, grid=(groups,), in_specs=[pl.BlockSpec((til...  5.17 us
    dot_general x1, matrix products, project(): jnp.einsum('gtd,gdn->tn', parts[:, :toks], weight, preferred_element_type...  4.87 us
  transfers between devices with their start and end apart: 4, of which 3 were waited for; matrix products, arithmetic and copies ran while one was open for 2% of the time, Pallas kernels for 10%

profile of v2, /device:TPU:1, one launch (start us, length us, event | category | flops | bytes accessed | tf_op | source)
XLA Modules:
  0.0 240.8 jit_solution(7091777684761411439)
XLA Ops:
  7.2 0.0 copy-start.3
  7.2 0.0 copy-start.4
  7.2 0.0 copy-start.5
  7.2 0.0 all-gather.2.cloned.1.call-start
  7.2 0.7 all-gather.2.cloned.1.call-update
  7.9 1.1 convert_reduce_fusion.1.own_ref
  9.1 0.7 broadcast_in_dim.7
  9.7 19.3 %all-to-all-start.3 = ((bf16[64,8,128]{2,1,0:T(8,128)(2,1)}), bf16[64,8,128]{2,1,0:T(8,128)(2,1)S(1)}, u32[]{:S(2)}, u32[]{:S(2)}) async-start(bf16[64,8,128]{2,1,0:T(8,128)(2,1)} %broadcast_in_dim.7), calls=%async_computation.3 | async-start | bytes 262144 | tf_op jit(solution)/shard_map/all_to_all | solution.py:402
  29.0 0.2 iota_compare_fusion.1
  29.2 1.6 convert_reduce_fusion.rank_ref
  30.9 13.1 %all-to-all-done.3 = bf16[64,8,128]{2,1,0:T(8,128)(2,1)S(1)} async-done(((bf16[64,8,128]{2,1,0:T(8,128)(2,1)}), bf16[64,8,128]{2,1,0:T(8,128)(2,1)S(1)}, u32[]{:S(2)}, u32[]{:S(2)}) %all-to-all-start.3) | async-done | bytes 131104 | tf_op jit(solution)/shard_map/all_to_all | solution.py:402
  44.0 2.9 %shard_map.68 = (s32[2,768]{1,0:T(2,128)S(1)}, f32[64,128]{1,0:T(8,128)S(1)}, f32[16,64]{1,0:T(8,128)S(1)}, s32[8,128]{1,0:T(8,128)S(1)}, s32[16,128]{1,0:T(8,128)S(1)}, /*index=5*/f32[8,128]{1,0:T(8,128)S(1)}) custom-call(s32[1]{0:T(128)} %bitcast.10.me_ref, bf16[64,1024]{1,0:T(8,128)(2,1)S(1)} %bitcast.39, f32[2,512]{1,0:T(2,128)S(1)} %convert_reduce_fusion.1.own_ref, ...), custom_call_target="tpu_custom_call" | custom-call | flops 1000000000 | bytes 1000000 | tf_op jit(solution)/shard_map/pallas_call | solution.py:186
  46.9 0.0 copy-done.3
  46.9 0.0 copy-done.4
  46.9 0.0 copy-done.5
  46.9 7.0 %shard_map.69 = bf16[2560,384]{1,0:T(8,128)(2,1)S(1)} custom-call(s32[2,768]{1,0:T(2,128)S(1)} %get-tuple-element.56.place_ref, bf16[768,256]{1,0:T(8,128)(2,1)S(1)} %copy-done.3, bf16[768,256]{1,0:T(8,128)(2,1)S(1)} %copy-done.4, bf16[768,256]{1,0:T(8,128)(2,1)S(1)} %copy-done.5), custom_call_target="tpu_custom_call" | custom-call | flops 3019898880 | bytes 1966080 | tf_op jit(solution)/shard_map/pallas_call | solution.py:221
  53.9 96.0 %all_to_all.53 = bf16[64,40,384]{2,1,0:T(8,128)(2,1)S(1)} all-to-all(bf16[64,40,384]{2,1,0:T(8,128)(2,1)S(1)} %bitcast.30), channel_id=1, replica_groups=mesh['seq'=64,'head'=8] {'seq'}, dimensions={0} | all-to-all | bytes 3932160 | tf_op jit(solution)/shard_map/all_to_all | solution.py:402
  149.9 9.6 %shard_map.70 = bf16[2560,128]{1,0:T(8,128)(2,1)} custom-call(f32[64,128]{1,0:T(8,128)S(1)} %get-tuple-element.59.ends_ref, f32[16,64]{1,0:T(8,128)S(1)} %get-tuple-element.60.ends_t_ref, s32[8,128]{1,0:T(8,128)S(1)} %get-tuple-element.61.sums_row_ref, bf16[2560,384]{1,0:T(8,128)(2,1)S(1)} %bitcast.29), custom_call_target="tpu_custom_call" | custom-call | flops 1677721600 | bytes 2621440 | tf_op jit(solution)/shard_map/pallas_call | solution.py:330
  159.5 0.0 copy-start.1
  159.5 9.8 %all-to-all-start.5 = ((bf16[64,40,128]{2,1,0:T(8,128)(2,1)}), bf16[64,40,128]{2,1,0:T(8,128)(2,1)S(1)}, u32[]{:S(2)}, u32[]{:S(2)}) async-start(bf16[64,40,128]{2,1,0:T(8,128)(2,1)} %bitcast.14), calls=%async_computation.5 | async-start | bytes 1310720 | tf_op jit(solution)/shard_map/all_to_all | solution.py:402
  169.4 0.2 copy.10
  169.6 33.7 %all-to-all-done.5 = bf16[64,40,128]{2,1,0:T(8,128)(2,1)S(1)} async-done(((bf16[64,40,128]{2,1,0:T(8,128)(2,1)}), bf16[64,40,128]{2,1,0:T(8,128)(2,1)S(1)}, u32[]{:S(2)}, u32[]{:S(2)}) %all-to-all-start.5) | async-done | bytes 655392 | tf_op jit(solution)/shard_map/all_to_all | solution.py:402
  203.3 5.2 %shard_map.71 = (bf16[8,112,256]{2,1,0:T(8,128)(2,1)}, f32[16,128]{1,0:T(8,128)S(1)}) custom-call(s32[768,2]{1,0:T(8,128)S(1)} %bitcast.33, s32[16,128]{1,0:T(8,128)S(1)} %get-tuple-element.57.sums_col_ref, f32[8,128]{1,0:T(8,128)S(1)} %get-tuple-element.58.over_ref, bf16[2560,128]{1,0:T(8,128)(2,1)S(1)} %bitcast.32), custom_call_target="tpu_custom_call" | custom-call | flops 1006632960 | bytes 655360 | tf_op jit(solution)/shard_map/pallas_call | solution.py:375
  208.5 9.8 %all-to-all-start.6 = ((bf16[8,112,256]{2,1,0:T(8,128)(2,1)}), bf16[8,112,256]{2,1,0:T(8,128)(2,1)S(1)}, u32[]{:S(2)}, u32[]{:S(2)}) async-start(bf16[8,112,256]{2,1,0:T(8,128)(2,1)} %get-tuple-element.62), calls=%async_computation.6 | async-start | bytes 917504 | tf_op jit(solution)/shard_map/all_to_all | solution.py:402
  218.2 8.8 %all-to-all-done.6 = bf16[8,112,256]{2,1,0:T(8,128)(2,1)S(1)} async-done(((bf16[8,112,256]{2,1,0:T(8,128)(2,1)}), bf16[8,112,256]{2,1,0:T(8,128)(2,1)S(1)}, u32[]{:S(2)}, u32[]{:S(2)}) %all-to-all-start.6) | async-done | bytes 458784 | tf_op jit(solution)/shard_map/all_to_all | solution.py:402
  227.0 0.6 slice_reduce_fusion
  228.3 0.0 all-gather.2.cloned.1.call-done
  228.3 0.0 copy-done.1
  228.3 4.9 %conditional.2 = (f32[8,256]{1,0:T(8,128)S(1)}, bf16[96,2048]{1,0:T(8,128)(2,1)S(1)}) conditional(s32[]{:T(128)} %convert_element_type.29, (bf16[8,112,256]{2,1,0:T(8,128)(2,1)S(1)}, bf16[2048,2048]{1,0:T(8,128)(2,1)}, f32[8,256]{1,0:T(8,128)S(1)}) %tuple.19, (bf16[64,1024]{1,0:T(8,128)(2,1)S(1)}, f32[2,512]{1,0:T(2,128)S(1)}, ...), branch_computations={%region_3.0_spmd, %region_4.0_spmd} | conditional | flops 21132857344 | bytes 38335152
  228.3 4.9 %fusion = bf16[96,2048]{1,0:T(8,128)(2,1)S(1)} fusion(bf16[8,256,2048]{2,1,0:T(8,128)(2,1)} %bitcast.35, bf16[8,112,256]{2,1,0:T(8,128)(2,1)S(1)} %get-tuple-element.25), kind=kOutput, calls=%fused_computation.1 | convolution fusion | flops 805502976 | bytes 9175040 | tf_op jit(solution)/shard_map/cond/branch_0_fun/gtd,gdn->tn/dot_general | solution.py:424
  233.2 0.0 copy-start
  233.2 0.0 copy-start.2
  233.2 0.7 copy-done
  234.0 0.0 copy-done.2
  (5 shorter events, 0.0 us)
Async XLA Ops:
  7.2 39.7 %copy-start.3 = (bf16[768,256]{1,0:T(8,128)(2,1)S(1)}, bf16[768,256]{1,0:T(8,128)(2,1)}, u32[]{:S(2)}) copy-start(bf16[768,256]{1,0:T(8,128)(2,1)} %q_ref.1) | copy-start | bytes 1179652
  7.2 39.7 %copy-start.4 = (bf16[768,256]{1,0:T(8,128)(2,1)S(1)}, bf16[768,256]{1,0:T(8,128)(2,1)}, u32[]{:S(2)}) copy-start(bf16[768,256]{1,0:T(8,128)(2,1)} %k_ref.1) | copy-start | bytes 1179652
  7.2 39.7 %copy-start.5 = (bf16[768,256]{1,0:T(8,128)(2,1)S(1)}, bf16[768,256]{1,0:T(8,128)(2,1)}, u32[]{:S(2)}) copy-start(bf16[768,256]{1,0:T(8,128)(2,1)} %v_ref.1) | copy-start | bytes 1179652
  7.2 221.1 %all-gather.2.cloned.1.call-start = ((), (), s32[]{:S(2)}) async-start(), calls=%async_computation.7 | async-start | bytes 9437184 | tf_op jit(solution)/shard_map/all_gather | solution.py:435
  9.7 34.2 %all-to-all-start.3 = ((bf16[64,8,128]{2,1,0:T(8,128)(2,1)}), bf16[64,8,128]{2,1,0:T(8,128)(2,1)S(1)}, u32[]{:S(2)}, u32[]{:S(2)}) async-start(bf16[64,8,128]{2,1,0:T(8,128)(2,1)} %broadcast_in_dim.7), calls=%async_computation.3 | async-start | bytes 262144 | tf_op jit(solution)/shard_map/all_to_all | solution.py:402
  159.5 68.8 %copy-start.1 = (s32[2,768]{1,0:T(2,128)S(1)}, s32[2,768]{1,0:T(2,128)}, u32[]{:S(2)}) copy-start(s32[2,768]{1,0:T(2,128)} %ids_ref.1) | copy-start | bytes 18436
  159.5 43.8 %all-to-all-start.5 = ((bf16[64,40,128]{2,1,0:T(8,128)(2,1)}), bf16[64,40,128]{2,1,0:T(8,128)(2,1)S(1)}, u32[]{:S(2)}, u32[]{:S(2)}) async-start(bf16[64,40,128]{2,1,0:T(8,128)(2,1)} %bitcast.14), calls=%async_computation.5 | async-start | bytes 1310720 | tf_op jit(solution)/shard_map/all_to_all | solution.py:402
  208.5 18.6 %all-to-all-start.6 = ((bf16[8,112,256]{2,1,0:T(8,128)(2,1)}), bf16[8,112,256]{2,1,0:T(8,128)(2,1)S(1)}, u32[]{:S(2)}, u32[]{:S(2)}) async-start(bf16[8,112,256]{2,1,0:T(8,128)(2,1)} %get-tuple-element.62), calls=%async_computation.6 | async-start | bytes 917504 | tf_op jit(solution)/shard_map/all_to_all | solution.py:402
  233.2 0.7 copy-start
  233.2 0.7 copy-start.2
Sparse Core Ops, SparseCore 0:
  10.2 63.0 all-gather.1

commit v3 on v2

--- a/solution.py
+++ b/solution.py
@@ -10,8 +10,7 @@
 
 CLUSTERS = 512
 MOST = 5
-ROOM = 40
-DEALS = 3
+ROOM = 32
 TILE = 256
 LANES = 128
 PARAMS = pltpu.CompilerParams(vmem_limit_bytes=48 * 1024 * 1024)
@@ -42,12 +41,66 @@
     return jnp.sum(jnp.where(eye, row, 0.0), axis=1, keepdims=True)
 
 
-def deal(position, owners, turn):
+def deal(position, owners):
     bits = owners.bit_length() - 1
     level = position >> bits
     spot = position & (owners - 1)
-    spot = jnp.where((level & 1) == 1, owners - 1 - spot, spot)
-    return (spot + level * (turn * 11)) & (owners - 1), level
+    return jnp.where((level & 1) == 1, owners - 1 - spot, spot), level
+
+
+def match(room, counts, at_rows, at_cols):
+    owners = counts[0].shape[0]
+    shape = (owners, LANES)
+    first = dot_t(flags(iota((owners, CLUSTERS), 0) == at_rows[0]), counts[0])
+    second = dot(counts[1], flags(iota((CLUSTERS, LANES), 1) == at_cols[1]))
+    most = jnp.zeros(shape, F32)
+    for s in range(owners):
+        most = jnp.maximum(most, first[:, s : s + 1] + second[s : s + 1, :])
+    lane = iota((1, LANES), 1)
+    fit = jnp.where((most <= float(room)) & (lane < owners), 1.0, 0.0)
+    state = jnp.concatenate([fit, jnp.broadcast_to(lane.astype(F32), (8, LANES))], axis=0)
+    eye = iota(shape, 0) == iota(shape, 1)
+
+    def pick(mask, block):
+        return jnp.sum(jnp.where(mask, block[0:owners], 0.0), axis=0, keepdims=True)
+
+    def misfits(state):
+        return float(owners) - jnp.sum(jnp.where(eye, state[0:owners], 0.0))
+
+    def swap(step, state):
+        turn = step % (owners - 1) + 1
+        across = iota((LANES, LANES), 0) == (iota((LANES, LANES), 1) ^ turn)
+        moved = dot(state.astype(BF16), flags(across))
+        across = across[0:owners]
+        gain = pick(across, state) * pick(eye, moved)
+        settled = pick(eye, state) * pick(across, moved)
+        return jnp.where(gain * (1.0 - settled) > 0.5, moved, state)
+
+    def more(carry):
+        step, left, _ = carry
+        return (left > 0.5) & (step < 4 * (owners - 1))
+
+    def rounds(carry):
+        step, _, state = carry
+        for _ in range(3):
+            state = swap(step, state)
+            step = step + 1
+        return step, misfits(state), state
+
+    _, left, state = lax.while_loop(more, rounds, (jnp.int32(0), misfits(state), state))
+    label = state[owners : owners + 1, :]
+    label_col = jnp.sum(jnp.where(eye, label, 0.0), axis=1, keepdims=True).astype(I32)
+    wide = (owners, CLUSTERS)
+    row = jnp.sum(
+        jnp.where(label_col == at_rows[1], iota(wide, 0).astype(F32), 0.0), axis=0, keepdims=True
+    )
+    wide = (CLUSTERS, LANES)
+    col = jnp.sum(
+        jnp.where(label.astype(I32) == at_cols[1], iota(wide, 1).astype(F32), 0.0),
+        axis=1,
+        keepdims=True,
+    )
+    return row.astype(I32), col.astype(I32), jnp.where(left > 0.5, 1.0, 0.0)
 
 
 def plan_kernel(
@@ -71,8 +124,7 @@
     square = (CLUSTERS, CLUSTERS)
     cluster_row = iota((1, CLUSTERS), 1).astype(F32)
     home = flags(iota((owners, CLUSTERS), 1) // owned == iota((owners, CLUSTERS), 0))
-    owner_lane = iota((CLUSTERS, LANES), 1)
-    counts, spots, loads = [], [], []
+    counts, at_rows, at_cols, level_rows, level_cols = [], [], [], [], []
     for h in range(heads):
         count = all_ref[:, h * CLUSTERS : (h + 1) * CLUSTERS]
         total = jnp.sum(count.astype(F32), axis=0, keepdims=True)
@@ -81,31 +133,14 @@
         spot_row = jnp.sum(jnp.where(order_col > order_row, 1.0, 0.0), axis=0, keepdims=True)
         spot_col = jnp.sum(jnp.where(order_row > order_col, 1.0, 0.0), axis=1, keepdims=True)
         counts.append(count)
-        spots.append((spot_row.astype(I32), spot_col.astype(I32)))
-        tries = []
-        for turn in range(1 if h == 0 else DEALS):
-            at_col, _ = deal(spots[h][1], owners, turn)
-            load = dot((count.astype(F32) + home.astype(F32)).astype(BF16), flags(at_col == owner_lane))
-            tries.append(load)
-        loads.append(tries)
-    fits = [
-        jnp.max(jnp.max(loads[0][0] + load, axis=1, keepdims=True), axis=0, keepdims=True)
-        <= float(room)
-        for load in loads[1]
-    ]
-    over_ref[...] = jnp.broadcast_to(
-        jnp.where(fits[0] | fits[1] | fits[2], 0.0, 1.0), over_ref.shape
-    )
-    at_rows, at_cols, level_rows, level_cols = [], [], [], []
-    for h in range(heads):
-        for axis, at, level in ((0, at_rows, level_rows), (1, at_cols, level_cols)):
-            chosen, lev = deal(spots[h][axis], owners, 0)
-            if h == 1:
-                second, _ = deal(spots[h][axis], owners, 1)
-                third, _ = deal(spots[h][axis], owners, 2)
-                chosen = jnp.where(fits[0], chosen, jnp.where(fits[1], second, third))
+        for spot, at, level in ((spot_row, at_rows, level_rows), (spot_col, at_cols, level_cols)):
+            chosen, lev = deal(spot.astype(I32), owners)
             at.append(chosen)
             level.append(lev)
+    at_rows[1], at_cols[1], over = match(
+        room, [(c.astype(F32) + home.astype(F32)).astype(BF16) for c in counts], at_rows, at_cols
+    )
+    over_ref[...] = jnp.broadcast_to(over, over_ref.shape)
 
     owns = [jnp.broadcast_to(own_ref[h : h + 1, :], (8, CLUSTERS)).astype(BF16) for h in range(heads)]
     for h in range(heads):

time: 241 us -> 221 us (0.917)
  blocking collectives: 96 us -> 81.7 us
  waiting for transfers between devices: 56.2 us -> 51.6 us
    all_to_all x1, blocking collectives: 96 us -> 81.7 us  [exchange(): return lax.all_to_all(rows, axis, split_axis=0, concat_axis=0, tiled=True)]
    all_to_all x3, waiting for transfers between devices: 55.5 us -> 50.9 us  [exchange(): return lax.all_to_all(rows, axis, split_axis=0, concat_axis=0, tiled=True)]
    pallas_call x1, Pallas kernels: 2.9 us -> 6.38 us  [make_plan(): pl.pallas_call(functools.partial(plan_kernel, room), in_specs=[pl.BlockSp...]
    pallas_call x1, Pallas kernels: 9.59 us -> 6.7 us  [attend(): pl.pallas_call(functools.partial(attend_kernel, room), out_shape=shape, c...]
  transfers between devices with their start and end apart: 4 -> 4, of which waited for: 3 -> 3; matrix products, arithmetic and copies ran while one was open for 2% -> 2% of each run, Pallas kernels for 10% -> 11%
where the time goes in v3:
time: 221 us
  blocking collectives  81.7 us (37%)
  waiting for transfers between devices  51.6 us (23%)
  starting transfers between devices  39 us (18%)
  Pallas kernels  23.5 us (11%)
  between operations  14.8 us (7%)
  matrix products  4.87 us (2%)
  other arithmetic  3.57 us (2%)
    all_to_all x1, blocking collectives, exchange(): return lax.all_to_all(rows, axis, split_axis=0, concat_axis=0, tiled=True)  81.7 us
    all_to_all x3, waiting for transfers between devices, exchange(): return lax.all_to_all(rows, axis, split_axis=0, concat_axis=0, tiled=True)  50.9 us
    all_to_all x3, starting transfers between devices, exchange(): return lax.all_to_all(rows, axis, split_axis=0, concat_axis=0, tiled=True)  39 us
    pallas_call x1, Pallas kernels, attend(): pl.pallas_call(functools.partial(attend_kernel, room), out_shape=shape, c...  6.7 us
    pallas_call x1, Pallas kernels, make_plan(): pl.pallas_call(functools.partial(plan_kernel, room), in_specs=[pl.BlockSp...  6.38 us
    pallas_call x1, Pallas kernels, pack(): pl.pallas_call(pack_kernel, grid=(rows_all // tile,), in_specs=[pl.BlockS...  5.61 us
    dot_general x1, matrix products, project(): jnp.einsum('gtd,gdn->tn', parts[:, :toks], weight, preferred_element_type...  4.87 us
    pallas_call x1, Pallas kernels, unpack(): pl.pallas_call(unpack_kernel, grid=(groups,), in_specs=[pl.BlockSpec((til...  4.8 us
  transfers between devices with their start and end apart: 4, of which 3 were waited for; matrix products, arithmetic and copies ran while one was open for 2% of the time, Pallas kernels for 11%

profile of v3, /device:TPU:1, one launch (start us, length us, event | category | flops | bytes accessed | tf_op | source)
XLA Modules:
  0.0 220.7 jit_solution(17896517291566536309)
XLA Ops:
  7.2 0.0 copy-start.3
  7.2 0.0 copy-start.4
  7.2 0.0 copy-start.5
  7.2 0.0 all-gather.2.cloned.1.call-start
  7.2 0.7 all-gather.2.cloned.1.call-update
  7.9 1.1 convert_reduce_fusion.1.own_ref
  9.1 0.7 broadcast_in_dim.7
  9.7 19.3 %all-to-all-start.3 = ((bf16[64,8,128]{2,1,0:T(8,128)(2,1)}), bf16[64,8,128]{2,1,0:T(8,128)(2,1)S(1)}, u32[]{:S(2)}, u32[]{:S(2)}) async-start(bf16[64,8,128]{2,1,0:T(8,128)(2,1)} %broadcast_in_dim.7), calls=%async_computation.3 | async-start | bytes 262144 | tf_op jit(solution)/shard_map/all_to_all | solution.py:437
  29.0 0.2 iota_compare_fusion.1
  29.2 1.6 convert_reduce_fusion.rank_ref
  30.9 13.1 %all-to-all-done.3 = bf16[64,8,128]{2,1,0:T(8,128)(2,1)S(1)} async-done(((bf16[64,8,128]{2,1,0:T(8,128)(2,1)}), bf16[64,8,128]{2,1,0:T(8,128)(2,1)S(1)}, u32[]{:S(2)}, u32[]{:S(2)}) %all-to-all-start.3) | async-done | bytes 131104 | tf_op jit(solution)/shard_map/all_to_all | solution.py:437
  44.0 6.4 %shard_map.68 = (s32[2,768]{1,0:T(2,128)S(1)}, f32[64,128]{1,0:T(8,128)S(1)}, f32[16,64]{1,0:T(8,128)S(1)}, s32[8,128]{1,0:T(8,128)S(1)}, s32[16,128]{1,0:T(8,128)S(1)}, /*index=5*/f32[8,128]{1,0:T(8,128)S(1)}) custom-call(s32[1]{0:T(128)} %bitcast.10.me_ref, bf16[64,1024]{1,0:T(8,128)(2,1)S(1)} %bitcast.39, f32[2,512]{1,0:T(2,128)S(1)} %convert_reduce_fusion.1.own_ref, ...), custom_call_target="tpu_custom_call" | custom-call | flops 1000000000 | bytes 1000000 | tf_op jit(solution)/shard_map/pallas_call | solution.py:221
  50.3 0.0 copy-done.3
  50.3 0.0 copy-done.4
  50.3 0.0 copy-done.5
  50.4 5.6 %shard_map.69 = bf16[2048,384]{1,0:T(8,128)(2,1)S(1)} custom-call(s32[2,768]{1,0:T(2,128)S(1)} %get-tuple-element.56.place_ref, bf16[768,256]{1,0:T(8,128)(2,1)S(1)} %copy-done.3, bf16[768,256]{1,0:T(8,128)(2,1)S(1)} %copy-done.4, bf16[768,256]{1,0:T(8,128)(2,1)S(1)} %copy-done.5), custom_call_target="tpu_custom_call" | custom-call | flops 2415919104 | bytes 1572864 | tf_op jit(solution)/shard_map/pallas_call | solution.py:256
  56.0 81.7 %all_to_all.53 = bf16[64,32,384]{2,1,0:T(8,128)(2,1)S(1)} all-to-all(bf16[64,32,384]{2,1,0:T(8,128)(2,1)S(1)} %bitcast.31), channel_id=1, replica_groups=mesh['seq'=64,'head'=8] {'seq'}, dimensions={0} | all-to-all | bytes 3145728 | tf_op jit(solution)/shard_map/all_to_all | solution.py:437
  137.7 0.0 copy-start.1
  137.7 6.7 %shard_map.70 = bf16[2048,128]{1,0:T(8,128)(2,1)} custom-call(f32[64,128]{1,0:T(8,128)S(1)} %get-tuple-element.59.ends_ref, f32[16,64]{1,0:T(8,128)S(1)} %get-tuple-element.60.ends_t_ref, s32[8,128]{1,0:T(8,128)S(1)} %get-tuple-element.61.sums_row_ref, bf16[2048,384]{1,0:T(8,128)(2,1)S(1)} %bitcast.30), custom_call_target="tpu_custom_call" | custom-call | flops 1073741824 | bytes 2097152 | tf_op jit(solution)/shard_map/pallas_call | solution.py:365
  144.4 7.8 %all-to-all-start.5 = ((bf16[64,32,128]{2,1,0:T(8,128)(2,1)}), bf16[64,32,128]{2,1,0:T(8,128)(2,1)S(1)}, u32[]{:S(2)}, u32[]{:S(2)}) async-start(bf16[64,32,128]{2,1,0:T(8,128)(2,1)} %bitcast.14), calls=%async_computation.5 | async-start | bytes 1048576 | tf_op jit(solution)/shard_map/all_to_all | solution.py:437
  152.2 0.2 copy.10
  152.4 29.1 %all-to-all-done.5 = bf16[64,32,128]{2,1,0:T(8,128)(2,1)S(1)} async-done(((bf16[64,32,128]{2,1,0:T(8,128)(2,1)}), bf16[64,32,128]{2,1,0:T(8,128)(2,1)S(1)}, u32[]{:S(2)}, u32[]{:S(2)}) %all-to-all-start.5) | async-done | bytes 524320 | tf_op jit(solution)/shard_map/all_to_all | solution.py:437
  181.5 4.8 %shard_map.71 = (bf16[8,112,256]{2,1,0:T(8,128)(2,1)}, f32[16,128]{1,0:T(8,128)S(1)}) custom-call(s32[768,2]{1,0:T(8,128)S(1)} %bitcast.33, s32[16,128]{1,0:T(8,128)S(1)} %get-tuple-element.57.sums_col_ref, f32[8,128]{1,0:T(8,128)S(1)} %get-tuple-element.58.over_ref, bf16[2048,128]{1,0:T(8,128)(2,1)S(1)} %bitcast.32), custom_call_target="tpu_custom_call" | custom-call | flops 805306368 | bytes 524288 | tf_op jit(solution)/shard_map/pallas_call | solution.py:410
  186.3 11.9 %all-to-all-start.6 = ((bf16[8,112,256]{2,1,0:T(8,128)(2,1)}), bf16[8,112,256]{2,1,0:T(8,128)(2,1)S(1)}, u32[]{:S(2)}, u32[]{:S(2)}) async-start(bf16[8,112,256]{2,1,0:T(8,128)(2,1)} %get-tuple-element.62), calls=%async_computation.6 | async-start | bytes 917504 | tf_op jit(solution)/shard_map/all_to_all | solution.py:437
  198.2 8.8 %all-to-all-done.6 = bf16[8,112,256]{2,1,0:T(8,128)(2,1)S(1)} async-done(((bf16[8,112,256]{2,1,0:T(8,128)(2,1)}), bf16[8,112,256]{2,1,0:T(8,128)(2,1)S(1)}, u32[]{:S(2)}, u32[]{:S(2)}) %all-to-all-start.6) | async-done | bytes 458784 | tf_op jit(solution)/shard_map/all_to_all | solution.py:437
  206.9 0.6 slice_reduce_fusion
  208.2 0.0 all-gather.2.cloned.1.call-done
  208.2 0.0 copy-done.1
  208.2 4.9 %conditional.2 = (f32[8,256]{1,0:T(8,128)S(1)}, bf16[96,2048]{1,0:T(8,128)(2,1)S(1)}) conditional(s32[]{:T(128)} %convert_element_type.29, (bf16[8,112,256]{2,1,0:T(8,128)(2,1)S(1)}, bf16[2048,2048]{1,0:T(8,128)(2,1)}, f32[8,256]{1,0:T(8,128)S(1)}) %tuple.19, (bf16[64,1024]{1,0:T(8,128)(2,1)S(1)}, f32[2,512]{1,0:T(2,128)S(1)}, ...), branch_computations={%region_3.0_spmd, %region_4.0_spmd} | conditional | flops 21132857344 | bytes 38335152
  208.3 4.9 %fusion = bf16[96,2048]{1,0:T(8,128)(2,1)S(1)} fusion(bf16[8,256,2048]{2,1,0:T(8,128)(2,1)} %bitcast.35, bf16[8,112,256]{2,1,0:T(8,128)(2,1)S(1)} %get-tuple-element.25), kind=kOutput, calls=%fused_computation.1 | convolution fusion | flops 805502976 | bytes 9175040 | tf_op jit(solution)/shard_map/cond/branch_0_fun/gtd,gdn->tn/dot_general | solution.py:459
  213.1 0.0 copy-start
  213.2 0.0 copy-start.2
  213.2 0.7 copy-done
  213.9 0.0 copy-done.2
  (5 shorter events, 0.0 us)
Async XLA Ops:
  7.2 43.2 %copy-start.3 = (bf16[768,256]{1,0:T(8,128)(2,1)S(1)}, bf16[768,256]{1,0:T(8,128)(2,1)}, u32[]{:S(2)}) copy-start(bf16[768,256]{1,0:T(8,128)(2,1)} %q_ref.1) | copy-start | bytes 1179652
  7.2 43.2 %copy-start.4 = (bf16[768,256]{1,0:T(8,128)(2,1)S(1)}, bf16[768,256]{1,0:T(8,128)(2,1)}, u32[]{:S(2)}) copy-start(bf16[768,256]{1,0:T(8,128)(2,1)} %k_ref.1) | copy-start | bytes 1179652
  7.2 43.2 %copy-start.5 = (bf16[768,256]{1,0:T(8,128)(2,1)S(1)}, bf16[768,256]{1,0:T(8,128)(2,1)}, u32[]{:S(2)}) copy-start(bf16[768,256]{1,0:T(8,128)(2,1)} %v_ref.1) | copy-start | bytes 1179652
  7.2 201.0 %all-gather.2.cloned.1.call-start = ((), (), s32[]{:S(2)}) async-start(), calls=%async_computation.7 | async-start | bytes 9437184 | tf_op jit(solution)/shard_map/all_gather | solution.py:470
  9.7 34.2 %all-to-all-start.3 = ((bf16[64,8,128]{2,1,0:T(8,128)(2,1)}), bf16[64,8,128]{2,1,0:T(8,128)(2,1)S(1)}, u32[]{:S(2)}, u32[]{:S(2)}) async-start(bf16[64,8,128]{2,1,0:T(8,128)(2,1)} %broadcast_in_dim.7), calls=%async_computation.3 | async-start | bytes 262144 | tf_op jit(solution)/shard_map/all_to_all | solution.py:437
  137.7 70.5 %copy-start.1 = (s32[2,768]{1,0:T(2,128)S(1)}, s32[2,768]{1,0:T(2,128)}, u32[]{:S(2)}) copy-start(s32[2,768]{1,0:T(2,128)} %ids_ref.1) | copy-start | bytes 18436
  144.4 37.0 %all-to-all-start.5 = ((bf16[64,32,128]{2,1,0:T(8,128)(2,1)}), bf16[64,32,128]{2,1,0:T(8,128)(2,1)S(1)}, u32[]{:S(2)}, u32[]{:S(2)}) async-start(bf16[64,32,128]{2,1,0:T(8,128)(2,1)} %bitcast.14), calls=%async_computation.5 | async-start | bytes 1048576 | tf_op jit(solution)/shard_map/all_to_all | solution.py:437
  186.3 20.7 %all-to-all-start.6 = ((bf16[8,112,256]{2,1,0:T(8,128)(2,1)}), bf16[8,112,256]{2,1,0:T(8,128)(2,1)S(1)}, u32[]{:S(2)}, u32[]{:S(2)}) async-start(bf16[8,112,256]{2,1,0:T(8,128)(2,1)} %get-tuple-element.62), calls=%async_computation.6 | async-start | bytes 917504 | tf_op jit(solution)/shard_map/all_to_all | solution.py:437
  213.1 0.7 copy-start
  213.2 0.7 copy-start.2
Sparse Core Ops, SparseCore 0:
  10.2 63.0 all-gather.1

commit v4 on v2

--- a/solution.py
+++ b/solution.py
@@ -10,9 +10,9 @@
 
 CLUSTERS = 512
 MOST = 5
-ROOM = 40
-DEALS = 3
+ROOM = 32
 TILE = 256
+FAR = 2.0**100
 LANES = 128
 PARAMS = pltpu.CompilerParams(vmem_limit_bytes=48 * 1024 * 1024)
 F32 = jnp.float32
@@ -34,6 +34,10 @@
 
 def dot_t(a, b):
     return lax.dot_general(a, b, (((1,), (1,)), ((), ())), preferred_element_type=F32)
+
+
+def shift_of(room):
+    return room.bit_length() - 1
 
 
 def to_col(row):
@@ -48,6 +52,100 @@
     spot = position & (owners - 1)
     spot = jnp.where((level & 1) == 1, owners - 1 - spot, spot)
     return (spot + level * (turn * 11)) & (owners - 1), level
+
+
+def match(room, counts, spot_rows, spot_cols, scr):
+    set_scr, flip_scr, move_scr, row_scr, col_scr, first_scr, first_t_scr, state_scr, turned_scr = scr
+    owners = counts[0].shape[0]
+    shape = (owners, LANES)
+    square = (LANES, LANES)
+    tall = (CLUSTERS, LANES)
+    wide = (owners, CLUSTERS)
+    rows, cols, level_rows, level_cols = [], [], [], []
+    for h in range(2):
+        for spot, at, levels in ((spot_rows, rows, level_rows), (spot_cols, cols, level_cols)):
+            chosen, level = deal(spot[h], owners, 0)
+            at.append(chosen)
+            levels.append(level)
+    count_scr = counts[1]
+    row_scr[...] = jnp.broadcast_to(spot_rows[1], row_scr.shape)
+    col_scr[...] = jnp.broadcast_to(spot_cols[1], col_scr.shape)
+    first_t_scr[...] = dot_t(flags(iota(wide, 0) == rows[0]), counts[0][...])
+    eye = flags(iota((CLUSTERS, CLUSTERS), 0) == iota((CLUSTERS, CLUSTERS), 1))
+    flip_scr[...] = dot_t(eye, counts[1][...]).astype(BF16)
+    set_scr[...] = flags(iota(tall, 1) == cols[0])
+    first_scr[...] = dot(counts[0][...], set_scr[...])
+
+    def misfits():
+        eye = iota(shape, 0) == iota(shape, 1)
+        return float(owners) - jnp.sum(jnp.where(eye, state_scr[0:owners, :], 0.0))
+
+    def fits(by_row, by_lane):
+        most = jnp.zeros(shape, F32)
+        for s in range(owners):
+            most = jnp.maximum(most, by_row[:, s : s + 1] + by_lane[s : s + 1, :])
+        return jnp.where((most <= float(room)) & (iota(shape, 1) < owners), 1.0, 0.0)
+
+    def trade(step):
+        eye = iota(shape, 0) == iota(shape, 1)
+        fit = state_scr[0:owners, :]
+        pairs = fit * turned_scr[0:owners, :]
+        fine = jnp.where(eye, fit, 0.0)
+        fine_row = jnp.sum(fine, axis=0, keepdims=True)
+        fine_col = jnp.sum(fine, axis=1, keepdims=True)
+
+        def granted(asker, asked, bad, good, axis):
+            order = (asker * 37 + asked * 11 + step * 7) & (owners - 1)
+            asks = pairs * (1.0 - bad) * good * (order + 1).astype(F32)
+            asks = jnp.where(asks == jnp.max(asks, axis=axis, keepdims=True), asks, 0.0)
+            asks = jnp.where(asks == jnp.max(asks, axis=1 - axis, keepdims=True), asks, 0.0)
+            return jnp.minimum(asks, 1.0)
+
+        both = granted(iota(shape, 0), iota(shape, 1), fine_col, fine_row, 1)
+        both += granted(iota(shape, 1), iota(shape, 0), fine_row, fine_col, 0)
+        settled = 1.0 - jnp.sum(both, axis=0, keepdims=True)
+        move_scr[...] = jnp.where(
+            iota(square, 0) == iota(square, 1), settled, 0.0
+        ).astype(BF16)
+        move_scr[0:owners, :] = (both + jnp.where(eye, settled, 0.0)).astype(BF16)
+        state_scr[...] = dot(state_scr[...].astype(BF16), move_scr[...])
+        turned_scr[...] = dot(move_scr[...], turned_scr[...].astype(BF16))
+
+    def attempt(carry):
+        turn, _ = carry
+        at_row, _ = deal(row_scr[0:1, :], owners, turn)
+        at_col, _ = deal(col_scr[...], owners, turn)
+        set_scr[...] = flags(iota(tall, 1) == at_col)
+        second = dot(count_scr[...], set_scr[...])
+        second_t = dot(flags(iota(wide, 0) == at_row), flip_scr[...])
+        state_scr[...] = iota(square, 1).astype(F32)
+        state_scr[0:owners, :] = fits(first_t_scr[...], second)
+        turned_scr[...] = jnp.zeros(square, F32)
+        turned_scr[0:owners, :] = fits(second_t, first_scr[...])
+
+        def trades(carry):
+            step, _ = carry
+            trade(step)
+            return step + 1, misfits()
+
+        _, left = lax.while_loop(
+            lambda c: (c[1] > 0.5) & (c[0] < 6), trades, (jnp.int32(0), misfits())
+        )
+        return turn + 1, left
+
+    turn, left = lax.while_loop(
+        lambda c: (c[1] > 0.5) & (c[0] < 8), attempt, (jnp.int32(0), jnp.float32(1.0))
+    )
+    label = state_scr[owners : owners + 1, :]
+    eye = iota(shape, 0) == iota(shape, 1)
+    label_col = jnp.sum(jnp.where(eye, label, 0.0), axis=1, keepdims=True).astype(I32)
+    at_row, _ = deal(row_scr[0:1, :], owners, turn - 1)
+    at_col, _ = deal(col_scr[...], owners, turn - 1)
+    row = jnp.where(label_col == at_row, iota(wide, 0).astype(F32), 0.0)
+    rows[1] = jnp.sum(row, axis=0, keepdims=True).astype(I32)
+    col = jnp.where(label.astype(I32) == at_col, iota(tall, 1).astype(F32), 0.0)
+    cols[1] = jnp.sum(col, axis=1, keepdims=True).astype(I32)
+    return rows, cols, level_rows, level_cols, left
 
 
 def plan_kernel(
@@ -62,17 +160,17 @@
     ends_t_ref,
     sums_row_ref,
     sums_col_ref,
+    first_ref,
     over_ref,
+    *scratch,
 ):
     me = me_ref[0]
     owners = all_ref.shape[0]
     owned = CLUSTERS // owners
     heads = ids_ref.shape[0]
-    square = (CLUSTERS, CLUSTERS)
     cluster_row = iota((1, CLUSTERS), 1).astype(F32)
     home = flags(iota((owners, CLUSTERS), 1) // owned == iota((owners, CLUSTERS), 0))
-    owner_lane = iota((CLUSTERS, LANES), 1)
-    counts, spots, loads = [], [], []
+    counts, spot_rows, spot_cols = [], [], []
     for h in range(heads):
         count = all_ref[:, h * CLUSTERS : (h + 1) * CLUSTERS]
         total = jnp.sum(count.astype(F32), axis=0, keepdims=True)
@@ -81,31 +179,14 @@
         spot_row = jnp.sum(jnp.where(order_col > order_row, 1.0, 0.0), axis=0, keepdims=True)
         spot_col = jnp.sum(jnp.where(order_row > order_col, 1.0, 0.0), axis=1, keepdims=True)
         counts.append(count)
-        spots.append((spot_row.astype(I32), spot_col.astype(I32)))
-        tries = []
-        for turn in range(1 if h == 0 else DEALS):
-            at_col, _ = deal(spots[h][1], owners, turn)
-            load = dot((count.astype(F32) + home.astype(F32)).astype(BF16), flags(at_col == owner_lane))
-            tries.append(load)
-        loads.append(tries)
-    fits = [
-        jnp.max(jnp.max(loads[0][0] + load, axis=1, keepdims=True), axis=0, keepdims=True)
-        <= float(room)
-        for load in loads[1]
-    ]
-    over_ref[...] = jnp.broadcast_to(
-        jnp.where(fits[0] | fits[1] | fits[2], 0.0, 1.0), over_ref.shape
-    )
-    at_rows, at_cols, level_rows, level_cols = [], [], [], []
-    for h in range(heads):
-        for axis, at, level in ((0, at_rows, level_rows), (1, at_cols, level_cols)):
-            chosen, lev = deal(spots[h][axis], owners, 0)
-            if h == 1:
-                second, _ = deal(spots[h][axis], owners, 1)
-                third, _ = deal(spots[h][axis], owners, 2)
-                chosen = jnp.where(fits[0], chosen, jnp.where(fits[1], second, third))
-            at.append(chosen)
-            level.append(lev)
+        spot_rows.append(spot_row.astype(I32))
+        spot_cols.append(spot_col.astype(I32))
+    for scr, count in zip(scratch[:heads], counts):
+        scr[...] = (count.astype(F32) + home.astype(F32)).astype(BF16)
+    at_rows, at_cols, level_rows, level_cols, left = match(
+        room, scratch[:heads], spot_rows, spot_cols, scratch[heads:]
+    )
+    over_ref[...] = jnp.full(over_ref.shape, jnp.where(left > 0.5, 1.0, 0.0))
 
     owns = [jnp.broadcast_to(own_ref[h : h + 1, :], (8, CLUSTERS)).astype(BF16) for h in range(heads)]
     for h in range(heads):
@@ -167,6 +248,8 @@
             jnp.where(hit, (level_rows[h] + h * owned).astype(F32), 0.0), axis=1, keepdims=True
         )
         sent += dot(owns[h], flags(at_cols[h] == lane))
+        if h == 0:
+            first_ref[...] = sent
     small = iota((items, LANES), 1)
     ahead = (at_lane == at_item) & (turn_lane < turn_item) & (small < items)
     queue = jnp.sum(jnp.where(ahead, 1.0, 0.0), axis=1, keepdims=True)
@@ -186,7 +269,7 @@
     return pl.pallas_call(
         functools.partial(plan_kernel, room),
         in_specs=[pl.BlockSpec(memory_space=pltpu.SMEM), vmem, vmem, vmem, vmem],
-        out_specs=[vmem] * 6,
+        out_specs=[vmem] * 7,
         out_shape=(
             jax.ShapeDtypeStruct((heads, toks), I32),
             jax.ShapeDtypeStruct((owners, LANES), F32),
@@ -194,34 +277,58 @@
             jax.ShapeDtypeStruct((8, LANES), I32),
             jax.ShapeDtypeStruct((items, LANES), I32),
             jax.ShapeDtypeStruct((8, LANES), F32),
+            jax.ShapeDtypeStruct((8, LANES), F32),
         ),
+        scratch_shapes=[
+            pltpu.VMEM((owners, CLUSTERS), BF16),
+            pltpu.VMEM((owners, CLUSTERS), BF16),
+            pltpu.VMEM((CLUSTERS, LANES), BF16),
+            pltpu.VMEM((CLUSTERS, owners), BF16),
+            pltpu.VMEM((LANES, LANES), BF16),
+            pltpu.VMEM((8, CLUSTERS), I32),
+            pltpu.VMEM((CLUSTERS, LANES), I32),
+            pltpu.VMEM((owners, LANES), F32),
+            pltpu.VMEM((owners, owners), F32),
+            pltpu.VMEM((LANES, LANES), F32),
+            pltpu.VMEM((LANES, LANES), F32),
+        ],
         compiler_params=PARAMS,
         cost_estimate=pl.CostEstimate(flops=10**9, bytes_accessed=10**6, transcendentals=0),
     )(me, everyone, own, cluster_ids, rank)
 
 
-def pack_kernel(place_ref, q_ref, k_ref, v_ref, out_ref):
+def pack_kernel(room, place_ref, first_ref, q_ref, k_ref, v_ref, out_ref):
     rows, toks = out_ref.shape[0], q_ref.shape[0]
-    heads = place_ref.shape[0]
-    width = q_ref.shape[1] // heads
-    wanted = iota((rows, toks), 0) + pl.program_id(0) * rows
-    picks = [flags(wanted == place_ref[h : h + 1, :]) for h in range(heads)]
+    width = out_ref.shape[1] // 3
+    base = pl.program_id(0) * rows
+    wanted = iota((rows, toks), 0) + base
+    pick = flags((wanted == place_ref[0:1, :]) | (wanted == place_ref[1:2, :]))
+    place = iota((rows, LANES), 0) + base
+    here = (place >> shift_of(room)) == iota((rows, LANES), 1)
+    first = jnp.sum(jnp.where(here, first_ref[0:1, :], 0.0), axis=1, keepdims=True)
+    is_first = (place[:, 0:1] & (room - 1)).astype(F32) < first
     for part, ref in enumerate((q_ref, k_ref, v_ref)):
-        moved = jnp.zeros((rows, width), F32)
-        for h in range(heads):
-            moved += dot(picks[h], ref[:, h * width : (h + 1) * width])
+        moved = dot(pick, ref[...])
+        moved = jnp.where(is_first, moved[:, 0:width], moved[:, width:])
         out_ref[:, part * width : (part + 1) * width] = moved.astype(out_ref.dtype)
 
 
-def pack(place, queries, keys, values, rows_all):
+def pack(place, first, queries, keys, values, room, owners):
     toks, width = queries.shape
     heads = place.shape[0]
+    rows_all = owners * room
     tile = 512
     whole = pl.BlockSpec((toks, width), lambda i: (0, 0))
     return pl.pallas_call(
-        pack_kernel,
+        functools.partial(pack_kernel, room),
         grid=(rows_all // tile,),
-        in_specs=[pl.BlockSpec((heads, toks), lambda i: (0, 0)), whole, whole, whole],
+        in_specs=[
+            pl.BlockSpec((heads, toks), lambda i: (0, 0)),
+            pl.BlockSpec(first.shape, lambda i: (0, 0)),
+            whole,
+            whole,
+            whole,
+        ],
         out_specs=pl.BlockSpec((tile, 3 * width // heads), lambda i: (i, 0)),
         out_shape=jax.ShapeDtypeStruct((rows_all, 3 * width // heads), queries.dtype),
         compiler_params=PARAMS,
@@ -230,20 +337,26 @@
             bytes_accessed=rows_all * width * 3,
             transcendentals=0,
         ),
-    )(place, queries, keys, values)
-
-
-def row_ids(room, rows, ends_ref, ends_t_ref):
+    )(place, first, queries, keys, values)
+
+
+def ids_along(room, rows, ends_t_ref):
     items, sources = ends_t_ref.shape
-    spread = flags(iota((sources, rows), 1) // room == iota((sources, rows), 0))
+    spread = flags((iota((sources, rows), 1) >> shift_of(room)) == iota((sources, rows), 0))
     ends_row = dot(ends_t_ref[...].astype(BF16), spread)
-    slot_row = (iota((items, rows), 1) % room).astype(F32)
-    id_row = jnp.sum(jnp.where(ends_row <= slot_row, 1.0, 0.0), axis=0, keepdims=True)
-    spread = flags(iota((rows, sources), 0) // room == iota((rows, sources), 1))
-    ends_col = dot(spread, ends_ref[...].astype(BF16))
-    slot_col = (iota((rows, LANES), 0) % room).astype(F32)
-    past = (ends_col <= slot_col) & (iota((rows, LANES), 1) < items)
-    return id_row, jnp.sum(jnp.where(past, 1.0, 0.0), axis=1, keepdims=True)
+    slot_row = (iota((items, rows), 1) & (room - 1)).astype(F32)
+    return jnp.sum(jnp.where(ends_row <= slot_row, 1.0, 0.0), axis=0, keepdims=True)
+
+
+def ids_down(room, rows, items, ends_ref):
+    sources = ends_ref.shape[0]
+    spread = flags((iota((rows, sources), 0) >> shift_of(room)) == iota((rows, sources), 1))
+    lane = iota(ends_ref.shape, 1)
+    ends = jnp.where(lane < items, ends_ref[...], float(2 * LANES))
+    starts = jnp.where(lane == 0, 0.0, pltpu.roll(ends, 1, 1))
+    bounds = dot(spread, jnp.concatenate([starts, ends], axis=1).astype(BF16))
+    slot = (iota((rows, LANES), 0) & (room - 1)).astype(F32)
+    return (bounds[:, 0:LANES] <= slot) & (slot < bounds[:, LANES:])
 
 
 def unit_sums(key_rows, id_row, items):
@@ -274,46 +387,79 @@
     return dot(pick[:, 0 : sums.shape[0]], sums)
 
 
-def attend_kernel(room, ends_ref, ends_t_ref, sums_row_ref, x_ref, out_ref):
+def fill(room, ends_ref, ends_t_ref, x_ref, query_scr, key_scr, value_scr):
+    rows, width = x_ref.shape[0], x_ref.shape[1] // 3
+    items = ends_t_ref.shape[0]
+    inside = ids_down(room, rows, items, ends_ref)
+    query_scr[:, 0:width] = x_ref[:, 0:width]
+    query_scr[:, width:] = jnp.where(inside, 0.0, -FAR).astype(BF16)
+    key_scr[:, 0:width] = x_ref[:, width : 2 * width]
+    key_scr[:, width:] = flags(inside)
+    value_scr[:, 0:width] = x_ref[:, 2 * width : 3 * width]
+    value_scr[:, width:] = jnp.ones((rows, LANES), BF16)
+    return unit_sums(x_ref[:, width : 2 * width], ids_along(room, rows, ends_t_ref), items)
+
+
+def weigh(pieces, values, width):
+    scale = math.log2(math.e) / math.sqrt(width)
+    highest = jnp.max(pieces[0], axis=1, keepdims=True)
+    for scores in pieces[1:]:
+        highest = jnp.maximum(highest, jnp.max(scores, axis=1, keepdims=True))
+    result = jnp.zeros((highest.shape[0], width + LANES), F32)
+    for scores, value in zip(pieces, values):
+        raised = jnp.exp2((scores - highest) * scale)
+        result += dot(raised.astype(BF16), value)
+    return result[:, 0:width] / result[:, width : width + 1]
+
+
+def homeward(begin, tile, sums_row_ref, sums):
+    pick = flags(iota((tile, LANES), 0) + begin == sums_row_ref[0:1, :])
+    return dot(pick[:, 0 : sums.shape[0]], sums)
+
+
+def attend_kernel(
+    room, ends_ref, ends_t_ref, sums_row_ref, x_ref, out_ref, query_scr, key_scr, value_scr
+):
     rows, width = out_ref.shape
-    id_row, id_col = row_ids(room, rows, ends_ref, ends_t_ref)
-    sums = unit_sums(x_ref[:, width : 2 * width], id_row, ends_t_ref.shape[0])
+    sums = fill(room, ends_ref, ends_t_ref, x_ref, query_scr, key_scr, value_scr)
     for begin in range(0, rows, TILE):
         end = begin + TILE
-        query = x_ref[begin:end, 0:width]
-        at = id_col[begin:end]
+        query = query_scr[begin:end, :]
         pieces, values = [], []
         if begin:
-            scores = dot_t(query, x_ref[0:begin, width : 2 * width])
-            pieces.append(jnp.where(at == id_row[:, 0:begin], scores, -1e30))
-            values.append(x_ref[0:begin, 2 * width : 3 * width])
-        scores = dot_t(query, x_ref[begin:end, width : 2 * width])
-        allowed = (at == id_row[:, begin:end]) & (iota((TILE, TILE), 1) <= iota((TILE, TILE), 0))
-        pieces.append(jnp.where(allowed, scores, -1e30))
-        values.append(x_ref[begin:end, 2 * width : 3 * width])
+            pieces.append(dot_t(query, key_scr[0:begin, :]))
+            values.append(value_scr[0:begin, :])
+        scores = dot_t(query, key_scr[begin:end, :])
+        allowed = iota((TILE, TILE), 1) <= iota((TILE, TILE), 0)
+        pieces.append(jnp.where(allowed, scores, -FAR))
+        values.append(value_scr[begin:end, :])
         result = weigh(pieces, values, width) + homeward(begin, TILE, sums_row_ref, sums)
         out_ref[begin:end] = result.astype(out_ref.dtype)
 
 
 def attend_tile_kernel(
-    room, ends_ref, ends_t_ref, sums_row_ref, x_ref, out_ref, row_scr, col_scr, sums_scr
+    room,
+    ends_ref,
+    ends_t_ref,
+    sums_row_ref,
+    x_ref,
+    out_ref,
+    query_scr,
+    key_scr,
+    value_scr,
+    sums_scr,
 ):
     tile, width = out_ref.shape
     rows = x_ref.shape[0]
 
     @pl.when(pl.program_id(0) == 0)
     def _():
-        id_row, id_col = row_ids(room, rows, ends_ref, ends_t_ref)
-        row_scr[...] = jnp.broadcast_to(id_row, row_scr.shape)
-        col_scr[...] = jnp.broadcast_to(id_col, col_scr.shape)
-        sums_scr[...] = unit_sums(x_ref[:, width : 2 * width], id_row, ends_t_ref.shape[0])
+        sums_scr[...] = fill(room, ends_ref, ends_t_ref, x_ref, query_scr, key_scr, value_scr)
 
     begin = pl.multiple_of(pl.program_id(0) * tile, tile)
-    scores = dot_t(x_ref[pl.ds(begin, tile), 0:width], x_ref[:, width : 2 * width])
-    allowed = (col_scr[pl.ds(begin, tile), 0:1] == row_scr[0:1, :]) & (
-        iota((tile, rows), 1) <= iota((tile, rows), 0) + begin
-    )
-    result = weigh([jnp.where(allowed, scores, -1e30)], [x_ref[:, 2 * width : 3 * width]], width)
+    scores = dot_t(query_scr[pl.ds(begin, tile), :], key_scr[...])
+    allowed = iota((tile, rows), 1) <= iota((tile, rows), 0) + begin
+    result = weigh([jnp.where(allowed, scores, -FAR)], [value_scr[...]], width)
     out_ref[...] = (result + homeward(begin, tile, sums_row_ref, sums_scr[...])).astype(out_ref.dtype)
 
 
@@ -326,10 +472,12 @@
         transcendentals=rows * rows // 2,
     )
     given = (ends, ends_t, sums_row, received)
+    filled = [pltpu.VMEM((rows, width + LANES), BF16)] * 3
     if rows <= 4096:
         return pl.pallas_call(
             functools.partial(attend_kernel, room),
             out_shape=shape,
+            scratch_shapes=filled,
             compiler_params=PARAMS,
             cost_estimate=cost,
         )(*given)
@@ -340,53 +488,57 @@
         in_specs=[pl.BlockSpec(x.shape, lambda i: (0, 0)) for x in given],
         out_specs=pl.BlockSpec((tile, width), lambda i: (i, 0)),
         out_shape=shape,
-        scratch_shapes=[
-            pltpu.VMEM((8, rows), F32),
-            pltpu.VMEM((rows, LANES), F32),
-            pltpu.VMEM((ends_t.shape[0], width), BF16),
-        ],
+        scratch_shapes=filled + [pltpu.VMEM((ends_t.shape[0], width), BF16)],
         compiler_params=PARAMS,
         cost_estimate=cost,
     )(*given)
 
 
 def unpack_kernel(place_ref, sums_col_ref, over_ref, back_ref, out_ref, sums_ref):
-    toks, rows = place_ref.shape[0], back_ref.shape[0]
-    width = back_ref.shape[1]
+    toks, heads = place_ref.shape
+    rows, width = back_ref.shape
+    groups = out_ref.shape[0]
+    share = toks // groups
     back = back_ref[...]
-    for h in range(place_ref.shape[1]):
+    for h in range(heads):
         pick = flags(iota((toks, rows), 1) == place_ref[:, h : h + 1])
-        moved = dot(pick, back)
-        out_ref[0, 0:toks, h * width : (h + 1) * width] = moved.astype(out_ref.dtype)
-    spare = out_ref.shape[1] - toks
-    out_ref[0, toks:, :] = jnp.broadcast_to(over_ref[0:1, 0:1], (spare, out_ref.shape[2])).astype(
-        out_ref.dtype
-    )
-    items = sums_col_ref.shape[0]
-    pick = flags(iota((items, rows), 1) == sums_col_ref[:, 0:1])
-    sums_ref[...] = dot(pick, back)
+        moved = dot(pick, back).astype(out_ref.dtype)
+        for g in range(groups):
+            out_ref[g, 0:share, h * width : (h + 1) * width] = moved[g * share : (g + 1) * share]
+    spare = out_ref.shape[1] - share
+    for g in range(groups):
+        out_ref[g, share:, :] = jnp.broadcast_to(
+            over_ref[0:1, 0:1], (spare, out_ref.shape[2])
+        ).astype(out_ref.dtype)
+
+    @pl.when(pl.program_id(0) == 0)
+    def _():
+        items = sums_col_ref.shape[0]
+        pick = flags(iota((items, rows), 1) == sums_col_ref[:, 0:1])
+        sums_ref[...] = dot(pick, back)
 
 
 def unpack(place, sums_col, over, back, groups):
     (toks, heads), (rows, width) = place.shape, back.shape
-    tile = toks // groups
+    share = toks // groups
     items = sums_col.shape[0]
+    steps = max(1, min(groups, groups * rows // 8192))
     whole = lambda i: (0, 0)
     return pl.pallas_call(
         unpack_kernel,
-        grid=(groups,),
+        grid=(steps,),
         in_specs=[
-            pl.BlockSpec((tile, heads), lambda i: (i, 0)),
+            pl.BlockSpec((toks // steps, heads), lambda i: (i, 0)),
             pl.BlockSpec(sums_col.shape, whole),
             pl.BlockSpec(over.shape, whole),
             pl.BlockSpec((rows, width), whole),
         ],
         out_specs=(
-            pl.BlockSpec((1, tile + 16, heads * width), lambda i: (i, 0, 0)),
+            pl.BlockSpec((groups // steps, share + 16, heads * width), lambda i: (i, 0, 0)),
             pl.BlockSpec((items, width), whole),
         ),
         out_shape=(
-            jax.ShapeDtypeStruct((groups, tile + 16, heads * width), back.dtype),
+            jax.ShapeDtypeStruct((groups, share + 16, heads * width), back.dtype),
             jax.ShapeDtypeStruct((items, width), F32),
         ),
         compiler_params=PARAMS,
@@ -406,10 +558,10 @@
     heads = cluster_ids.shape[0]
     owners = everyone.shape[0]
     me = lax.axis_index("seq").astype(I32)[None]
-    place, ends, ends_t, sums_row, sums_col, over = make_plan(
+    place, ends, ends_t, sums_row, sums_col, first, over = make_plan(
         me, everyone, own, cluster_ids, rank, room
     )
-    sent = pack(place, queries, keys, values, owners * room)
+    sent = pack(place, first, queries, keys, values, room, owners)
     received = exchange(sent, "seq")
     back = exchange(attend(ends, ends_t, sums_row, received, room), "seq")
     share, sums = unpack(place.T, sums_col, over, back, lax.axis_size("head"))
@@ -439,7 +591,7 @@
     rank = jnp.sum((same & (spot[:, None] < spot[None, :])[None]).astype(I32), axis=1)
     given = (queries, keys, values, cluster_ids, rank, own, everyone)
     parts, key_sums = routed(ROOM, *given)
-    full_room = -(-heads * CLUSTERS // owners * (MOST + 1) // 16) * 16
+    full_room = 1 << (heads * CLUSTERS // owners * (MOST + 1) - 1).bit_length()
 
     def again():
         wide, wide_sums = routed(full_room, *given)

time: 241 us -> 884 us (3.67)
  blocking collectives: 96 us -> 359 us
  Pallas kernels: 24.7 us -> 281 us
  waiting for transfers between devices: 56.2 us -> 155 us
  starting transfers between devices: 38.9 us -> 61.8 us
    all_to_all x1 -> x2, blocking collectives: 96 us -> 359 us  [exchange(): return lax.all_to_all(rows, axis, split_axis=0, concat_axis=0, tiled=True)]
    pallas_call x3 -> x6, Pallas kernels: 21.8 us -> 272 us  [the longest x1 235 us: attend(): pl.pallas_call(functools.partial(attend_tile_kernel, room), grid=(rows //...]
    all_to_all x3 -> x5, waiting for transfers between devices: 55.5 us -> 154 us  [exchange(): return lax.all_to_all(rows, axis, split_axis=0, concat_axis=0, tiled=True)]
    all_to_all x3 -> x5, starting transfers between devices: 38.9 us -> 61.8 us  [exchange(): return lax.all_to_all(rows, axis, split_axis=0, concat_axis=0, tiled=True)]
  transfers between devices with their start and end apart: 4 -> 6, of which waited for: 3 -> 5; matrix products, arithmetic and copies ran while one was open for 2% -> 1% of each run, Pallas kernels for 10% -> 2%
where the time goes in v4:
time: 884 us; the launch traced here: 883 us
  blocking collectives  359 us (41%)
  Pallas kernels  281 us (32%)
  waiting for transfers between devices  155 us (18%)
  starting transfers between devices  61.8 us (7%)
  between operations  14.8 us (2%)
    all_to_all x2, blocking collectives, exchange(): return lax.all_to_all(rows, axis, split_axis=0, concat_axis=0, tiled=True)  359 us
    pallas_call x1, Pallas kernels, attend(): pl.pallas_call(functools.partial(attend_tile_kernel, room), grid=(rows //...  235 us
    all_to_all x5, waiting for transfers between devices, exchange(): return lax.all_to_all(rows, axis, split_axis=0, concat_axis=0, tiled=True)  154 us
    all_to_all x5, starting transfers between devices, exchange(): return lax.all_to_all(rows, axis, split_axis=0, concat_axis=0, tiled=True)  61.8 us
    pallas_call x2, Pallas kernels, pack(): pl.pallas_call(functools.partial(pack_kernel, room), grid=(rows_all // ti...  18.6 us
  transfers between devices with their start and end apart: 6, of which 5 were waited for; matrix products, arithmetic and copies ran while one was open for 1% of the time, Pallas kernels for 2%

profile of v4, /device:TPU:1, one launch (start us, length us, event | category | flops | bytes accessed | tf_op | source)
XLA Modules:
  0.0 883.3 jit_solution(16504034025601080813)
XLA Ops:
  7.2 0.0 copy-start.4
  7.2 0.0 copy-start.5
  7.2 0.0 copy-start.6
  7.2 0.0 all-gather.2.cloned.1.call-start
  7.2 0.7 all-gather.2.cloned.1.call-update
  7.9 1.1 convert_reduce_fusion.1.own_ref
  9.1 0.7 broadcast_in_dim.7
  9.7 19.3 %all-to-all-start.3 = ((bf16[64,8,128]{2,1,0:T(8,128)(2,1)}), bf16[64,8,128]{2,1,0:T(8,128)(2,1)S(1)}, u32[]{:S(2)}, u32[]{:S(2)}) async-start(bf16[64,8,128]{2,1,0:T(8,128)(2,1)} %broadcast_in_dim.7), calls=%async_computation.3 | async-start | bytes 262144 | tf_op jit(solution)/shard_map/all_to_all | solution.py:554
  29.0 0.2 iota_compare_fusion.1
  29.2 1.6 convert_reduce_fusion.rank_ref
  30.9 13.1 %all-to-all-done.3 = bf16[64,8,128]{2,1,0:T(8,128)(2,1)S(1)} async-done(((bf16[64,8,128]{2,1,0:T(8,128)(2,1)}), bf16[64,8,128]{2,1,0:T(8,128)(2,1)S(1)}, u32[]{:S(2)}, u32[]{:S(2)}) %all-to-all-start.3) | async-done | bytes 131104 | tf_op jit(solution)/shard_map/all_to_all | solution.py:554
  44.0 5.2 shard_map.68
  49.1 0.0 copy-done.4
  49.1 0.0 copy-done.5
  49.1 0.0 copy-done.6
  49.1 3.6 shard_map.69
  52.7 79.0 %all_to_all.53 = bf16[64,32,384]{2,1,0:T(8,128)(2,1)S(1)} all-to-all(bf16[64,32,384]{2,1,0:T(8,128)(2,1)S(1)} %bitcast.31), channel_id=1, replica_groups=mesh['seq'=64,'head'=8] {'seq'}, dimensions={0} | all-to-all | bytes 3145728 | tf_op jit(solution)/shard_map/all_to_all | solution.py:554
  131.8 0.0 copy-start.2
  131.8 6.6 shard_map.70
  138.4 9.9 %all-to-all-start.5 = ((bf16[64,32,128]{2,1,0:T(8,128)(2,1)}), bf16[64,32,128]{2,1,0:T(8,128)(2,1)S(1)}, u32[]{:S(2)}, u32[]{:S(2)}) async-start(bf16[64,32,128]{2,1,0:T(8,128)(2,1)} %bitcast.14), calls=%async_computation.5 | async-start | bytes 1048576 | tf_op jit(solution)/shard_map/all_to_all | solution.py:554
  148.3 0.2 copy.10
  148.5 28.7 %all-to-all-done.5 = bf16[64,32,128]{2,1,0:T(8,128)(2,1)S(1)} async-done(((bf16[64,32,128]{2,1,0:T(8,128)(2,1)}), bf16[64,32,128]{2,1,0:T(8,128)(2,1)S(1)}, u32[]{:S(2)}, u32[]{:S(2)}) %all-to-all-start.5) | async-done | bytes 524320 | tf_op jit(solution)/shard_map/all_to_all | solution.py:554
  177.2 3.0 shard_map.71
  180.3 12.1 %all-to-all-start.6 = ((bf16[8,112,256]{2,1,0:T(8,128)(2,1)}), bf16[8,112,256]{2,1,0:T(8,128)(2,1)S(1)}, u32[]{:S(2)}, u32[]{:S(2)}) async-start(bf16[8,112,256]{2,1,0:T(8,128)(2,1)} %get-tuple-element.65), calls=%async_computation.6 | async-start | bytes 917504 | tf_op jit(solution)/shard_map/all_to_all | solution.py:554
  192.4 8.8 all-to-all-done.6
  201.2 0.6 slice_reduce_fusion
  202.4 0.0 all-gather.2.cloned.1.call-done
  202.5 0.0 copy-done.2
  202.5 673.2 %conditional.2 = (f32[8,256]{1,0:T(8,128)S(1)}, bf16[96,2048]{1,0:T(8,128)(2,1)S(1)}) conditional(s32[]{:T(128)} %convert_element_type.29, (bf16[8,112,256]{2,1,0:T(8,128)(2,1)S(1)}, bf16[2048,2048]{1,0:T(8,128)(2,1)}, f32[8,256]{1,0:T(8,128)S(1)}) %tuple.19, (bf16[64,1024]{1,0:T(8,128)(2,1)S(1)}, f32[2,512]{1,0:T(2,128)S(1)}, ...), branch_computations={%region_3.0_spmd, %region_4.0_spmd} | conditional | flops 31870275584 | bytes 55636684
  202.5 3.5 branch_1_fun.4
  206.0 15.1 %branch_1_fun.5 = bf16[8192,384]{1,0:T(8,128)(2,1)} custom-call(s32[2,768]{1,0:T(2,128)S(1)} %get-tuple-element.32.place_ref, f32[8,128]{1,0:T(8,128)S(1)} %get-tuple-element.38.first_ref, bf16[768,256]{1,0:T(8,128)(2,1)S(1)} %get-tuple-element.39.q_ref, bf16[768,256]{1,0:T(8,128)(2,1)S(1)} %get-tuple-element.40.k_ref, ...), custom_call_target="tpu_custom_call" | custom-call | flops 9663676416 | bytes 6291456 | tf_op jit(solution)/shard_map/cond/branch_1_fun/pallas_call | solution.py:322
  221.1 280.3 %all_to_all.52 = bf16[64,128,384]{2,1,0:T(8,128)(2,1)} all-to-all(bf16[64,128,384]{2,1,0:T(8,128)(2,1)} %bitcast.38), channel_id=1, replica_groups=mesh['seq'=64,'head'=8] {'seq'}, dimensions={0} | all-to-all | bytes 12582912 | tf_op jit(solution)/shard_map/cond/branch_1_fun/all_to_all | solution.py:554
  501.4 234.5 %branch_1_fun.6 = bf16[8192,128]{1,0:T(8,128)(2,1)S(1)} custom-call(f32[64,128]{1,0:T(8,128)S(1)} %get-tuple-element.35.ends_ref, f32[16,64]{1,0:T(8,128)S(1)} %get-tuple-element.36.ends_t_ref, s32[8,128]{1,0:T(8,128)S(1)} %get-tuple-element.37.sums_row_ref, bf16[8192,384]{1,0:T(8,128)(2,1)} %bitcast.37), custom_call_target="tpu_custom_call" | custom-call | flops 17179869184 | bytes 8388608 | tf_op jit(solution)/shard_map/cond/branch_1_fun/pallas_call | solution.py:485
  735.9 0.0 copy-start
  735.9 1.4 copy-done
  737.3 10.6 %all-to-all-start.1 = ((bf16[64,128,128]{2,1,0:T(8,128)(2,1)}), bf16[64,128,128]{2,1,0:T(8,128)(2,1)S(1)}, u32[]{:S(2)}, u32[]{:S(2)}) async-start(bf16[64,128,128]{2,1,0:T(8,128)(2,1)} %bitcast.29), calls=%async_computation.1 | async-start | bytes 4194304 | tf_op jit(solution)/shard_map/cond/branch_1_fun/all_to_all | solution.py:554
  748.0 0.2 copy.9
  748.1 94.6 %all-to-all-done.1 = bf16[64,128,128]{2,1,0:T(8,128)(2,1)S(1)} async-done(((bf16[64,128,128]{2,1,0:T(8,128)(2,1)}), bf16[64,128,128]{2,1,0:T(8,128)(2,1)S(1)}, u32[]{:S(2)}, u32[]{:S(2)}) %all-to-all-start.1) | async-done | bytes 2097184 | tf_op jit(solution)/shard_map/cond/branch_1_fun/all_to_all | solution.py:554
  842.7 9.5 %branch_1_fun.7 = (bf16[8,112,256]{2,1,0:T(8,128)(2,1)}, f32[16,128]{1,0:T(8,128)S(1)}) custom-call(s32[768,2]{1,0:T(8,128)S(1)} %bitcast.34, s32[16,128]{1,0:T(8,128)S(1)} %get-tuple-element.33.sums_col_ref, f32[8,128]{1,0:T(8,128)S(1)} %get-tuple-element.34.over_ref, bf16[8192,128]{1,0:T(8,128)(2,1)S(1)} %bitcast.28), custom_call_target="tpu_custom_call" | custom-call | flops 3221225472 | bytes 2097152 | tf_op jit(solution)/shard_map/cond/branch_1_fun/pallas_call | solution.py:527
  852.2 9.8 %all-to-all-start.2 = ((bf16[8,112,256]{2,1,0:T(8,128)(2,1)}), bf16[8,112,256]{2,1,0:T(8,128)(2,1)S(1)}, u32[]{:S(2)}, u32[]{:S(2)}) async-start(bf16[8,112,256]{2,1,0:T(8,128)(2,1)} %get-tuple-element.42), calls=%async_computation.2 | async-start | bytes 917504 | tf_op jit(solution)/shard_map/cond/branch_1_fun/all_to_all | solution.py:554
  862.0 8.8 all-to-all-done.2
  870.8 4.9 fusion.2
  875.7 0.0 copy-start.1
  875.7 0.0 copy-start.3
  875.7 0.7 copy-done.1
  876.4 0.0 copy-done.3
  (7 shorter events, 0.1 us)
Async XLA Ops:
  7.2 42.0 %copy-start.4 = (bf16[768,256]{1,0:T(8,128)(2,1)S(1)}, bf16[768,256]{1,0:T(8,128)(2,1)}, u32[]{:S(2)}) copy-start(bf16[768,256]{1,0:T(8,128)(2,1)} %q_ref.1) | copy-start | bytes 1179652
  7.2 41.9 %copy-start.5 = (bf16[768,256]{1,0:T(8,128)(2,1)S(1)}, bf16[768,256]{1,0:T(8,128)(2,1)}, u32[]{:S(2)}) copy-start(bf16[768,256]{1,0:T(8,128)(2,1)} %k_ref.1) | copy-start | bytes 1179652
  7.2 41.9 %copy-start.6 = (bf16[768,256]{1,0:T(8,128)(2,1)S(1)}, bf16[768,256]{1,0:T(8,128)(2,1)}, u32[]{:S(2)}) copy-start(bf16[768,256]{1,0:T(8,128)(2,1)} %v_ref.1) | copy-start | bytes 1179652
  7.2 195.3 %all-gather.2.cloned.1.call-start = ((), (), s32[]{:S(2)}) async-start(), calls=%async_computation.7 | async-start | bytes 9437184 | tf_op jit(solution)/shard_map/all_gather | solution.py:587
  9.7 34.2 %all-to-all-start.3 = ((bf16[64,8,128]{2,1,0:T(8,128)(2,1)}), bf16[64,8,128]{2,1,0:T(8,128)(2,1)S(1)}, u32[]{:S(2)}, u32[]{:S(2)}) async-start(bf16[64,8,128]{2,1,0:T(8,128)(2,1)} %broadcast_in_dim.7), calls=%async_computation.3 | async-start | bytes 262144 | tf_op jit(solution)/shard_map/all_to_all | solution.py:554
  131.8 70.7 %copy-start.2 = (s32[2,768]{1,0:T(2,128)S(1)}, s32[2,768]{1,0:T(2,128)}, u32[]{:S(2)}) copy-start(s32[2,768]{1,0:T(2,128)} %ids_ref.1) | copy-start | bytes 18436
  138.4 38.8 %all-to-all-start.5 = ((bf16[64,32,128]{2,1,0:T(8,128)(2,1)}), bf16[64,32,128]{2,1,0:T(8,128)(2,1)S(1)}, u32[]{:S(2)}, u32[]{:S(2)}) async-start(bf16[64,32,128]{2,1,0:T(8,128)(2,1)} %bitcast.14), calls=%async_computation.5 | async-start | bytes 1048576 | tf_op jit(solution)/shard_map/all_to_all | solution.py:554
  180.3 20.9 %all-to-all-start.6 = ((bf16[8,112,256]{2,1,0:T(8,128)(2,1)}), bf16[8,112,256]{2,1,0:T(8,128)(2,1)S(1)}, u32[]{:S(2)}, u32[]{:S(2)}) async-start(bf16[8,112,256]{2,1,0:T(8,128)(2,1)} %get-tuple-element.65), calls=%async_computation.6 | async-start | bytes 917504 | tf_op jit(solution)/shard_map/all_to_all | solution.py:554
  735.9 1.4 copy-start
  737.3 105.4 %all-to-all-start.1 = ((bf16[64,128,128]{2,1,0:T(8,128)(2,1)}), bf16[64,128,128]{2,1,0:T(8,128)(2,1)S(1)}, u32[]{:S(2)}, u32[]{:S(2)}) async-start(bf16[64,128,128]{2,1,0:T(8,128)(2,1)} %bitcast.29), calls=%async_computation.1 | async-start | bytes 4194304 | tf_op jit(solution)/shard_map/cond/branch_1_fun/all_to_all | solution.py:554
  852.2 18.6 %all-to-all-start.2 = ((bf16[8,112,256]{2,1,0:T(8,128)(2,1)}), bf16[8,112,256]{2,1,0:T(8,128)(2,1)S(1)}, u32[]{:S(2)}, u32[]{:S(2)}) async-start(bf16[8,112,256]{2,1,0:T(8,128)(2,1)} %get-tuple-element.42), calls=%async_computation.2 | async-start | bytes 917504 | tf_op jit(solution)/shard_map/cond/branch_1_fun/all_to_all | solution.py:554
  875.7 0.7 copy-start.1
  875.7 0.7 copy-start.3
Sparse Core Ops, SparseCore 0:
  10.2 63.0 all-gather.1

commit v5 on v4

--- a/solution.py
+++ b/solution.py
@@ -14,7 +14,7 @@
 TILE = 256
 FAR = 2.0**100
 LANES = 128
-PARAMS = pltpu.CompilerParams(vmem_limit_bytes=48 * 1024 * 1024)
+PARAMS = pltpu.CompilerParams(vmem_limit_bytes=40 * 1024 * 1024)
 F32 = jnp.float32
 BF16 = jnp.bfloat16
 I32 = jnp.int32
@@ -149,22 +149,8 @@
 
 
 def plan_kernel(
-    room,
-    me_ref,
-    all_ref,
-    own_ref,
-    ids_ref,
-    rank_ref,
-    place_ref,
-    ends_ref,
-    ends_t_ref,
-    sums_row_ref,
-    sums_col_ref,
-    first_ref,
-    over_ref,
-    *scratch,
+    room, all_ref, own_ref, ids_ref, rank_ref, place_ref, rows_ref, cols_ref, first_ref, over_ref, *scratch
 ):
-    me = me_ref[0]
     owners = all_ref.shape[0]
     owned = CLUSTERS // owners
     heads = ids_ref.shape[0]
@@ -201,6 +187,42 @@
         found = dot(table, member).astype(I32)
         place_ref[h : h + 1, :] = found[0:1] * room + found[1:2] + rank_ref[h : h + 1, :]
 
+    rows_ref[...] = jnp.concatenate(at_rows + level_rows + [jnp.zeros((4, CLUSTERS), I32)], axis=0)
+    column = iota((CLUSTERS, LANES), 1)
+    found = jnp.zeros((CLUSTERS, LANES), I32)
+    for i, values in enumerate(at_cols + level_cols):
+        found = jnp.where(column == i, values, found)
+    cols_ref[...] = found
+    set_scr = scratch[heads]
+    set_scr[...] = flags(at_cols[0] == column)
+    first_ref[...] = dot(owns[0], set_scr[...])
+
+
+def arrive_kernel(
+    room,
+    me_ref,
+    all_ref,
+    own_ref,
+    rows_ref,
+    cols_ref,
+    sums_row_ref,
+    sums_col_ref,
+    query_ref,
+    key_ref,
+    member_ref,
+):
+    me = me_ref[0]
+    owners = all_ref.shape[0]
+    owned = CLUSTERS // owners
+    heads = own_ref.shape[0]
+    cluster_row = iota((1, CLUSTERS), 1).astype(F32)
+    counts = [all_ref[:, h * CLUSTERS : (h + 1) * CLUSTERS] for h in range(heads)]
+    owns = [jnp.broadcast_to(own_ref[h : h + 1, :], (8, CLUSTERS)).astype(BF16) for h in range(heads)]
+    at_rows = [rows_ref[h : h + 1, :] for h in range(heads)]
+    level_rows = [rows_ref[heads + h : heads + h + 1, :] for h in range(heads)]
+    at_cols = [cols_ref[:, h : h + 1] for h in range(heads)]
+    level_cols = [cols_ref[:, heads + h : heads + h + 1] for h in range(heads)]
+
     items = heads * owned
     lane = iota((CLUSTERS, LANES), 1)
     item = iota((items, CLUSTERS), 0)
@@ -215,8 +237,12 @@
         id_row += jnp.sum(jnp.where(hit, iota(lane.shape, 0).astype(F32), 0.0), axis=0, keepdims=True)
         hit = (at_rows[h] == me) & (level_rows[h] + h * owned == item)
         id_col += jnp.sum(jnp.where(hit, cluster_row, 0.0), axis=1, keepdims=True)
-    ends_ref[...] = ends
-    ends_t_ref[...] = ends_t
+    rows = key_ref.shape[0]
+    inside = ids_down(room, rows, items, ends)
+    query_ref[...] = jnp.where(inside, 0.0, -FAR).astype(BF16)
+    key_ref[...] = flags(inside)
+    id_along = ids_along(room, rows, ends_t)
+    member_ref[...] = flags(iota((items, rows), 0).astype(F32) == id_along)
 
     back_row = id_row.astype(I32) // owned
     back_col = id_col.astype(I32) // owned
@@ -248,8 +274,6 @@
             jnp.where(hit, (level_rows[h] + h * owned).astype(F32), 0.0), axis=1, keepdims=True
         )
         sent += dot(owns[h], flags(at_cols[h] == lane))
-        if h == 0:
-            first_ref[...] = sent
     small = iota((items, LANES), 1)
     ahead = (at_lane == at_item) & (turn_lane < turn_item) & (small < items)
     queue = jnp.sum(jnp.where(ahead, 1.0, 0.0), axis=1, keepdims=True)
@@ -261,21 +285,15 @@
     )
 
 
-def make_plan(me, everyone, own, cluster_ids, rank, room):
+def make_plan(everyone, own, cluster_ids, rank, room):
     heads, toks = cluster_ids.shape
     owners = everyone.shape[0]
-    items = heads * CLUSTERS // owners
-    vmem = pl.BlockSpec(memory_space=pltpu.VMEM)
     return pl.pallas_call(
         functools.partial(plan_kernel, room),
-        in_specs=[pl.BlockSpec(memory_space=pltpu.SMEM), vmem, vmem, vmem, vmem],
-        out_specs=[vmem] * 7,
         out_shape=(
             jax.ShapeDtypeStruct((heads, toks), I32),
-            jax.ShapeDtypeStruct((owners, LANES), F32),
-            jax.ShapeDtypeStruct((items, owners), F32),
-            jax.ShapeDtypeStruct((8, LANES), I32),
-            jax.ShapeDtypeStruct((items, LANES), I32),
+            jax.ShapeDtypeStruct((8, CLUSTERS), I32),
+            jax.ShapeDtypeStruct((CLUSTERS, LANES), I32),
             jax.ShapeDtypeStruct((8, LANES), F32),
             jax.ShapeDtypeStruct((8, LANES), F32),
         ),
@@ -294,7 +312,27 @@
         ],
         compiler_params=PARAMS,
         cost_estimate=pl.CostEstimate(flops=10**9, bytes_accessed=10**6, transcendentals=0),
-    )(me, everyone, own, cluster_ids, rank)
+    )(everyone, own, cluster_ids, rank)
+
+
+def arrive(me, everyone, own, rows, cols, room):
+    owners = everyone.shape[0]
+    items = own.shape[0] * CLUSTERS // owners
+    vmem = pl.BlockSpec(memory_space=pltpu.VMEM)
+    return pl.pallas_call(
+        functools.partial(arrive_kernel, room),
+        in_specs=[pl.BlockSpec(memory_space=pltpu.SMEM)] + [vmem] * 4,
+        out_specs=[vmem] * 5,
+        out_shape=(
+            jax.ShapeDtypeStruct((8, LANES), I32),
+            jax.ShapeDtypeStruct((items, LANES), I32),
+            jax.ShapeDtypeStruct((owners * room, LANES), BF16),
+            jax.ShapeDtypeStruct((owners * room, LANES), BF16),
+            jax.ShapeDtypeStruct((items, owners * room), BF16),
+        ),
+        compiler_params=PARAMS,
+        cost_estimate=pl.CostEstimate(flops=10**9, bytes_accessed=10**6, transcendentals=0),
+    )(me, everyone, own, rows, cols)
 
 
 def pack_kernel(room, place_ref, first_ref, q_ref, k_ref, v_ref, out_ref):
@@ -340,64 +378,42 @@
     )(place, first, queries, keys, values)
 
 
-def ids_along(room, rows, ends_t_ref):
-    items, sources = ends_t_ref.shape
+def ids_along(room, rows, ends_t):
+    items, sources = ends_t.shape
     spread = flags((iota((sources, rows), 1) >> shift_of(room)) == iota((sources, rows), 0))
-    ends_row = dot(ends_t_ref[...].astype(BF16), spread)
+    ends_row = dot(ends_t.astype(BF16), spread)
     slot_row = (iota((items, rows), 1) & (room - 1)).astype(F32)
     return jnp.sum(jnp.where(ends_row <= slot_row, 1.0, 0.0), axis=0, keepdims=True)
 
 
-def ids_down(room, rows, items, ends_ref):
-    sources = ends_ref.shape[0]
+def ids_down(room, rows, items, ends):
+    sources = ends.shape[0]
     spread = flags((iota((rows, sources), 0) >> shift_of(room)) == iota((rows, sources), 1))
-    lane = iota(ends_ref.shape, 1)
-    ends = jnp.where(lane < items, ends_ref[...], float(2 * LANES))
+    lane = iota(ends.shape, 1)
+    ends = jnp.where(lane < items, ends, float(2 * LANES))
     starts = jnp.where(lane == 0, 0.0, pltpu.roll(ends, 1, 1))
     bounds = dot(spread, jnp.concatenate([starts, ends], axis=1).astype(BF16))
     slot = (iota((rows, LANES), 0) & (room - 1)).astype(F32)
     return (bounds[:, 0:LANES] <= slot) & (slot < bounds[:, LANES:])
 
 
-def unit_sums(key_rows, id_row, items):
+def unit_sums(key_rows, member):
     key_float = key_rows.astype(F32)
     unit = key_float * lax.rsqrt(jnp.sum(key_float * key_float, axis=1, keepdims=True) + 1e-06)
     high = unit.astype(BF16)
     low = (unit - high.astype(F32)).astype(BF16)
-    member = flags(iota((items, id_row.shape[1]), 0).astype(F32) == id_row)
     return (dot(member, high) + dot(member, low)).astype(BF16)
 
 
-def weigh(pieces, values, width):
-    scale = math.log2(math.e) / math.sqrt(width)
-    highest = jnp.max(pieces[0], axis=1, keepdims=True)
-    for scores in pieces[1:]:
-        highest = jnp.maximum(highest, jnp.max(scores, axis=1, keepdims=True))
-    total = jnp.zeros_like(highest)
-    result = jnp.zeros((highest.shape[0], width), F32)
-    for scores, value in zip(pieces, values):
-        raised = jnp.exp2((scores - highest) * scale)
-        total += jnp.sum(raised, axis=1, keepdims=True)
-        result += dot(raised.astype(BF16), value)
-    return result / total
-
-
-def homeward(begin, tile, sums_row_ref, sums):
-    pick = flags(iota((tile, LANES), 0) + begin == sums_row_ref[0:1, :])
-    return dot(pick[:, 0 : sums.shape[0]], sums)
-
-
-def fill(room, ends_ref, ends_t_ref, x_ref, query_scr, key_scr, value_scr):
+def fill(query_ref, key_ref, member_ref, x_ref, query_scr, key_scr, value_scr):
     rows, width = x_ref.shape[0], x_ref.shape[1] // 3
-    items = ends_t_ref.shape[0]
-    inside = ids_down(room, rows, items, ends_ref)
     query_scr[:, 0:width] = x_ref[:, 0:width]
-    query_scr[:, width:] = jnp.where(inside, 0.0, -FAR).astype(BF16)
+    query_scr[:, width:] = query_ref[...]
     key_scr[:, 0:width] = x_ref[:, width : 2 * width]
-    key_scr[:, width:] = flags(inside)
+    key_scr[:, width:] = key_ref[...]
     value_scr[:, 0:width] = x_ref[:, 2 * width : 3 * width]
     value_scr[:, width:] = jnp.ones((rows, LANES), BF16)
-    return unit_sums(x_ref[:, width : 2 * width], ids_along(room, rows, ends_t_ref), items)
+    return unit_sums(x_ref[:, width : 2 * width], member_ref[...])
 
 
 def weigh(pieces, values, width):
@@ -418,10 +434,10 @@
 
 
 def attend_kernel(
-    room, ends_ref, ends_t_ref, sums_row_ref, x_ref, out_ref, query_scr, key_scr, value_scr
+    query_ref, key_ref, member_ref, sums_row_ref, x_ref, out_ref, query_scr, key_scr, value_scr
 ):
     rows, width = out_ref.shape
-    sums = fill(room, ends_ref, ends_t_ref, x_ref, query_scr, key_scr, value_scr)
+    sums = fill(query_ref, key_ref, member_ref, x_ref, query_scr, key_scr, value_scr)
     for begin in range(0, rows, TILE):
         end = begin + TILE
         query = query_scr[begin:end, :]
@@ -438,9 +454,9 @@
 
 
 def attend_tile_kernel(
-    room,
-    ends_ref,
-    ends_t_ref,
+    query_ref,
+    key_ref,
+    member_ref,
     sums_row_ref,
     x_ref,
     out_ref,
@@ -454,7 +470,7 @@
 
     @pl.when(pl.program_id(0) == 0)
     def _():
-        sums_scr[...] = fill(room, ends_ref, ends_t_ref, x_ref, query_scr, key_scr, value_scr)
+        sums_scr[...] = fill(query_ref, key_ref, member_ref, x_ref, query_scr, key_scr, value_scr)
 
     begin = pl.multiple_of(pl.program_id(0) * tile, tile)
     scores = dot_t(query_scr[pl.ds(begin, tile), :], key_scr[...])
@@ -463,7 +479,7 @@
     out_ref[...] = (result + homeward(begin, tile, sums_row_ref, sums_scr[...])).astype(out_ref.dtype)
 
 
-def attend(ends, ends_t, sums_row, received, room):
+def attend(query_far, key_far, member, sums_row, received):
     rows, width = received.shape[0], received.shape[1] // 3
     shape = jax.ShapeDtypeStruct((rows, width), received.dtype)
     cost = pl.CostEstimate(
@@ -471,11 +487,11 @@
         bytes_accessed=rows * width * 8,
         transcendentals=rows * rows // 2,
     )
-    given = (ends, ends_t, sums_row, received)
+    given = (query_far, key_far, member, sums_row, received)
     filled = [pltpu.VMEM((rows, width + LANES), BF16)] * 3
     if rows <= 4096:
         return pl.pallas_call(
-            functools.partial(attend_kernel, room),
+            attend_kernel,
             out_shape=shape,
             scratch_shapes=filled,
             compiler_params=PARAMS,
@@ -483,12 +499,12 @@
         )(*given)
     tile = 128
     return pl.pallas_call(
-        functools.partial(attend_tile_kernel, room),
+        attend_tile_kernel,
         grid=(rows // tile,),
         in_specs=[pl.BlockSpec(x.shape, lambda i: (0, 0)) for x in given],
         out_specs=pl.BlockSpec((tile, width), lambda i: (i, 0)),
         out_shape=shape,
-        scratch_shapes=filled + [pltpu.VMEM((ends_t.shape[0], width), BF16)],
+        scratch_shapes=filled + [pltpu.VMEM((member.shape[0], width), BF16)],
         compiler_params=PARAMS,
         cost_estimate=cost,
     )(*given)
@@ -558,23 +574,53 @@
     heads = cluster_ids.shape[0]
     owners = everyone.shape[0]
     me = lax.axis_index("seq").astype(I32)[None]
-    place, ends, ends_t, sums_row, sums_col, first, over = make_plan(
-        me, everyone, own, cluster_ids, rank, room
-    )
-    sent = pack(place, first, queries, keys, values, room, owners)
-    received = exchange(sent, "seq")
-    back = exchange(attend(ends, ends_t, sums_row, received, room), "seq")
+    place, rows, cols, first, over = make_plan(everyone, own, cluster_ids, rank, room)
+    received = exchange(pack(place, first, queries, keys, values, room, owners), "seq")
+    sums_row, sums_col, query_far, key_far, member = arrive(me, everyone, own, rows, cols, room)
+    back = exchange(attend(query_far, key_far, member, sums_row, received), "seq")
     share, sums = unpack(place.T, sums_col, over, back, lax.axis_size("head"))
     parts = exchange(share, "head")
     owned = CLUSTERS // owners
-    return parts, jnp.concatenate([sums[h * owned : (h + 1) * owned] for h in range(heads)], axis=1)
+    sums = jnp.concatenate([sums[h * owned : (h + 1) * owned] for h in range(heads)], axis=1)
+    return parts, sums
+
+
+def project_kernel(parts_ref, weight_ref, out_ref, total_scr):
+    step, toks = pl.program_id(0), out_ref.shape[0]
+    part = dot(parts_ref[0, 0:toks, :], weight_ref[...])
+
+    @pl.when(step == 0)
+    def _():
+        total_scr[...] = part
+
+    @pl.when(step > 0)
+    def _():
+        total_scr[...] += part
+
+    @pl.when(step == pl.num_programs(0) - 1)
+    def _():
+        out_ref[...] = total_scr[...].astype(out_ref.dtype)
 
 
 def project(parts, weight):
-    toks = parts.shape[1] - 16
-    weight = weight.reshape(parts.shape[0], parts.shape[2], weight.shape[1])
-    total = jnp.einsum("gtd,gdn->tn", parts[:, :toks], weight, preferred_element_type=F32)
-    return total.astype(BF16)
+    groups, toks, width = parts.shape
+    toks -= 16
+    deep, wide = weight.shape
+    return pl.pallas_call(
+        project_kernel,
+        grid=(groups,),
+        in_specs=[
+            pl.BlockSpec((1,) + parts.shape[1:], lambda i: (i, 0, 0)),
+            pl.BlockSpec((width, wide), lambda i: (i, 0)),
+        ],
+        out_specs=pl.BlockSpec((toks, wide), lambda i: (0, 0)),
+        out_shape=jax.ShapeDtypeStruct((toks, wide), BF16),
+        scratch_shapes=[pltpu.VMEM((toks, wide), F32)],
+        compiler_params=pltpu.CompilerParams(vmem_limit_bytes=16 * 1024 * 1024),
+        cost_estimate=pl.CostEstimate(
+            flops=2 * toks * deep * wide, bytes_accessed=deep * wide * 2, transcendentals=0
+        ),
+    )(parts, weight)
 
 
 def body(queries, keys, values, cluster_ids, out_weight):

time: 884 us -> 215 us (0.24)
  blocking collectives: 359 us -> 0 us
  Pallas kernels: 281 us -> 26.7 us
  waiting for transfers between devices: 155 us -> 122 us
  starting transfers between devices: 61.8 us -> 45.1 us
    all_to_all x2 -> x0, blocking collectives: 359 us -> none  [exchange(): return lax.all_to_all(rows, axis, split_axis=0, concat_axis=0, tiled=True)]
    pallas_call x4, Pallas kernels: 250 us -> 19.4 us  [the longest x1 7.12 us: project(): pl.pallas_call(project_kernel, grid=(groups,), in_specs=[pl.BlockSpec((1,...]
    all_to_all x5 -> x4, waiting for transfers between devices: 154 us -> 122 us  [exchange(): return lax.all_to_all(rows, axis, split_axis=0, concat_axis=0, tiled=True)]
    all_to_all x5 -> x4, starting transfers between devices: 61.8 us -> 45.1 us  [exchange(): return lax.all_to_all(rows, axis, split_axis=0, concat_axis=0, tiled=True)]
    pallas_call x2 -> x1, Pallas kernels: 18.6 us -> 4.33 us  [pack(): pl.pallas_call(functools.partial(pack_kernel, room), grid=(rows_all // ti...]
    pallas_call x2 -> x1, Pallas kernels: 12.5 us -> 3.05 us  [unpack(): pl.pallas_call(unpack_kernel, grid=(steps,), in_specs=[pl.BlockSpec((toks...]
  transfers between devices with their start and end apart: 6 -> 5, of which waited for: 5 -> 4; matrix products, arithmetic and copies ran while one was open for 1% -> 2% of each run, Pallas kernels for 2% -> 9%
where the time goes in v5:
time: 215 us; the launch traced here: 214 us
  waiting for transfers between devices  122 us (57%)
  starting transfers between devices  45.1 us (21%)
  Pallas kernels  26.7 us (12%)
  between operations  14.9 us (7%)
  other arithmetic  3.59 us (2%)
    all_to_all x4, waiting for transfers between devices, exchange(): return lax.all_to_all(rows, axis, split_axis=0, concat_axis=0, tiled=True)  122 us
    all_to_all x4, starting transfers between devices, exchange(): return lax.all_to_all(rows, axis, split_axis=0, concat_axis=0, tiled=True)  45.1 us
    pallas_call x1, Pallas kernels, project(): pl.pallas_call(project_kernel, grid=(groups,), in_specs=[pl.BlockSpec((1,...  7.12 us
    pallas_call x1, Pallas kernels, attend(): pl.pallas_call(attend_kernel, out_shape=shape, scratch_shapes=filled, com...  6.22 us
    pallas_call x1, Pallas kernels, make_plan(): pl.pallas_call(functools.partial(plan_kernel, room), out_shape=(jax.Shape...  4.56 us
    pallas_call x1, Pallas kernels, pack(): pl.pallas_call(functools.partial(pack_kernel, room), grid=(rows_all // ti...  4.33 us
  transfers between devices with their start and end apart: 5, of which 4 were waited for; matrix products, arithmetic and copies ran while one was open for 2% of the time, Pallas kernels for 9%

profile of v5, /device:TPU:1, one launch (start us, length us, event | category | flops | bytes accessed | tf_op | source)
XLA Modules:
  0.0 214.3 jit_solution(13967292150584221666)
XLA Ops:
  7.2 0.0 copy-start.5
  7.2 0.0 all-gather.2.cloned.1.call-start
  7.2 0.7 all-gather.2.cloned.1.call-update
  7.9 1.1 convert_reduce_fusion.1.own_ref
  9.0 0.7 broadcast_in_dim.6
  9.7 19.3 %all-to-all-start.3 = ((bf16[64,8,128]{2,1,0:T(8,128)(2,1)}), bf16[64,8,128]{2,1,0:T(8,128)(2,1)S(1)}, u32[]{:S(2)}, u32[]{:S(2)}) async-start(bf16[64,8,128]{2,1,0:T(8,128)(2,1)} %broadcast_in_dim.6), calls=%async_computation.3 | async-start | bytes 262144 | tf_op jit(solution)/shard_map/all_to_all | solution.py:570
  29.0 0.2 iota_compare_fusion.1
  29.2 0.0 copy-start.7
  29.2 0.0 copy-start.9
  29.2 0.0 copy-start.11
  29.2 1.7 convert_reduce_fusion.rank_ref
  30.9 13.0 %all-to-all-done.3 = bf16[64,8,128]{2,1,0:T(8,128)(2,1)S(1)} async-done(((bf16[64,8,128]{2,1,0:T(8,128)(2,1)}), bf16[64,8,128]{2,1,0:T(8,128)(2,1)S(1)}, u32[]{:S(2)}, u32[]{:S(2)}) %all-to-all-start.3) | async-done | bytes 131104 | tf_op jit(solution)/shard_map/all_to_all | solution.py:570
  43.9 0.0 copy-done.5
  44.0 4.6 %shard_map.70 = (s32[2,768]{1,0:T(2,128)S(1)}, s32[8,512]{1,0:T(8,128)S(1)}, s32[512,128]{1,0:T(8,128)S(1)}, f32[8,128]{1,0:T(8,128)S(1)}, f32[8,128]{1,0:T(8,128)S(1)}) custom-call(bf16[64,1024]{1,0:T(8,128)(2,1)S(1)} %bitcast.24, f32[2,512]{1,0:T(2,128)S(1)} %convert_reduce_fusion.1.own_ref, s32[2,768]{1,0:T(2,128)S(1)} %copy-done.5, ...), custom_call_target="tpu_custom_call" | custom-call | flops 1000000000 | bytes 1000000 | tf_op jit(solution)/shard_map/pallas_call | solution.py:291
  48.5 0.0 copy-done.7
  48.5 0.0 copy-done.9
  48.5 0.0 copy-done.11
  48.5 4.3 %shard_map.72 = bf16[2048,384]{1,0:T(8,128)(2,1)} custom-call(s32[2,768]{1,0:T(2,128)S(1)} %get-tuple-element.59.place_ref, f32[8,128]{1,0:T(8,128)S(1)} %get-tuple-element.68.first_ref, bf16[768,256]{1,0:T(8,128)(2,1)S(1)} %copy-done.7, bf16[768,256]{1,0:T(8,128)(2,1)S(1)} %copy-done.9, bf16[768,256]{1,0:T(8,128)(2,1)S(1)} %copy-done.11), custom_call_target="tpu_custom_call" | custom-call | flops 2415919104 | bytes 1572864 | tf_op jit(solution)/shard_map/pallas_call | solution.py:360
  52.9 6.6 %all-to-all-start.4 = ((bf16[64,32,384]{2,1,0:T(8,128)(2,1)}), bf16[64,32,384]{2,1,0:T(8,128)(2,1)S(1)}, u32[]{:S(2)}, u32[]{:S(2)}) async-start(bf16[64,32,384]{2,1,0:T(8,128)(2,1)} %bitcast.8), calls=%async_computation.4 | async-start | bytes 3145728 | tf_op jit(solution)/shard_map/all_to_all | solution.py:570
  59.5 1.5 shard_map.71
  60.9 71.1 %all-to-all-done.4 = bf16[64,32,384]{2,1,0:T(8,128)(2,1)S(1)} async-done(((bf16[64,32,384]{2,1,0:T(8,128)(2,1)}), bf16[64,32,384]{2,1,0:T(8,128)(2,1)S(1)}, u32[]{:S(2)}, u32[]{:S(2)}) %all-to-all-start.4) | async-done | bytes 1572896 | tf_op jit(solution)/shard_map/all_to_all | solution.py:570
  132.0 6.2 %shard_map.73 = bf16[2048,128]{1,0:T(8,128)(2,1)} custom-call(bf16[2048,128]{1,0:T(8,128)(2,1)S(1)} %get-tuple-element.64.query_ref, bf16[2048,128]{1,0:T(8,128)(2,1)S(1)} %get-tuple-element.65.key_ref, bf16[16,2048]{1,0:T(8,128)(2,1)S(1)} %get-tuple-element.66.member_ref, s32[8,128]{1,0:T(8,128)S(1)} %get-tuple-element.67.sums_row_ref, ...), custom_call_target="tpu_custom_call" | custom-call | flops 1073741824 | bytes 2097152 | tf_op jit(solution)/shard_map/pallas_call | solution.py:493
  138.3 10.0 %all-to-all-start.5 = ((bf16[64,32,128]{2,1,0:T(8,128)(2,1)}), bf16[64,32,128]{2,1,0:T(8,128)(2,1)S(1)}, u32[]{:S(2)}, u32[]{:S(2)}) async-start(bf16[64,32,128]{2,1,0:T(8,128)(2,1)} %bitcast.10), calls=%async_computation.5 | async-start | bytes 1048576 | tf_op jit(solution)/shard_map/all_to_all | solution.py:570
  148.3 0.0 copy-start.8
  148.3 0.0 copy-start.10
  148.3 0.0 copy-start.12
  148.3 0.2 copy.12
  148.5 28.7 %all-to-all-done.5 = bf16[64,32,128]{2,1,0:T(8,128)(2,1)S(1)} async-done(((bf16[64,32,128]{2,1,0:T(8,128)(2,1)}), bf16[64,32,128]{2,1,0:T(8,128)(2,1)S(1)}, u32[]{:S(2)}, u32[]{:S(2)}) %all-to-all-start.5) | async-done | bytes 524320 | tf_op jit(solution)/shard_map/all_to_all | solution.py:570
  177.2 3.1 %shard_map.74 = (bf16[8,112,256]{2,1,0:T(8,128)(2,1)}, f32[16,128]{1,0:T(8,128)S(1)}) custom-call(s32[768,2]{1,0:T(8,128)S(1)} %bitcast.21, s32[16,128]{1,0:T(8,128)S(1)} %get-tuple-element.62.sums_col_ref, f32[8,128]{1,0:T(8,128)S(1)} %get-tuple-element.63.over_ref, bf16[2048,128]{1,0:T(8,128)(2,1)S(1)} %bitcast.20), custom_call_target="tpu_custom_call" | custom-call | flops 805306368 | bytes 524288 | tf_op jit(solution)/shard_map/pallas_call | solution.py:543
  180.2 9.2 %all-to-all-start.6 = ((bf16[8,112,256]{2,1,0:T(8,128)(2,1)}), bf16[8,112,256]{2,1,0:T(8,128)(2,1)S(1)}, u32[]{:S(2)}, u32[]{:S(2)}) async-start(bf16[8,112,256]{2,1,0:T(8,128)(2,1)} %get-tuple-element.69), calls=%async_computation.6 | async-start | bytes 917504 | tf_op jit(solution)/shard_map/all_to_all | solution.py:570
  189.5 8.8 %all-to-all-done.6 = bf16[8,112,256]{2,1,0:T(8,128)(2,1)S(1)} async-done(((bf16[8,112,256]{2,1,0:T(8,128)(2,1)}), bf16[8,112,256]{2,1,0:T(8,128)(2,1)S(1)}, u32[]{:S(2)}, u32[]{:S(2)}) %all-to-all-start.6) | async-done | bytes 458784 | tf_op jit(solution)/shard_map/all_to_all | solution.py:570
  198.2 0.6 slice_reduce_fusion
  199.5 0.0 all-gather.2.cloned.1.call-done
  199.5 0.0 copy-done.8
  199.5 0.0 copy-done.10
  199.6 0.0 copy-done.12
  199.6 7.1 %conditional.1 = (f32[8,256]{1,0:T(8,128)S(1)}, bf16[96,2048]{1,0:T(8,128)(2,1)S(1)}) conditional(s32[]{:T(128)} %convert_element_type.24, (bf16[8,112,256]{2,1,0:T(8,128)(2,1)S(1)}, bf16[2048,2048]{1,0:T(8,128)(2,1)}, f32[8,256]{1,0:T(8,128)S(1)}) %tuple.15, (bf16[64,1024]{1,0:T(8,128)(2,1)S(1)}, f32[2,512]{1,0:T(2,128)S(1)}, ...), branch_computations={%region_3.0_spmd, %region_4.0_spmd} | conditional | flops 32870078464 | bytes 104084856 | solution.py:649
  199.6 7.1 %branch_0_fun.1 = bf16[96,2048]{1,0:T(8,128)(2,1)S(1)} custom-call(bf16[8,112,256]{2,1,0:T(8,128)(2,1)S(1)} %get-tuple-element.22.parts_ref, bf16[2048,2048]{1,0:T(8,128)(2,1)} %get-tuple-element.23.weight_ref), custom_call_target="tpu_custom_call" | custom-call | flops 805306368 | bytes 8388608 | tf_op jit(solution)/shard_map/cond/branch_0_fun/pallas_call | solution.py:609
  206.7 0.0 copy-start.4
  206.7 0.0 copy-start.6
  206.7 0.7 copy-done.4
  207.5 0.0 copy-done.6
  (5 shorter events, 0.0 us)
Async XLA Ops:
  7.2 36.8 %copy-start.5 = (s32[2,768]{1,0:T(2,128)S(1)}, s32[2,768]{1,0:T(2,128)}, u32[]{:S(2)}) copy-start(s32[2,768]{1,0:T(2,128)} %ids_ref.1) | copy-start | bytes 18436
  7.2 192.4 %all-gather.2.cloned.1.call-start = ((), (), s32[]{:S(2)}) async-start(), calls=%async_computation.7 | async-start | bytes 9437184 | tf_op jit(solution)/shard_map/all_gather | solution.py:633
  9.7 34.2 %all-to-all-start.3 = ((bf16[64,8,128]{2,1,0:T(8,128)(2,1)}), bf16[64,8,128]{2,1,0:T(8,128)(2,1)S(1)}, u32[]{:S(2)}, u32[]{:S(2)}) async-start(bf16[64,8,128]{2,1,0:T(8,128)(2,1)} %broadcast_in_dim.6), calls=%async_computation.3 | async-start | bytes 262144 | tf_op jit(solution)/shard_map/all_to_all | solution.py:570
  29.2 19.3 %copy-start.7 = (bf16[768,256]{1,0:T(8,128)(2,1)S(1)}, bf16[768,256]{1,0:T(8,128)(2,1)}, u32[]{:S(2)}) copy-start(bf16[768,256]{1,0:T(8,128)(2,1)} %q_ref.1) | copy-start | bytes 1179652
  29.2 19.3 %copy-start.9 = (bf16[768,256]{1,0:T(8,128)(2,1)S(1)}, bf16[768,256]{1,0:T(8,128)(2,1)}, u32[]{:S(2)}) copy-start(bf16[768,256]{1,0:T(8,128)(2,1)} %k_ref.1) | copy-start | bytes 1179652
  29.2 19.3 %copy-start.11 = (bf16[768,256]{1,0:T(8,128)(2,1)S(1)}, bf16[768,256]{1,0:T(8,128)(2,1)}, u32[]{:S(2)}) copy-start(bf16[768,256]{1,0:T(8,128)(2,1)} %v_ref.1) | copy-start | bytes 1179652
  52.9 79.2 %all-to-all-start.4 = ((bf16[64,32,384]{2,1,0:T(8,128)(2,1)}), bf16[64,32,384]{2,1,0:T(8,128)(2,1)S(1)}, u32[]{:S(2)}, u32[]{:S(2)}) async-start(bf16[64,32,384]{2,1,0:T(8,128)(2,1)} %bitcast.8), calls=%async_computation.4 | async-start | bytes 3145728 | tf_op jit(solution)/shard_map/all_to_all | solution.py:570
  138.3 38.9 %all-to-all-start.5 = ((bf16[64,32,128]{2,1,0:T(8,128)(2,1)}), bf16[64,32,128]{2,1,0:T(8,128)(2,1)S(1)}, u32[]{:S(2)}, u32[]{:S(2)}) async-start(bf16[64,32,128]{2,1,0:T(8,128)(2,1)} %bitcast.10), calls=%async_computation.5 | async-start | bytes 1048576 | tf_op jit(solution)/shard_map/all_to_all | solution.py:570
  148.3 51.3 %copy-start.8 = (bf16[768,256]{1,0:T(8,128)(2,1)S(1)}, bf16[768,256]{1,0:T(8,128)(2,1)}, u32[]{:S(2)}) copy-start(bf16[768,256]{1,0:T(8,128)(2,1)} %q_ref.1) | copy-start | bytes 1179652
  148.3 51.3 %copy-start.10 = (bf16[768,256]{1,0:T(8,128)(2,1)S(1)}, bf16[768,256]{1,0:T(8,128)(2,1)}, u32[]{:S(2)}) copy-start(bf16[768,256]{1,0:T(8,128)(2,1)} %k_ref.1) | copy-start | bytes 1179652
  148.3 51.3 %copy-start.12 = (bf16[768,256]{1,0:T(8,128)(2,1)S(1)}, bf16[768,256]{1,0:T(8,128)(2,1)}, u32[]{:S(2)}) copy-start(bf16[768,256]{1,0:T(8,128)(2,1)} %v_ref.1) | copy-start | bytes 1179652
  180.2 18.0 %all-to-all-start.6 = ((bf16[8,112,256]{2,1,0:T(8,128)(2,1)}), bf16[8,112,256]{2,1,0:T(8,128)(2,1)S(1)}, u32[]{:S(2)}, u32[]{:S(2)}) async-start(bf16[8,112,256]{2,1,0:T(8,128)(2,1)} %get-tuple-element.69), calls=%async_computation.6 | async-start | bytes 917504 | tf_op jit(solution)/shard_map/all_to_all | solution.py:570
  206.7 0.7 copy-start.4
  206.7 0.7 copy-start.6
Sparse Core Ops, SparseCore 0:
  10.2 63.0 all-gather.1

commit v6 on v5

--- a/solution.py
+++ b/solution.py
@@ -585,42 +585,11 @@
     return parts, sums
 
 
-def project_kernel(parts_ref, weight_ref, out_ref, total_scr):
-    step, toks = pl.program_id(0), out_ref.shape[0]
-    part = dot(parts_ref[0, 0:toks, :], weight_ref[...])
-
-    @pl.when(step == 0)
-    def _():
-        total_scr[...] = part
-
-    @pl.when(step > 0)
-    def _():
-        total_scr[...] += part
-
-    @pl.when(step == pl.num_programs(0) - 1)
-    def _():
-        out_ref[...] = total_scr[...].astype(out_ref.dtype)
-
-
 def project(parts, weight):
-    groups, toks, width = parts.shape
-    toks -= 16
-    deep, wide = weight.shape
-    return pl.pallas_call(
-        project_kernel,
-        grid=(groups,),
-        in_specs=[
-            pl.BlockSpec((1,) + parts.shape[1:], lambda i: (i, 0, 0)),
-            pl.BlockSpec((width, wide), lambda i: (i, 0)),
-        ],
-        out_specs=pl.BlockSpec((toks, wide), lambda i: (0, 0)),
-        out_shape=jax.ShapeDtypeStruct((toks, wide), BF16),
-        scratch_shapes=[pltpu.VMEM((toks, wide), F32)],
-        compiler_params=pltpu.CompilerParams(vmem_limit_bytes=16 * 1024 * 1024),
-        cost_estimate=pl.CostEstimate(
-            flops=2 * toks * deep * wide, bytes_accessed=deep * wide * 2, transcendentals=0
-        ),
-    )(parts, weight)
+    toks = parts.shape[1] - 16
+    weight = weight.reshape(parts.shape[0], parts.shape[2], weight.shape[1])
+    total = jnp.einsum("gtd,gdn->tn", parts[:, :toks], weight, preferred_element_type=F32)
+    return total.astype(BF16)
 
 
 def body(queries, keys, values, cluster_ids, out_weight):

time: 215 us -> 213 us (level)
  Pallas kernels: 26.7 us -> 19.9 us
  matrix products: 0 us -> 4.87 us
    pallas_call x1 -> x0, Pallas kernels: 7.12 us -> none  [project(): pl.pallas_call(project_kernel, grid=(groups,), in_specs=[pl.BlockSpec((1,...]
    dot_general x0 -> x1, matrix products: none -> 4.87 us  [project(): jnp.einsum('gtd,gdn->tn', parts[:, :toks], weight, preferred_element_type...]
where the time goes in v6:
time: 213 us; the launch traced here: 212 us
  waiting for transfers between devices  122 us (57%)
  starting transfers between devices  45.1 us (21%)
  Pallas kernels  19.9 us (9%)
  between operations  14.9 us (7%)
  matrix products  4.87 us (2%)
  other arithmetic  3.57 us (2%)
    all_to_all x4, waiting for transfers between devices, exchange(): return lax.all_to_all(rows, axis, split_axis=0, concat_axis=0, tiled=True)  122 us
    all_to_all x4, starting transfers between devices, exchange(): return lax.all_to_all(rows, axis, split_axis=0, concat_axis=0, tiled=True)  45.1 us
    pallas_call x1, Pallas kernels, attend(): pl.pallas_call(attend_kernel, out_shape=shape, scratch_shapes=filled, com...  6.22 us
    dot_general x1, matrix products, project(): jnp.einsum('gtd,gdn->tn', parts[:, :toks], weight, preferred_element_type...  4.87 us
    pallas_call x1, Pallas kernels, make_plan(): pl.pallas_call(functools.partial(plan_kernel, room), out_shape=(jax.Shape...  4.79 us
    pallas_call x1, Pallas kernels, pack(): pl.pallas_call(functools.partial(pack_kernel, room), grid=(rows_all // ti...  4.33 us
  transfers between devices with their start and end apart: 5, of which 4 were waited for; matrix products, arithmetic and copies ran while one was open for 2% of the time, Pallas kernels for 9%

profile of v6, /device:TPU:1, one launch (start us, length us, event | category | flops | bytes accessed | tf_op | source)
XLA Modules:
  0.0 212.3 jit_solution(15889858846497357703)
XLA Ops:
  7.2 0.0 copy-start.7
  7.2 0.0 copy-start.9
  7.2 0.0 copy-start.11
  7.2 0.0 all-gather.2.cloned.1.call-start
  7.2 0.7 all-gather.2.cloned.1.call-update
  7.9 1.1 convert_reduce_fusion.1.own_ref
  9.1 0.7 broadcast_in_dim.6
  9.8 19.3 %all-to-all-start.3 = ((bf16[64,8,128]{2,1,0:T(8,128)(2,1)}), bf16[64,8,128]{2,1,0:T(8,128)(2,1)S(1)}, u32[]{:S(2)}, u32[]{:S(2)}) async-start(bf16[64,8,128]{2,1,0:T(8,128)(2,1)} %broadcast_in_dim.6), calls=%async_computation.3 | async-start | bytes 262144 | tf_op jit(solution)/shard_map/all_to_all | solution.py:570
  29.0 0.2 iota_compare_fusion.1
  29.2 1.6 convert_reduce_fusion.rank_ref
  30.9 13.1 %all-to-all-done.3 = bf16[64,8,128]{2,1,0:T(8,128)(2,1)S(1)} async-done(((bf16[64,8,128]{2,1,0:T(8,128)(2,1)}), bf16[64,8,128]{2,1,0:T(8,128)(2,1)S(1)}, u32[]{:S(2)}, u32[]{:S(2)}) %all-to-all-start.3) | async-done | bytes 131104 | tf_op jit(solution)/shard_map/all_to_all | solution.py:570
  44.0 4.8 %shard_map.68 = (s32[2,768]{1,0:T(2,128)S(1)}, s32[8,512]{1,0:T(8,128)S(1)}, s32[512,128]{1,0:T(8,128)S(1)}, f32[8,128]{1,0:T(8,128)S(1)}, f32[8,128]{1,0:T(8,128)S(1)}) custom-call(bf16[64,1024]{1,0:T(8,128)(2,1)S(1)} %bitcast.38, f32[2,512]{1,0:T(2,128)S(1)} %convert_reduce_fusion.1.own_ref, s32[2,768]{1,0:T(2,128)} %ids_ref.1, ...), custom_call_target="tpu_custom_call" | custom-call | flops 1000000000 | bytes 1000000 | tf_op jit(solution)/shard_map/pallas_call | solution.py:291
  48.8 0.0 copy-done.7
  48.8 0.0 copy-done.9
  48.8 0.0 copy-done.11
  48.8 4.3 %shard_map.70 = bf16[2048,384]{1,0:T(8,128)(2,1)} custom-call(s32[2,768]{1,0:T(2,128)S(1)} %get-tuple-element.64.place_ref, f32[8,128]{1,0:T(8,128)S(1)} %get-tuple-element.73.first_ref, bf16[768,256]{1,0:T(8,128)(2,1)S(1)} %copy-done.7, bf16[768,256]{1,0:T(8,128)(2,1)S(1)} %copy-done.9, bf16[768,256]{1,0:T(8,128)(2,1)S(1)} %copy-done.11), custom_call_target="tpu_custom_call" | custom-call | flops 2415919104 | bytes 1572864 | tf_op jit(solution)/shard_map/pallas_call | solution.py:360
  53.1 6.6 %all-to-all-start.4 = ((bf16[64,32,384]{2,1,0:T(8,128)(2,1)}), bf16[64,32,384]{2,1,0:T(8,128)(2,1)S(1)}, u32[]{:S(2)}, u32[]{:S(2)}) async-start(bf16[64,32,384]{2,1,0:T(8,128)(2,1)} %bitcast.12), calls=%async_computation.4 | async-start | bytes 3145728 | tf_op jit(solution)/shard_map/all_to_all | solution.py:570
  59.7 1.5 shard_map.69
  61.2 71.0 %all-to-all-done.4 = bf16[64,32,384]{2,1,0:T(8,128)(2,1)S(1)} async-done(((bf16[64,32,384]{2,1,0:T(8,128)(2,1)}), bf16[64,32,384]{2,1,0:T(8,128)(2,1)S(1)}, u32[]{:S(2)}, u32[]{:S(2)}) %all-to-all-start.4) | async-done | bytes 1572896 | tf_op jit(solution)/shard_map/all_to_all | solution.py:570
  132.1 6.2 %shard_map.71 = bf16[2048,128]{1,0:T(8,128)(2,1)} custom-call(bf16[2048,128]{1,0:T(8,128)(2,1)S(1)} %get-tuple-element.69.query_ref, bf16[2048,128]{1,0:T(8,128)(2,1)S(1)} %get-tuple-element.70.key_ref, bf16[16,2048]{1,0:T(8,128)(2,1)S(1)} %get-tuple-element.71.member_ref, s32[8,128]{1,0:T(8,128)S(1)} %get-tuple-element.72.sums_row_ref, ...), custom_call_target="tpu_custom_call" | custom-call | flops 1073741824 | bytes 2097152 | tf_op jit(solution)/shard_map/pallas_call | solution.py:493
  138.4 0.0 copy-start.5
  138.4 0.0 copy-start.8
  138.4 0.0 copy-start.10
  138.4 0.0 copy-start.12
  138.4 10.0 %all-to-all-start.5 = ((bf16[64,32,128]{2,1,0:T(8,128)(2,1)}), bf16[64,32,128]{2,1,0:T(8,128)(2,1)S(1)}, u32[]{:S(2)}, u32[]{:S(2)}) async-start(bf16[64,32,128]{2,1,0:T(8,128)(2,1)} %bitcast.14), calls=%async_computation.5 | async-start | bytes 1048576 | tf_op jit(solution)/shard_map/all_to_all | solution.py:570
  148.4 0.2 copy.10
  148.6 28.8 %all-to-all-done.5 = bf16[64,32,128]{2,1,0:T(8,128)(2,1)S(1)} async-done(((bf16[64,32,128]{2,1,0:T(8,128)(2,1)}), bf16[64,32,128]{2,1,0:T(8,128)(2,1)S(1)}, u32[]{:S(2)}, u32[]{:S(2)}) %all-to-all-start.5) | async-done | bytes 524320 | tf_op jit(solution)/shard_map/all_to_all | solution.py:570
  177.4 3.1 %shard_map.72 = (bf16[8,112,256]{2,1,0:T(8,128)(2,1)}, f32[16,128]{1,0:T(8,128)S(1)}) custom-call(s32[768,2]{1,0:T(8,128)S(1)} %bitcast.33, s32[16,128]{1,0:T(8,128)S(1)} %get-tuple-element.67.sums_col_ref, f32[8,128]{1,0:T(8,128)S(1)} %get-tuple-element.68.over_ref, bf16[2048,128]{1,0:T(8,128)(2,1)S(1)} %bitcast.32), custom_call_target="tpu_custom_call" | custom-call | flops 805306368 | bytes 524288 | tf_op jit(solution)/shard_map/pallas_call | solution.py:543
  180.5 9.2 %all-to-all-start.6 = ((bf16[8,112,256]{2,1,0:T(8,128)(2,1)}), bf16[8,112,256]{2,1,0:T(8,128)(2,1)S(1)}, u32[]{:S(2)}, u32[]{:S(2)}) async-start(bf16[8,112,256]{2,1,0:T(8,128)(2,1)} %get-tuple-element.74), calls=%async_computation.6 | async-start | bytes 917504 | tf_op jit(solution)/shard_map/all_to_all | solution.py:570
  189.7 8.8 %all-to-all-done.6 = bf16[8,112,256]{2,1,0:T(8,128)(2,1)S(1)} async-done(((bf16[8,112,256]{2,1,0:T(8,128)(2,1)}), bf16[8,112,256]{2,1,0:T(8,128)(2,1)S(1)}, u32[]{:S(2)}, u32[]{:S(2)}) %all-to-all-start.6) | async-done | bytes 458784 | tf_op jit(solution)/shard_map/all_to_all | solution.py:570
  198.4 0.6 slice_reduce_fusion
  199.7 0.0 all-gather.2.cloned.1.call-done
  199.7 0.0 copy-done.5
  199.7 0.0 copy-done.8
  199.7 0.0 copy-done.10
  199.8 0.0 copy-done.12
  199.8 4.9 %conditional.2 = (f32[8,256]{1,0:T(8,128)S(1)}, bf16[96,2048]{1,0:T(8,128)(2,1)S(1)}) conditional(s32[]{:T(128)} %convert_element_type.29, (bf16[8,112,256]{2,1,0:T(8,128)(2,1)S(1)}, bf16[2048,2048]{1,0:T(8,128)(2,1)}, f32[8,256]{1,0:T(8,128)S(1)}) %tuple.19, (bf16[64,1024]{1,0:T(8,128)(2,1)S(1)}, f32[2,512]{1,0:T(2,128)S(1)}, ...), branch_computations={%region_3.0_spmd, %region_4.0_spmd} | conditional | flops 32870275072 | bytes 104871288
  199.8 4.9 %fusion = bf16[96,2048]{1,0:T(8,128)(2,1)S(1)} fusion(bf16[8,256,2048]{2,1,0:T(8,128)(2,1)} %bitcast.35, bf16[8,112,256]{2,1,0:T(8,128)(2,1)S(1)} %get-tuple-element.25), kind=kOutput, calls=%fused_computation.1 | convolution fusion | flops 805502976 | bytes 9175040 | tf_op jit(solution)/shard_map/cond/branch_0_fun/gtd,gdn->tn/dot_general | solution.py:591
  204.7 0.0 copy-start.4
  204.7 0.0 copy-start.6
  204.7 0.7 copy-done.4
  205.4 0.0 copy-done.6
  (5 shorter events, 0.0 us)
Async XLA Ops:
  7.2 41.6 %copy-start.7 = (bf16[768,256]{1,0:T(8,128)(2,1)S(1)}, bf16[768,256]{1,0:T(8,128)(2,1)}, u32[]{:S(2)}) copy-start(bf16[768,256]{1,0:T(8,128)(2,1)} %q_ref.1) | copy-start | bytes 1179652
  7.2 41.6 %copy-start.9 = (bf16[768,256]{1,0:T(8,128)(2,1)S(1)}, bf16[768,256]{1,0:T(8,128)(2,1)}, u32[]{:S(2)}) copy-start(bf16[768,256]{1,0:T(8,128)(2,1)} %k_ref.1) | copy-start | bytes 1179652
  7.2 41.6 %copy-start.11 = (bf16[768,256]{1,0:T(8,128)(2,1)S(1)}, bf16[768,256]{1,0:T(8,128)(2,1)}, u32[]{:S(2)}) copy-start(bf16[768,256]{1,0:T(8,128)(2,1)} %v_ref.1) | copy-start | bytes 1179652
  7.2 192.5 %all-gather.2.cloned.1.call-start = ((), (), s32[]{:S(2)}) async-start(), calls=%async_computation.7 | async-start | bytes 9437184 | tf_op jit(solution)/shard_map/all_gather | solution.py:602
  9.8 34.2 %all-to-all-start.3 = ((bf16[64,8,128]{2,1,0:T(8,128)(2,1)}), bf16[64,8,128]{2,1,0:T(8,128)(2,1)S(1)}, u32[]{:S(2)}, u32[]{:S(2)}) async-start(bf16[64,8,128]{2,1,0:T(8,128)(2,1)} %broadcast_in_dim.6), calls=%async_computation.3 | async-start | bytes 262144 | tf_op jit(solution)/shard_map/all_to_all | solution.py:570
  53.1 79.0 %all-to-all-start.4 = ((bf16[64,32,384]{2,1,0:T(8,128)(2,1)}), bf16[64,32,384]{2,1,0:T(8,128)(2,1)S(1)}, u32[]{:S(2)}, u32[]{:S(2)}) async-start(bf16[64,32,384]{2,1,0:T(8,128)(2,1)} %bitcast.12), calls=%async_computation.4 | async-start | bytes 3145728 | tf_op jit(solution)/shard_map/all_to_all | solution.py:570
  138.4 61.4 %copy-start.5 = (s32[2,768]{1,0:T(2,128)S(1)}, s32[2,768]{1,0:T(2,128)}, u32[]{:S(2)}) copy-start(s32[2,768]{1,0:T(2,128)} %ids_ref.1) | copy-start | bytes 18436
  138.4 61.4 %copy-start.8 = (bf16[768,256]{1,0:T(8,128)(2,1)S(1)}, bf16[768,256]{1,0:T(8,128)(2,1)}, u32[]{:S(2)}) copy-start(bf16[768,256]{1,0:T(8,128)(2,1)} %q_ref.1) | copy-start | bytes 1179652
  138.4 61.4 %copy-start.10 = (bf16[768,256]{1,0:T(8,128)(2,1)S(1)}, bf16[768,256]{1,0:T(8,128)(2,1)}, u32[]{:S(2)}) copy-start(bf16[768,256]{1,0:T(8,128)(2,1)} %k_ref.1) | copy-start | bytes 1179652
  138.4 61.4 %copy-start.12 = (bf16[768,256]{1,0:T(8,128)(2,1)S(1)}, bf16[768,256]{1,0:T(8,128)(2,1)}, u32[]{:S(2)}) copy-start(bf16[768,256]{1,0:T(8,128)(2,1)} %v_ref.1) | copy-start | bytes 1179652
  138.4 39.0 %all-to-all-start.5 = ((bf16[64,32,128]{2,1,0:T(8,128)(2,1)}), bf16[64,32,128]{2,1,0:T(8,128)(2,1)S(1)}, u32[]{:S(2)}, u32[]{:S(2)}) async-start(bf16[64,32,128]{2,1,0:T(8,128)(2,1)} %bitcast.14), calls=%async_computation.5 | async-start | bytes 1048576 | tf_op jit(solution)/shard_map/all_to_all | solution.py:570
  180.5 18.0 %all-to-all-start.6 = ((bf16[8,112,256]{2,1,0:T(8,128)(2,1)}), bf16[8,112,256]{2,1,0:T(8,128)(2,1)S(1)}, u32[]{:S(2)}, u32[]{:S(2)}) async-start(bf16[8,112,256]{2,1,0:T(8,128)(2,1)} %get-tuple-element.74), calls=%async_computation.6 | async-start | bytes 917504 | tf_op jit(solution)/shard_map/all_to_all | solution.py:570
  204.7 0.7 copy-start.4
  204.7 0.7 copy-start.6
Sparse Core Ops, SparseCore 0:
  10.2 63.0 all-gather.1

commit v7 on v6

--- a/solution.py
+++ b/solution.py
@@ -335,16 +335,20 @@
     )(me, everyone, own, rows, cols)
 
 
+def of_first(room, rows, base, first_ref):
+    place = iota((rows, LANES), 0) + base
+    here = (place >> shift_of(room)) == iota((rows, LANES), 1)
+    first = jnp.sum(jnp.where(here, first_ref[0:1, :], 0.0), axis=1, keepdims=True)
+    return (place[:, 0:1] & (room - 1)).astype(F32) < first
+
+
 def pack_kernel(room, place_ref, first_ref, q_ref, k_ref, v_ref, out_ref):
     rows, toks = out_ref.shape[0], q_ref.shape[0]
     width = out_ref.shape[1] // 3
     base = pl.program_id(0) * rows
     wanted = iota((rows, toks), 0) + base
     pick = flags((wanted == place_ref[0:1, :]) | (wanted == place_ref[1:2, :]))
-    place = iota((rows, LANES), 0) + base
-    here = (place >> shift_of(room)) == iota((rows, LANES), 1)
-    first = jnp.sum(jnp.where(here, first_ref[0:1, :], 0.0), axis=1, keepdims=True)
-    is_first = (place[:, 0:1] & (room - 1)).astype(F32) < first
+    is_first = of_first(room, rows, base, first_ref)
     for part, ref in enumerate((q_ref, k_ref, v_ref)):
         moved = dot(pick, ref[...])
         moved = jnp.where(is_first, moved[:, 0:width], moved[:, width:])
@@ -438,16 +442,21 @@
 ):
     rows, width = out_ref.shape
     sums = fill(query_ref, key_ref, member_ref, x_ref, query_scr, key_scr, value_scr)
+
+    def scores_of(begin):
+        end = begin + TILE
+        query = query_scr[begin:end, :]
+        pieces = [dot_t(query, key_scr[0:begin, :])] if begin else []
+        scores = dot_t(query, key_scr[begin:end, :])
+        allowed = iota((TILE, TILE), 1) <= iota((TILE, TILE), 0)
+        return pieces + [jnp.where(allowed, scores, -FAR)]
+
+    ahead = scores_of(0)
     for begin in range(0, rows, TILE):
         end = begin + TILE
-        query = query_scr[begin:end, :]
-        pieces, values = [], []
-        if begin:
-            pieces.append(dot_t(query, key_scr[0:begin, :]))
-            values.append(value_scr[0:begin, :])
-        scores = dot_t(query, key_scr[begin:end, :])
-        allowed = iota((TILE, TILE), 1) <= iota((TILE, TILE), 0)
-        pieces.append(jnp.where(allowed, scores, -FAR))
+        pieces = ahead
+        ahead = scores_of(end) if end < rows else None
+        values = [value_scr[0:begin, :]] if begin else []
         values.append(value_scr[begin:end, :])
         result = weigh(pieces, values, width) + homeward(begin, TILE, sums_row_ref, sums)
         out_ref[begin:end] = result.astype(out_ref.dtype)
@@ -510,60 +519,63 @@
     )(*given)
 
 
-def unpack_kernel(place_ref, sums_col_ref, over_ref, back_ref, out_ref, sums_ref):
+def unpack_kernel(
+    room, place_ref, sums_col_ref, first_ref, over_ref, back_ref, out_ref, sums_ref, pair_scr
+):
     toks, heads = place_ref.shape
     rows, width = back_ref.shape
-    groups = out_ref.shape[0]
-    share = toks // groups
-    back = back_ref[...]
-    for h in range(heads):
-        pick = flags(iota((toks, rows), 1) == place_ref[:, h : h + 1])
-        moved = dot(pick, back).astype(out_ref.dtype)
-        for g in range(groups):
-            out_ref[g, 0:share, h * width : (h + 1) * width] = moved[g * share : (g + 1) * share]
-    spare = out_ref.shape[1] - share
-    for g in range(groups):
-        out_ref[g, share:, :] = jnp.broadcast_to(
-            over_ref[0:1, 0:1], (spare, out_ref.shape[2])
-        ).astype(out_ref.dtype)
+    groups, share, _ = out_ref.shape
 
     @pl.when(pl.program_id(0) == 0)
     def _():
+        back = back_ref[...]
+        is_first = of_first(room, rows, 0, first_ref)
+        pair_scr[:, 0:width] = jnp.where(is_first, back.astype(F32), 0.0).astype(BF16)
+        pair_scr[:, width:] = jnp.where(is_first, 0.0, back.astype(F32)).astype(BF16)
         items = sums_col_ref.shape[0]
         pick = flags(iota((items, rows), 1) == sums_col_ref[:, 0:1])
         sums_ref[...] = dot(pick, back)
 
-
-def unpack(place, sums_col, over, back, groups):
+    wanted = iota((toks, rows), 1)
+    pick = flags((wanted == place_ref[:, 0:1]) | (wanted == place_ref[:, 1:2]))
+    moved = dot(pick, pair_scr[...])
+    moved = jnp.where(over_ref[0:1, 0:1] > 0.5, jnp.nan, moved).astype(out_ref.dtype)
+    for g in range(groups):
+        out_ref[g] = moved[g * share : (g + 1) * share]
+
+
+def unpack(place, sums_col, first, over, back, groups, room):
     (toks, heads), (rows, width) = place.shape, back.shape
     share = toks // groups
     items = sums_col.shape[0]
     steps = max(1, min(groups, groups * rows // 8192))
     whole = lambda i: (0, 0)
     return pl.pallas_call(
-        unpack_kernel,
+        functools.partial(unpack_kernel, room),
         grid=(steps,),
         in_specs=[
             pl.BlockSpec((toks // steps, heads), lambda i: (i, 0)),
             pl.BlockSpec(sums_col.shape, whole),
+            pl.BlockSpec(first.shape, whole),
             pl.BlockSpec(over.shape, whole),
             pl.BlockSpec((rows, width), whole),
         ],
         out_specs=(
-            pl.BlockSpec((groups // steps, share + 16, heads * width), lambda i: (i, 0, 0)),
+            pl.BlockSpec((groups // steps, share, heads * width), lambda i: (i, 0, 0)),
             pl.BlockSpec((items, width), whole),
         ),
         out_shape=(
-            jax.ShapeDtypeStruct((groups, share + 16, heads * width), back.dtype),
+            jax.ShapeDtypeStruct((groups, share, heads * width), back.dtype),
             jax.ShapeDtypeStruct((items, width), F32),
         ),
+        scratch_shapes=[pltpu.VMEM((rows, heads * width), BF16)],
         compiler_params=PARAMS,
         cost_estimate=pl.CostEstimate(
             flops=2 * rows * toks * width * heads,
             bytes_accessed=rows * width * 2,
             transcendentals=0,
         ),
-    )(place, sums_col, over, back)
+    )(place, sums_col, first, over, back)
 
 
 def exchange(rows, axis):
@@ -578,7 +590,7 @@
     received = exchange(pack(place, first, queries, keys, values, room, owners), "seq")
     sums_row, sums_col, query_far, key_far, member = arrive(me, everyone, own, rows, cols, room)
     back = exchange(attend(query_far, key_far, member, sums_row, received), "seq")
-    share, sums = unpack(place.T, sums_col, over, back, lax.axis_size("head"))
+    share, sums = unpack(place.T, sums_col, first, over, back, lax.axis_size("head"), room)
     parts = exchange(share, "head")
     owned = CLUSTERS // owners
     sums = jnp.concatenate([sums[h * owned : (h + 1) * owned] for h in range(heads)], axis=1)
@@ -586,9 +598,8 @@
 
 
 def project(parts, weight):
-    toks = parts.shape[1] - 16
     weight = weight.reshape(parts.shape[0], parts.shape[2], weight.shape[1])
-    total = jnp.einsum("gtd,gdn->tn", parts[:, :toks], weight, preferred_element_type=F32)
+    total = jnp.einsum("gtd,gdn->tn", parts, weight, preferred_element_type=F32)
     return total.astype(BF16)
 
 
@@ -615,7 +626,7 @@
     def done():
         return project(parts, full_weight), key_sums
 
-    return lax.cond(jnp.max(parts[:, -1, 0].astype(F32)) > 0.5, again, done)
+    return lax.cond(jnp.any(jnp.isnan(parts[:, 0, 0])), again, done)
 
 
 def solution(mesh):

time: 213 us -> 213 us (level)
  no operation moved by 1% of the time
where the time goes in v7:
time: 213 us
  waiting for transfers between devices  122 us (57%)
  starting transfers between devices  46.6 us (22%)
  Pallas kernels  19.1 us (9%)
  between operations  14.9 us (7%)
  matrix products  4.89 us (2%)
  other arithmetic  3.6 us (2%)
    all_to_all x4, waiting for transfers between devices, exchange(): return lax.all_to_all(rows, axis, split_axis=0, concat_axis=0, tiled=True)  121 us
    all_to_all x4, starting transfers between devices, exchange(): return lax.all_to_all(rows, axis, split_axis=0, concat_axis=0, tiled=True)  46.5 us
    pallas_call x1, Pallas kernels, make_plan(): pl.pallas_call(functools.partial(plan_kernel, room), out_shape=(jax.Shape...  5.25 us
    pallas_call x1, Pallas kernels, attend(): pl.pallas_call(attend_kernel, out_shape=shape, scratch_shapes=filled, com...  5.12 us
    dot_general x1, matrix products, project(): total = jnp.einsum('gtd,gdn->tn', parts, weight, preferred_element_type=F32)  4.89 us
    pallas_call x1, Pallas kernels, pack(): pl.pallas_call(functools.partial(pack_kernel, room), grid=(rows_all // ti...  4.36 us
  transfers between devices with their start and end apart: 5, of which 4 were waited for; matrix products, arithmetic and copies ran while one was open for 2% of the time, Pallas kernels for 9%

profile of v7, /device:TPU:1, one launch (start us, length us, event | category | flops | bytes accessed | tf_op | source)
XLA Modules:
  0.0 212.5 jit_solution(13828893932997154127)
XLA Ops:
  7.2 0.0 copy-start.7
  7.2 0.0 copy-start.9
  7.2 0.0 copy-start.11
  7.2 0.0 all-gather.2.cloned.1.call-start
  7.2 0.7 all-gather.2.cloned.1.call-update
  7.9 1.1 convert_reduce_fusion.1.own_ref
  9.1 0.7 broadcast_in_dim.6
  9.8 19.3 %all-to-all-start.3 = ((bf16[64,8,128]{2,1,0:T(8,128)(2,1)}), bf16[64,8,128]{2,1,0:T(8,128)(2,1)S(1)}, u32[]{:S(2)}, u32[]{:S(2)}) async-start(bf16[64,8,128]{2,1,0:T(8,128)(2,1)} %broadcast_in_dim.6), calls=%async_computation.3 | async-start | bytes 262144 | tf_op jit(solution)/shard_map/all_to_all | solution.py:582
  29.0 0.2 iota_compare_fusion.1
  29.2 1.6 convert_reduce_fusion.rank_ref
  30.9 13.1 %all-to-all-done.3 = bf16[64,8,128]{2,1,0:T(8,128)(2,1)S(1)} async-done(((bf16[64,8,128]{2,1,0:T(8,128)(2,1)}), bf16[64,8,128]{2,1,0:T(8,128)(2,1)S(1)}, u32[]{:S(2)}, u32[]{:S(2)}) %all-to-all-start.3) | async-done | bytes 131104 | tf_op jit(solution)/shard_map/all_to_all | solution.py:582
  44.0 5.3 %shard_map.68 = (s32[2,768]{1,0:T(2,128)S(1)}, s32[8,512]{1,0:T(8,128)S(1)}, s32[512,128]{1,0:T(8,128)S(1)}, f32[8,128]{1,0:T(8,128)S(1)}, f32[8,128]{1,0:T(8,128)S(1)}) custom-call(bf16[64,1024]{1,0:T(8,128)(2,1)S(1)} %bitcast.40, f32[2,512]{1,0:T(2,128)S(1)} %convert_reduce_fusion.1.own_ref, s32[2,768]{1,0:T(2,128)} %ids_ref.1, ...), custom_call_target="tpu_custom_call" | custom-call | flops 1000000000 | bytes 1000000 | tf_op jit(solution)/shard_map/pallas_call | solution.py:291
  49.2 0.0 copy-done.7
  49.2 0.0 copy-done.9
  49.2 0.0 copy-done.11
  49.3 4.4 %shard_map.70 = bf16[2048,384]{1,0:T(8,128)(2,1)} custom-call(s32[2,768]{1,0:T(2,128)S(1)} %get-tuple-element.64.place_ref, f32[8,128]{1,0:T(8,128)S(1)} %get-tuple-element.68.first_ref, bf16[768,256]{1,0:T(8,128)(2,1)S(1)} %copy-done.7, bf16[768,256]{1,0:T(8,128)(2,1)S(1)} %copy-done.9, bf16[768,256]{1,0:T(8,128)(2,1)S(1)} %copy-done.11), custom_call_target="tpu_custom_call" | custom-call | flops 2415919104 | bytes 1572864 | tf_op jit(solution)/shard_map/pallas_call | solution.py:364
  53.6 6.6 %all-to-all-start.4 = ((bf16[64,32,384]{2,1,0:T(8,128)(2,1)}), bf16[64,32,384]{2,1,0:T(8,128)(2,1)S(1)}, u32[]{:S(2)}, u32[]{:S(2)}) async-start(bf16[64,32,384]{2,1,0:T(8,128)(2,1)} %bitcast.12), calls=%async_computation.4 | async-start | bytes 3145728 | tf_op jit(solution)/shard_map/all_to_all | solution.py:582
  60.2 1.5 shard_map.69
  61.7 71.0 %all-to-all-done.4 = bf16[64,32,384]{2,1,0:T(8,128)(2,1)S(1)} async-done(((bf16[64,32,384]{2,1,0:T(8,128)(2,1)}), bf16[64,32,384]{2,1,0:T(8,128)(2,1)S(1)}, u32[]{:S(2)}, u32[]{:S(2)}) %all-to-all-start.4) | async-done | bytes 1572896 | tf_op jit(solution)/shard_map/all_to_all | solution.py:582
  132.6 5.1 %shard_map.71 = bf16[2048,128]{1,0:T(8,128)(2,1)} custom-call(bf16[2048,128]{1,0:T(8,128)(2,1)S(1)} %get-tuple-element.70.query_ref, bf16[2048,128]{1,0:T(8,128)(2,1)S(1)} %get-tuple-element.71.key_ref, bf16[16,2048]{1,0:T(8,128)(2,1)S(1)} %get-tuple-element.72.member_ref, s32[8,128]{1,0:T(8,128)S(1)} %get-tuple-element.73.sums_row_ref, ...), custom_call_target="tpu_custom_call" | custom-call | flops 1073741824 | bytes 2097152 | tf_op jit(solution)/shard_map/pallas_call | solution.py:502
  137.8 0.0 copy-start.5
  137.8 0.0 copy-start.8
  137.8 0.0 copy-start.10
  137.8 0.0 copy-start.12
  137.8 10.0 %all-to-all-start.5 = ((bf16[64,32,128]{2,1,0:T(8,128)(2,1)}), bf16[64,32,128]{2,1,0:T(8,128)(2,1)S(1)}, u32[]{:S(2)}, u32[]{:S(2)}) async-start(bf16[64,32,128]{2,1,0:T(8,128)(2,1)} %bitcast.14), calls=%async_computation.5 | async-start | bytes 1048576 | tf_op jit(solution)/shard_map/all_to_all | solution.py:582
  147.8 0.2 copy.10
  148.0 28.8 %all-to-all-done.5 = bf16[64,32,128]{2,1,0:T(8,128)(2,1)S(1)} async-done(((bf16[64,32,128]{2,1,0:T(8,128)(2,1)}), bf16[64,32,128]{2,1,0:T(8,128)(2,1)S(1)}, u32[]{:S(2)}, u32[]{:S(2)}) %all-to-all-start.5) | async-done | bytes 524320 | tf_op jit(solution)/shard_map/all_to_all | solution.py:582
  176.8 2.9 %shard_map.72 = (bf16[8,96,256]{2,1,0:T(8,128)(2,1)}, f32[16,128]{1,0:T(8,128)S(1)}) custom-call(s32[768,2]{1,0:T(8,128)S(1)} %bitcast.35, s32[16,128]{1,0:T(8,128)S(1)} %get-tuple-element.67.sums_col_ref, f32[8,128]{1,0:T(8,128)S(1)} %get-tuple-element.68.first_ref, f32[8,128]{1,0:T(8,128)S(1)} %get-tuple-element.69.over_ref, bf16[2048,128]{1,0:T(8,128)(2,1)S(1)} %bitcast.34), custom_call_target="tpu_custom_call" | custom-call | flops 805306368 | bytes 524288 | tf_op jit(solution)/shard_map/pallas_call | solution.py:553
  179.7 10.6 %all-to-all-start.6 = ((bf16[8,96,256]{2,1,0:T(8,128)(2,1)}), bf16[8,96,256]{2,1,0:T(8,128)(2,1)S(1)}, u32[]{:S(2)}, u32[]{:S(2)}) async-start(bf16[8,96,256]{2,1,0:T(8,128)(2,1)} %get-tuple-element.74), calls=%async_computation.6 | async-start | bytes 786432 | tf_op jit(solution)/shard_map/all_to_all | solution.py:582
  190.3 8.1 %all-to-all-done.6 = bf16[8,96,256]{2,1,0:T(8,128)(2,1)S(1)} async-done(((bf16[8,96,256]{2,1,0:T(8,128)(2,1)}), bf16[8,96,256]{2,1,0:T(8,128)(2,1)S(1)}, u32[]{:S(2)}, u32[]{:S(2)}) %all-to-all-start.6) | async-done | bytes 393248 | tf_op jit(solution)/shard_map/all_to_all | solution.py:582
  198.4 0.6 compare_reduce_fusion
  199.7 0.0 all-gather.2.cloned.1.call-done
  199.7 0.0 copy-done.5
  199.7 0.0 copy-done.8
  199.7 0.0 copy-done.10
  199.7 0.0 copy-done.12
  199.7 5.2 %conditional.2 = (f32[8,256]{1,0:T(8,128)S(1)}, bf16[96,2048]{1,0:T(8,128)(2,1)S(1)}) conditional(s32[]{:T(128)} %convert_element_type.28, (bf16[2048,2048]{1,0:T(8,128)(2,1)}, bf16[8,96,256]{2,1,0:T(8,128)(2,1)S(1)}, f32[8,256]{1,0:T(8,128)S(1)}) %tuple.19, (bf16[64,1024]{1,0:T(8,128)(2,1)S(1)}, f32[2,512]{1,0:T(2,128)S(1)}, s32[2,768]{1,0:T(2,128)S(1)}, ...), branch_computations={%region_3.0_spmd, %region_4.0_spmd} | conditional | flops 32870275072 | bytes 104674680
  199.8 4.9 %fusion = bf16[96,2048]{1,0:T(8,128)(2,1)S(1)} fusion(bf16[8,96,256]{2,1,0:T(8,128)(2,1)S(1)} %get-tuple-element.25, bf16[8,256,2048]{2,1,0:T(8,128)(2,1)} %bitcast.37), kind=kOutput, calls=%fused_computation.1 | convolution fusion | flops 805502976 | bytes 9175040 | tf_op jit(solution)/shard_map/cond/branch_0_fun/gtd,gdn->tn/dot_general | solution.py:602
  204.9 0.0 copy-start.4
  204.9 0.0 copy-start.6
  204.9 0.7 copy-done.4
  205.7 0.0 copy-done.6
  (5 shorter events, 0.0 us)
Async XLA Ops:
  7.2 42.1 %copy-start.7 = (bf16[768,256]{1,0:T(8,128)(2,1)S(1)}, bf16[768,256]{1,0:T(8,128)(2,1)}, u32[]{:S(2)}) copy-start(bf16[768,256]{1,0:T(8,128)(2,1)} %q_ref.1) | copy-start | bytes 1179652
  7.2 42.1 %copy-start.9 = (bf16[768,256]{1,0:T(8,128)(2,1)S(1)}, bf16[768,256]{1,0:T(8,128)(2,1)}, u32[]{:S(2)}) copy-start(bf16[768,256]{1,0:T(8,128)(2,1)} %k_ref.1) | copy-start | bytes 1179652
  7.2 42.1 %copy-start.11 = (bf16[768,256]{1,0:T(8,128)(2,1)S(1)}, bf16[768,256]{1,0:T(8,128)(2,1)}, u32[]{:S(2)}) copy-start(bf16[768,256]{1,0:T(8,128)(2,1)} %v_ref.1) | copy-start | bytes 1179652
  7.2 192.5 %all-gather.2.cloned.1.call-start = ((), (), s32[]{:S(2)}) async-start(), calls=%async_computation.7 | async-start | bytes 9437184 | tf_op jit(solution)/shard_map/all_gather | solution.py:613
  9.8 34.2 %all-to-all-start.3 = ((bf16[64,8,128]{2,1,0:T(8,128)(2,1)}), bf16[64,8,128]{2,1,0:T(8,128)(2,1)S(1)}, u32[]{:S(2)}, u32[]{:S(2)}) async-start(bf16[64,8,128]{2,1,0:T(8,128)(2,1)} %broadcast_in_dim.6), calls=%async_computation.3 | async-start | bytes 262144 | tf_op jit(solution)/shard_map/all_to_all | solution.py:582
  53.6 79.0 %all-to-all-start.4 = ((bf16[64,32,384]{2,1,0:T(8,128)(2,1)}), bf16[64,32,384]{2,1,0:T(8,128)(2,1)S(1)}, u32[]{:S(2)}, u32[]{:S(2)}) async-start(bf16[64,32,384]{2,1,0:T(8,128)(2,1)} %bitcast.12), calls=%async_computation.4 | async-start | bytes 3145728 | tf_op jit(solution)/shard_map/all_to_all | solution.py:582
  137.8 62.0 %copy-start.5 = (s32[2,768]{1,0:T(2,128)S(1)}, s32[2,768]{1,0:T(2,128)}, u32[]{:S(2)}) copy-start(s32[2,768]{1,0:T(2,128)} %ids_ref.1) | copy-start | bytes 18436
  137.8 62.0 %copy-start.8 = (bf16[768,256]{1,0:T(8,128)(2,1)S(1)}, bf16[768,256]{1,0:T(8,128)(2,1)}, u32[]{:S(2)}) copy-start(bf16[768,256]{1,0:T(8,128)(2,1)} %q_ref.1) | copy-start | bytes 1179652
  137.8 62.0 %copy-start.10 = (bf16[768,256]{1,0:T(8,128)(2,1)S(1)}, bf16[768,256]{1,0:T(8,128)(2,1)}, u32[]{:S(2)}) copy-start(bf16[768,256]{1,0:T(8,128)(2,1)} %k_ref.1) | copy-start | bytes 1179652
  137.8 62.0 %copy-start.12 = (bf16[768,256]{1,0:T(8,128)(2,1)S(1)}, bf16[768,256]{1,0:T(8,128)(2,1)}, u32[]{:S(2)}) copy-start(bf16[768,256]{1,0:T(8,128)(2,1)} %v_ref.1) | copy-start | bytes 1179652
  137.8 39.0 %all-to-all-start.5 = ((bf16[64,32,128]{2,1,0:T(8,128)(2,1)}), bf16[64,32,128]{2,1,0:T(8,128)(2,1)S(1)}, u32[]{:S(2)}, u32[]{:S(2)}) async-start(bf16[64,32,128]{2,1,0:T(8,128)(2,1)} %bitcast.14), calls=%async_computation.5 | async-start | bytes 1048576 | tf_op jit(solution)/shard_map/all_to_all | solution.py:582
  179.7 18.7 %all-to-all-start.6 = ((bf16[8,96,256]{2,1,0:T(8,128)(2,1)}), bf16[8,96,256]{2,1,0:T(8,128)(2,1)S(1)}, u32[]{:S(2)}, u32[]{:S(2)}) async-start(bf16[8,96,256]{2,1,0:T(8,128)(2,1)} %get-tuple-element.74), calls=%async_computation.6 | async-start | bytes 786432 | tf_op jit(solution)/shard_map/all_to_all | solution.py:582
  204.9 0.7 copy-start.4
  204.9 0.7 copy-start.6
Sparse Core Ops, SparseCore 0:
  10.2 63.0 all-gather.1

commit v8 on v7

--- a/solution.py
+++ b/solution.py
@@ -359,7 +359,7 @@
     toks, width = queries.shape
     heads = place.shape[0]
     rows_all = owners * room
-    tile = 512
+    tile = 1024
     whole = pl.BlockSpec((toks, width), lambda i: (0, 0))
     return pl.pallas_call(
         functools.partial(pack_kernel, room),
@@ -603,13 +603,37 @@
     return total.astype(BF16)
 
 
+def count_kernel(ids_ref, own_ref, told_ref, member_scr):
+    heads, toks = ids_ref.shape
+    chunks = []
+    for h in range(heads):
+        member_scr[h] = flags(iota((CLUSTERS, toks), 0) == ids_ref[h : h + 1, :])
+        own = dot_t(jnp.ones((8, toks), BF16), member_scr[h])
+        own_ref[h : h + 1, :] = own[0:1]
+        chunks += [own[0:1, at : at + LANES] for at in range(0, CLUSTERS, LANES)]
+    told_ref[...] = jnp.broadcast_to(jnp.concatenate(chunks, axis=0)[None], told_ref.shape).astype(BF16)
+
+
+def count(cluster_ids, owners):
+    heads, toks = cluster_ids.shape
+    return pl.pallas_call(
+        count_kernel,
+        out_shape=(
+            jax.ShapeDtypeStruct((heads, CLUSTERS), F32),
+            jax.ShapeDtypeStruct((owners, heads * CLUSTERS // LANES, LANES), BF16),
+        ),
+        scratch_shapes=[pltpu.VMEM((heads, CLUSTERS, toks), BF16)],
+        compiler_params=PARAMS,
+        cost_estimate=pl.CostEstimate(flops=10**8, bytes_accessed=10**5, transcendentals=0),
+    )(cluster_ids)
+
+
 def body(queries, keys, values, cluster_ids, out_weight):
     heads, toks = cluster_ids.shape
     owners = lax.axis_size("seq")
-    clusters = jnp.arange(CLUSTERS, dtype=I32)
-    own = jnp.sum((cluster_ids[:, None, :] == clusters[None, :, None]).astype(F32), axis=2)
-    told = jnp.broadcast_to(own.astype(BF16).reshape(1, 8, LANES), (owners, 8, LANES))
+    own, told = count(cluster_ids, owners)
     everyone = exchange(told, "seq").reshape(owners, heads * CLUSTERS)
+    own, out_weight = lax.optimization_barrier((own, out_weight))
     full_weight = lax.all_gather(out_weight, "head", axis=0, tiled=True)
 
     spot = jnp.arange(toks, dtype=I32)

time: 213 us -> 210 us (0.986)
  transfers between devices with their start and end apart: 5 -> 5, of which waited for: 4 -> 4; matrix products, arithmetic and copies ran while one was open for 2% -> 1% of each run, Pallas kernels for 9% -> 9%
where the time goes in v8:
time: 210 us; the launch traced here: 209 us
  waiting for transfers between devices  121 us (58%)
  starting transfers between devices  44.9 us (21%)
  Pallas kernels  20.3 us (10%)
  between operations  14.9 us (7%)
  matrix products  4.89 us (2%)
  other arithmetic  2.47 us (1%)
    all_to_all x4, waiting for transfers between devices, exchange(): return lax.all_to_all(rows, axis, split_axis=0, concat_axis=0, tiled=True)  121 us
    all_to_all x4, starting transfers between devices, exchange(): return lax.all_to_all(rows, axis, split_axis=0, concat_axis=0, tiled=True)  44.9 us
    pallas_call x1, Pallas kernels, attend(): pl.pallas_call(attend_kernel, out_shape=shape, scratch_shapes=filled, com...  5.08 us
    dot_general x1, matrix products, project(): total = jnp.einsum('gtd,gdn->tn', parts, weight, preferred_element_type=F32)  4.89 us
    pallas_call x1, Pallas kernels, make_plan(): pl.pallas_call(functools.partial(plan_kernel, room), out_shape=(jax.Shape...  4.8 us
  transfers between devices with their start and end apart: 5, of which 4 were waited for; matrix products, arithmetic and copies ran while one was open for 1% of the time, Pallas kernels for 9%

profile of v8, /device:TPU:1, one launch (start us, length us, event | category | flops | bytes accessed | tf_op | source)
XLA Modules:
  0.0 209.5 jit_solution(6954879221625551123)
XLA Ops:
  7.2 0.0 copy-start.7
  7.2 0.0 copy-start.8
  7.2 0.0 copy-start.10
  7.2 0.0 all-gather.2.cloned.1.call-start
  7.2 2.0 shard_map.68
  9.2 0.0 all-gather.2.cloned.1.call-update
  9.2 19.3 %all-to-all-start.3 = ((bf16[64,8,128]{2,1,0:T(8,128)(2,1)}), bf16[64,8,128]{2,1,0:T(8,128)(2,1)S(1)}, u32[]{:S(2)}, u32[]{:S(2)}) async-start(bf16[64,8,128]{2,1,0:T(8,128)(2,1)} %get-tuple-element.68), calls=%async_computation.3 | async-start | bytes 262144 | tf_op jit(solution)/shard_map/all_to_all | solution.py:582
  28.5 0.2 iota_compare_fusion
  28.7 1.6 convert_reduce_fusion.rank_ref
  30.4 13.1 %all-to-all-done.3 = bf16[64,8,128]{2,1,0:T(8,128)(2,1)S(1)} async-done(((bf16[64,8,128]{2,1,0:T(8,128)(2,1)}), bf16[64,8,128]{2,1,0:T(8,128)(2,1)S(1)}, u32[]{:S(2)}, u32[]{:S(2)}) %all-to-all-start.3) | async-done | bytes 131104 | tf_op jit(solution)/shard_map/all_to_all | solution.py:582
  43.5 4.8 %shard_map.69 = (s32[2,768]{1,0:T(2,128)S(1)}, s32[8,512]{1,0:T(8,128)S(1)}, s32[512,128]{1,0:T(8,128)S(1)}, f32[8,128]{1,0:T(8,128)S(1)}, f32[8,128]{1,0:T(8,128)S(1)}) custom-call(bf16[64,1024]{1,0:T(8,128)(2,1)S(1)} %bitcast.40, f32[2,512]{1,0:T(2,128)S(1)} %get-tuple-element.70.own_ref, s32[2,768]{1,0:T(2,128)} %ids_ref.3, ...), custom_call_target="tpu_custom_call" | custom-call | flops 1000000000 | bytes 1000000 | tf_op jit(solution)/shard_map/pallas_call | solution.py:291
  48.3 0.0 copy-done.7
  48.3 0.0 copy-done.8
  48.3 0.0 copy-done.10
  48.3 4.1 %shard_map.71 = bf16[2048,384]{1,0:T(8,128)(2,1)} custom-call(s32[2,768]{1,0:T(2,128)S(1)} %get-tuple-element.71.place_ref, f32[8,128]{1,0:T(8,128)S(1)} %get-tuple-element.75.first_ref, bf16[768,256]{1,0:T(8,128)(2,1)S(1)} %copy-done.7, bf16[768,256]{1,0:T(8,128)(2,1)S(1)} %copy-done.8, bf16[768,256]{1,0:T(8,128)(2,1)S(1)} %copy-done.10), custom_call_target="tpu_custom_call" | custom-call | flops 2415919104 | bytes 1572864 | tf_op jit(solution)/shard_map/pallas_call | solution.py:364
  52.4 6.6 %all-to-all-start.4 = ((bf16[64,32,384]{2,1,0:T(8,128)(2,1)}), bf16[64,32,384]{2,1,0:T(8,128)(2,1)S(1)}, u32[]{:S(2)}, u32[]{:S(2)}) async-start(bf16[64,32,384]{2,1,0:T(8,128)(2,1)} %bitcast.12), calls=%async_computation.4 | async-start | bytes 3145728 | tf_op jit(solution)/shard_map/all_to_all | solution.py:582
  59.0 1.5 shard_map.70
  60.5 0.0 copy-start.5
  60.5 70.9 %all-to-all-done.4 = bf16[64,32,384]{2,1,0:T(8,128)(2,1)S(1)} async-done(((bf16[64,32,384]{2,1,0:T(8,128)(2,1)}), bf16[64,32,384]{2,1,0:T(8,128)(2,1)S(1)}, u32[]{:S(2)}, u32[]{:S(2)}) %all-to-all-start.4) | async-done | bytes 1572896 | tf_op jit(solution)/shard_map/all_to_all | solution.py:582
  131.4 5.1 %shard_map.72 = bf16[2048,128]{1,0:T(8,128)(2,1)} custom-call(bf16[2048,128]{1,0:T(8,128)(2,1)S(1)} %get-tuple-element.77.query_ref, bf16[2048,128]{1,0:T(8,128)(2,1)S(1)} %get-tuple-element.78.key_ref, bf16[16,2048]{1,0:T(8,128)(2,1)S(1)} %get-tuple-element.79.member_ref, s32[8,128]{1,0:T(8,128)S(1)} %get-tuple-element.80.sums_row_ref, ...), custom_call_target="tpu_custom_call" | custom-call | flops 1073741824 | bytes 2097152 | tf_op jit(solution)/shard_map/pallas_call | solution.py:502
  136.5 0.0 copy-start.9
  136.5 0.0 copy-start.11
  136.5 10.0 %all-to-all-start.5 = ((bf16[64,32,128]{2,1,0:T(8,128)(2,1)}), bf16[64,32,128]{2,1,0:T(8,128)(2,1)S(1)}, u32[]{:S(2)}, u32[]{:S(2)}) async-start(bf16[64,32,128]{2,1,0:T(8,128)(2,1)} %bitcast.14), calls=%async_computation.5 | async-start | bytes 1048576 | tf_op jit(solution)/shard_map/all_to_all | solution.py:582
  146.5 0.2 copy.10
  146.7 28.7 %all-to-all-done.5 = bf16[64,32,128]{2,1,0:T(8,128)(2,1)S(1)} async-done(((bf16[64,32,128]{2,1,0:T(8,128)(2,1)}), bf16[64,32,128]{2,1,0:T(8,128)(2,1)S(1)}, u32[]{:S(2)}, u32[]{:S(2)}) %all-to-all-start.5) | async-done | bytes 524320 | tf_op jit(solution)/shard_map/all_to_all | solution.py:582
  175.4 2.9 %shard_map.73 = (bf16[8,96,256]{2,1,0:T(8,128)(2,1)}, f32[16,128]{1,0:T(8,128)S(1)}) custom-call(s32[768,2]{1,0:T(8,128)S(1)} %bitcast.35, s32[16,128]{1,0:T(8,128)S(1)} %get-tuple-element.74.sums_col_ref, f32[8,128]{1,0:T(8,128)S(1)} %get-tuple-element.75.first_ref, f32[8,128]{1,0:T(8,128)S(1)} %get-tuple-element.76.over_ref, bf16[2048,128]{1,0:T(8,128)(2,1)S(1)} %bitcast.34), custom_call_target="tpu_custom_call" | custom-call | flops 805306368 | bytes 524288 | tf_op jit(solution)/shard_map/pallas_call | solution.py:553
  178.3 9.0 %all-to-all-start.6 = ((bf16[8,96,256]{2,1,0:T(8,128)(2,1)}), bf16[8,96,256]{2,1,0:T(8,128)(2,1)S(1)}, u32[]{:S(2)}, u32[]{:S(2)}) async-start(bf16[8,96,256]{2,1,0:T(8,128)(2,1)} %get-tuple-element.81), calls=%async_computation.6 | async-start | bytes 786432 | tf_op jit(solution)/shard_map/all_to_all | solution.py:582
  187.3 8.1 %all-to-all-done.6 = bf16[8,96,256]{2,1,0:T(8,128)(2,1)S(1)} async-done(((bf16[8,96,256]{2,1,0:T(8,128)(2,1)}), bf16[8,96,256]{2,1,0:T(8,128)(2,1)S(1)}, u32[]{:S(2)}, u32[]{:S(2)}) %all-to-all-start.6) | async-done | bytes 393248 | tf_op jit(solution)/shard_map/all_to_all | solution.py:582
  195.4 0.6 compare_reduce_fusion
  196.7 0.0 all-gather.2.cloned.1.call-done
  196.7 0.0 copy-done.5
  196.7 0.0 copy-done.9
  196.7 0.0 copy-done.11
  196.7 5.2 %conditional.2 = (f32[8,256]{1,0:T(8,128)S(1)}, bf16[96,2048]{1,0:T(8,128)(2,1)S(1)}) conditional(s32[]{:T(128)} %convert_element_type.12, (bf16[2048,2048]{1,0:T(8,128)(2,1)}, bf16[8,96,256]{2,1,0:T(8,128)(2,1)S(1)}, f32[8,256]{1,0:T(8,128)S(1)}) %tuple.21, (bf16[64,1024]{1,0:T(8,128)(2,1)S(1)}, f32[2,512]{1,0:T(2,128)S(1)}, s32[2,768]{1,0:T(2,128)S(1)}, ...), branch_computations={%region_2.0_spmd, %region_3.0_spmd} | conditional | flops 32870275072 | bytes 104674680
  196.7 4.9 %fusion = bf16[96,2048]{1,0:T(8,128)(2,1)S(1)} fusion(bf16[8,96,256]{2,1,0:T(8,128)(2,1)S(1)} %get-tuple-element.25, bf16[8,256,2048]{2,1,0:T(8,128)(2,1)} %bitcast.37), kind=kOutput, calls=%fused_computation.1 | convolution fusion | flops 805502976 | bytes 9175040 | tf_op jit(solution)/shard_map/cond/branch_0_fun/gtd,gdn->tn/dot_general | solution.py:602
  201.9 0.0 copy-start.4
  201.9 0.0 copy-start.6
  201.9 0.7 copy-done.4
  202.6 0.0 copy-done.6
  (3 shorter events, 0.0 us)
Async XLA Ops:
  7.2 41.1 %copy-start.7 = (bf16[768,256]{1,0:T(8,128)(2,1)S(1)}, bf16[768,256]{1,0:T(8,128)(2,1)}, u32[]{:S(2)}) copy-start(bf16[768,256]{1,0:T(8,128)(2,1)} %q_ref.1) | copy-start | bytes 1179652
  7.2 41.1 %copy-start.8 = (bf16[768,256]{1,0:T(8,128)(2,1)S(1)}, bf16[768,256]{1,0:T(8,128)(2,1)}, u32[]{:S(2)}) copy-start(bf16[768,256]{1,0:T(8,128)(2,1)} %k_ref.1) | copy-start | bytes 1179652
  7.2 41.1 %copy-start.10 = (bf16[768,256]{1,0:T(8,128)(2,1)S(1)}, bf16[768,256]{1,0:T(8,128)(2,1)}, u32[]{:S(2)}) copy-start(bf16[768,256]{1,0:T(8,128)(2,1)} %v_ref.1) | copy-start | bytes 1179652
  7.2 189.5 %all-gather.2.cloned.1.call-start = ((), (), s32[]{:S(2)}) async-start(), calls=%async_computation.7 | async-start | bytes 9437184 | tf_op jit(solution)/shard_map/all_gather | solution.py:637
  9.2 34.2 %all-to-all-start.3 = ((bf16[64,8,128]{2,1,0:T(8,128)(2,1)}), bf16[64,8,128]{2,1,0:T(8,128)(2,1)S(1)}, u32[]{:S(2)}, u32[]{:S(2)}) async-start(bf16[64,8,128]{2,1,0:T(8,128)(2,1)} %get-tuple-element.68), calls=%async_computation.3 | async-start | bytes 262144 | tf_op jit(solution)/shard_map/all_to_all | solution.py:582
  52.4 79.0 %all-to-all-start.4 = ((bf16[64,32,384]{2,1,0:T(8,128)(2,1)}), bf16[64,32,384]{2,1,0:T(8,128)(2,1)S(1)}, u32[]{:S(2)}, u32[]{:S(2)}) async-start(bf16[64,32,384]{2,1,0:T(8,128)(2,1)} %bitcast.12), calls=%async_computation.4 | async-start | bytes 3145728 | tf_op jit(solution)/shard_map/all_to_all | solution.py:582
  60.5 136.2 %copy-start.5 = (s32[2,768]{1,0:T(2,128)S(1)}, s32[2,768]{1,0:T(2,128)}, u32[]{:S(2)}) copy-start(s32[2,768]{1,0:T(2,128)} %ids_ref.3) | copy-start | bytes 18436
  136.5 60.2 %copy-start.9 = (bf16[768,256]{1,0:T(8,128)(2,1)S(1)}, bf16[768,256]{1,0:T(8,128)(2,1)}, u32[]{:S(2)}) copy-start(bf16[768,256]{1,0:T(8,128)(2,1)} %k_ref.1) | copy-start | bytes 1179652
  136.5 60.2 %copy-start.11 = (bf16[768,256]{1,0:T(8,128)(2,1)S(1)}, bf16[768,256]{1,0:T(8,128)(2,1)}, u32[]{:S(2)}) copy-start(bf16[768,256]{1,0:T(8,128)(2,1)} %v_ref.1) | copy-start | bytes 1179652
  136.5 38.9 %all-to-all-start.5 = ((bf16[64,32,128]{2,1,0:T(8,128)(2,1)}), bf16[64,32,128]{2,1,0:T(8,128)(2,1)S(1)}, u32[]{:S(2)}, u32[]{:S(2)}) async-start(bf16[64,32,128]{2,1,0:T(8,128)(2,1)} %bitcast.14), calls=%async_computation.5 | async-start | bytes 1048576 | tf_op jit(solution)/shard_map/all_to_all | solution.py:582
  178.3 17.1 %all-to-all-start.6 = ((bf16[8,96,256]{2,1,0:T(8,128)(2,1)}), bf16[8,96,256]{2,1,0:T(8,128)(2,1)S(1)}, u32[]{:S(2)}, u32[]{:S(2)}) async-start(bf16[8,96,256]{2,1,0:T(8,128)(2,1)} %get-tuple-element.81), calls=%async_computation.6 | async-start | bytes 786432 | tf_op jit(solution)/shard_map/all_to_all | solution.py:582
  201.9 0.7 copy-start.4
  201.9 0.7 copy-start.6
Sparse Core Ops, SparseCore 0:
  10.2 63.0 all-gather.1

commit v9 on v8

--- a/solution.py
+++ b/solution.py
@@ -548,7 +548,7 @@
     (toks, heads), (rows, width) = place.shape, back.shape
     share = toks // groups
     items = sums_col.shape[0]
-    steps = max(1, min(groups, groups * rows // 8192))
+    steps = max(1, min(groups, groups * rows // 16384))
     whole = lambda i: (0, 0)
     return pl.pallas_call(
         functools.partial(unpack_kernel, room),

time: 210 us -> 210 us (level)
  no operation moved by 1% of the time
where the time goes in v9:
time: 210 us
  waiting for transfers between devices  120 us (57%)
  starting transfers between devices  46.5 us (22%)
  Pallas kernels  20.1 us (10%)
  between operations  14.9 us (7%)
  matrix products  4.88 us (2%)
  other arithmetic  2.47 us (1%)
    all_to_all x4, waiting for transfers between devices, exchange(): return lax.all_to_all(rows, axis, split_axis=0, concat_axis=0, tiled=True)  120 us
    all_to_all x4, starting transfers between devices, exchange(): return lax.all_to_all(rows, axis, split_axis=0, concat_axis=0, tiled=True)  46.5 us
    pallas_call x1, Pallas kernels, attend(): pl.pallas_call(attend_kernel, out_shape=shape, scratch_shapes=filled, com...  5.08 us
    dot_general x1, matrix products, project(): total = jnp.einsum('gtd,gdn->tn', parts, weight, preferred_element_type=F32)  4.88 us
    pallas_call x1, Pallas kernels, make_plan(): pl.pallas_call(functools.partial(plan_kernel, room), out_shape=(jax.Shape...  4.8 us
  transfers between devices with their start and end apart: 5, of which 4 were waited for; matrix products, arithmetic and copies ran while one was open for 1% of the time, Pallas kernels for 9%

profile of v9, /device:TPU:1, one launch (start us, length us, event | category | flops | bytes accessed | tf_op | source)
XLA Modules:
  0.0 209.7 jit_solution(7411923041696878143)
XLA Ops:
  7.2 0.0 copy-start.7
  7.2 0.0 copy-start.8
  7.2 0.0 copy-start.10
  7.2 0.0 all-gather.2.cloned.1.call-start
  7.2 2.0 shard_map.68
  9.2 0.0 all-gather.2.cloned.1.call-update
  9.2 19.3 %all-to-all-start.3 = ((bf16[64,8,128]{2,1,0:T(8,128)(2,1)}), bf16[64,8,128]{2,1,0:T(8,128)(2,1)S(1)}, u32[]{:S(2)}, u32[]{:S(2)}) async-start(bf16[64,8,128]{2,1,0:T(8,128)(2,1)} %get-tuple-element.68), calls=%async_computation.3 | async-start | bytes 262144 | tf_op jit(solution)/shard_map/all_to_all | solution.py:582
  28.5 0.2 iota_compare_fusion
  28.7 1.6 convert_reduce_fusion.rank_ref
  30.4 13.1 %all-to-all-done.3 = bf16[64,8,128]{2,1,0:T(8,128)(2,1)S(1)} async-done(((bf16[64,8,128]{2,1,0:T(8,128)(2,1)}), bf16[64,8,128]{2,1,0:T(8,128)(2,1)S(1)}, u32[]{:S(2)}, u32[]{:S(2)}) %all-to-all-start.3) | async-done | bytes 131104 | tf_op jit(solution)/shard_map/all_to_all | solution.py:582
  43.5 4.8 %shard_map.69 = (s32[2,768]{1,0:T(2,128)S(1)}, s32[8,512]{1,0:T(8,128)S(1)}, s32[512,128]{1,0:T(8,128)S(1)}, f32[8,128]{1,0:T(8,128)S(1)}, f32[8,128]{1,0:T(8,128)S(1)}) custom-call(bf16[64,1024]{1,0:T(8,128)(2,1)S(1)} %bitcast.40, f32[2,512]{1,0:T(2,128)S(1)} %get-tuple-element.70.own_ref, s32[2,768]{1,0:T(2,128)} %ids_ref.3, ...), custom_call_target="tpu_custom_call" | custom-call | flops 1000000000 | bytes 1000000 | tf_op jit(solution)/shard_map/pallas_call | solution.py:291
  48.3 0.0 copy-done.7
  48.3 0.0 copy-done.8
  48.3 0.0 copy-done.10
  48.3 4.1 %shard_map.71 = bf16[2048,384]{1,0:T(8,128)(2,1)} custom-call(s32[2,768]{1,0:T(2,128)S(1)} %get-tuple-element.71.place_ref, f32[8,128]{1,0:T(8,128)S(1)} %get-tuple-element.75.first_ref, bf16[768,256]{1,0:T(8,128)(2,1)S(1)} %copy-done.7, bf16[768,256]{1,0:T(8,128)(2,1)S(1)} %copy-done.8, bf16[768,256]{1,0:T(8,128)(2,1)S(1)} %copy-done.10), custom_call_target="tpu_custom_call" | custom-call | flops 2415919104 | bytes 1572864 | tf_op jit(solution)/shard_map/pallas_call | solution.py:364
  52.4 6.6 %all-to-all-start.4 = ((bf16[64,32,384]{2,1,0:T(8,128)(2,1)}), bf16[64,32,384]{2,1,0:T(8,128)(2,1)S(1)}, u32[]{:S(2)}, u32[]{:S(2)}) async-start(bf16[64,32,384]{2,1,0:T(8,128)(2,1)} %bitcast.12), calls=%async_computation.4 | async-start | bytes 3145728 | tf_op jit(solution)/shard_map/all_to_all | solution.py:582
  59.0 1.5 shard_map.70
  60.5 0.0 copy-start.5
  60.5 69.7 %all-to-all-done.4 = bf16[64,32,384]{2,1,0:T(8,128)(2,1)S(1)} async-done(((bf16[64,32,384]{2,1,0:T(8,128)(2,1)}), bf16[64,32,384]{2,1,0:T(8,128)(2,1)S(1)}, u32[]{:S(2)}, u32[]{:S(2)}) %all-to-all-start.4) | async-done | bytes 1572896 | tf_op jit(solution)/shard_map/all_to_all | solution.py:582
  130.2 5.1 %shard_map.72 = bf16[2048,128]{1,0:T(8,128)(2,1)} custom-call(bf16[2048,128]{1,0:T(8,128)(2,1)S(1)} %get-tuple-element.77.query_ref, bf16[2048,128]{1,0:T(8,128)(2,1)S(1)} %get-tuple-element.78.key_ref, bf16[16,2048]{1,0:T(8,128)(2,1)S(1)} %get-tuple-element.79.member_ref, s32[8,128]{1,0:T(8,128)S(1)} %get-tuple-element.80.sums_row_ref, ...), custom_call_target="tpu_custom_call" | custom-call | flops 1073741824 | bytes 2097152 | tf_op jit(solution)/shard_map/pallas_call | solution.py:502
  135.3 0.0 copy-start.9
  135.3 0.0 copy-start.11
  135.3 10.8 %all-to-all-start.5 = ((bf16[64,32,128]{2,1,0:T(8,128)(2,1)}), bf16[64,32,128]{2,1,0:T(8,128)(2,1)S(1)}, u32[]{:S(2)}, u32[]{:S(2)}) async-start(bf16[64,32,128]{2,1,0:T(8,128)(2,1)} %bitcast.14), calls=%async_computation.5 | async-start | bytes 1048576 | tf_op jit(solution)/shard_map/all_to_all | solution.py:582
  146.1 0.2 copy.10
  146.3 28.7 %all-to-all-done.5 = bf16[64,32,128]{2,1,0:T(8,128)(2,1)S(1)} async-done(((bf16[64,32,128]{2,1,0:T(8,128)(2,1)}), bf16[64,32,128]{2,1,0:T(8,128)(2,1)S(1)}, u32[]{:S(2)}, u32[]{:S(2)}) %all-to-all-start.5) | async-done | bytes 524320 | tf_op jit(solution)/shard_map/all_to_all | solution.py:582
  175.0 2.7 %shard_map.73 = (bf16[8,96,256]{2,1,0:T(8,128)(2,1)}, f32[16,128]{1,0:T(8,128)S(1)}) custom-call(s32[768,2]{1,0:T(8,128)S(1)} %bitcast.35, s32[16,128]{1,0:T(8,128)S(1)} %get-tuple-element.74.sums_col_ref, f32[8,128]{1,0:T(8,128)S(1)} %get-tuple-element.75.first_ref, f32[8,128]{1,0:T(8,128)S(1)} %get-tuple-element.76.over_ref, bf16[2048,128]{1,0:T(8,128)(2,1)S(1)} %bitcast.34), custom_call_target="tpu_custom_call" | custom-call | flops 805306368 | bytes 524288 | tf_op jit(solution)/shard_map/pallas_call | solution.py:553
  177.7 9.8 %all-to-all-start.6 = ((bf16[8,96,256]{2,1,0:T(8,128)(2,1)}), bf16[8,96,256]{2,1,0:T(8,128)(2,1)S(1)}, u32[]{:S(2)}, u32[]{:S(2)}) async-start(bf16[8,96,256]{2,1,0:T(8,128)(2,1)} %get-tuple-element.81), calls=%async_computation.6 | async-start | bytes 786432 | tf_op jit(solution)/shard_map/all_to_all | solution.py:582
  187.5 8.1 %all-to-all-done.6 = bf16[8,96,256]{2,1,0:T(8,128)(2,1)S(1)} async-done(((bf16[8,96,256]{2,1,0:T(8,128)(2,1)}), bf16[8,96,256]{2,1,0:T(8,128)(2,1)S(1)}, u32[]{:S(2)}, u32[]{:S(2)}) %all-to-all-start.6) | async-done | bytes 393248 | tf_op jit(solution)/shard_map/all_to_all | solution.py:582
  195.6 0.6 compare_reduce_fusion
  196.9 0.0 all-gather.2.cloned.1.call-done
  196.9 0.0 copy-done.5
  196.9 0.0 copy-done.9
  196.9 0.0 copy-done.11
  197.0 5.2 %conditional.2 = (f32[8,256]{1,0:T(8,128)S(1)}, bf16[96,2048]{1,0:T(8,128)(2,1)S(1)}) conditional(s32[]{:T(128)} %convert_element_type.12, (bf16[2048,2048]{1,0:T(8,128)(2,1)}, bf16[8,96,256]{2,1,0:T(8,128)(2,1)S(1)}, f32[8,256]{1,0:T(8,128)S(1)}) %tuple.21, (bf16[64,1024]{1,0:T(8,128)(2,1)S(1)}, f32[2,512]{1,0:T(2,128)S(1)}, s32[2,768]{1,0:T(2,128)S(1)}, ...), branch_computations={%region_2.0_spmd, %region_3.0_spmd} | conditional | flops 32870275072 | bytes 104674680
  197.0 4.9 %fusion = bf16[96,2048]{1,0:T(8,128)(2,1)S(1)} fusion(bf16[8,96,256]{2,1,0:T(8,128)(2,1)S(1)} %get-tuple-element.25, bf16[8,256,2048]{2,1,0:T(8,128)(2,1)} %bitcast.37), kind=kOutput, calls=%fused_computation.1 | convolution fusion | flops 805502976 | bytes 9175040 | tf_op jit(solution)/shard_map/cond/branch_0_fun/gtd,gdn->tn/dot_general | solution.py:602
  202.1 0.0 copy-start.4
  202.1 0.0 copy-start.6
  202.1 0.7 copy-done.4
  202.9 0.0 copy-done.6
  (3 shorter events, 0.0 us)
Async XLA Ops:
  7.2 41.1 %copy-start.7 = (bf16[768,256]{1,0:T(8,128)(2,1)S(1)}, bf16[768,256]{1,0:T(8,128)(2,1)}, u32[]{:S(2)}) copy-start(bf16[768,256]{1,0:T(8,128)(2,1)} %q_ref.1) | copy-start | bytes 1179652
  7.2 41.1 %copy-start.8 = (bf16[768,256]{1,0:T(8,128)(2,1)S(1)}, bf16[768,256]{1,0:T(8,128)(2,1)}, u32[]{:S(2)}) copy-start(bf16[768,256]{1,0:T(8,128)(2,1)} %k_ref.1) | copy-start | bytes 1179652
  7.2 41.1 %copy-start.10 = (bf16[768,256]{1,0:T(8,128)(2,1)S(1)}, bf16[768,256]{1,0:T(8,128)(2,1)}, u32[]{:S(2)}) copy-start(bf16[768,256]{1,0:T(8,128)(2,1)} %v_ref.1) | copy-start | bytes 1179652
  7.2 189.7 %all-gather.2.cloned.1.call-start = ((), (), s32[]{:S(2)}) async-start(), calls=%async_computation.7 | async-start | bytes 9437184 | tf_op jit(solution)/shard_map/all_gather | solution.py:637
  9.2 34.2 %all-to-all-start.3 = ((bf16[64,8,128]{2,1,0:T(8,128)(2,1)}), bf16[64,8,128]{2,1,0:T(8,128)(2,1)S(1)}, u32[]{:S(2)}, u32[]{:S(2)}) async-start(bf16[64,8,128]{2,1,0:T(8,128)(2,1)} %get-tuple-element.68), calls=%async_computation.3 | async-start | bytes 262144 | tf_op jit(solution)/shard_map/all_to_all | solution.py:582
  52.4 77.8 %all-to-all-start.4 = ((bf16[64,32,384]{2,1,0:T(8,128)(2,1)}), bf16[64,32,384]{2,1,0:T(8,128)(2,1)S(1)}, u32[]{:S(2)}, u32[]{:S(2)}) async-start(bf16[64,32,384]{2,1,0:T(8,128)(2,1)} %bitcast.12), calls=%async_computation.4 | async-start | bytes 3145728 | tf_op jit(solution)/shard_map/all_to_all | solution.py:582
  60.5 136.4 %copy-start.5 = (s32[2,768]{1,0:T(2,128)S(1)}, s32[2,768]{1,0:T(2,128)}, u32[]{:S(2)}) copy-start(s32[2,768]{1,0:T(2,128)} %ids_ref.3) | copy-start | bytes 18436
  135.3 61.6 %copy-start.9 = (bf16[768,256]{1,0:T(8,128)(2,1)S(1)}, bf16[768,256]{1,0:T(8,128)(2,1)}, u32[]{:S(2)}) copy-start(bf16[768,256]{1,0:T(8,128)(2,1)} %k_ref.1) | copy-start | bytes 1179652
  135.3 61.6 %copy-start.11 = (bf16[768,256]{1,0:T(8,128)(2,1)S(1)}, bf16[768,256]{1,0:T(8,128)(2,1)}, u32[]{:S(2)}) copy-start(bf16[768,256]{1,0:T(8,128)(2,1)} %v_ref.1) | copy-start | bytes 1179652
  135.3 39.7 %all-to-all-start.5 = ((bf16[64,32,128]{2,1,0:T(8,128)(2,1)}), bf16[64,32,128]{2,1,0:T(8,128)(2,1)S(1)}, u32[]{:S(2)}, u32[]{:S(2)}) async-start(bf16[64,32,128]{2,1,0:T(8,128)(2,1)} %bitcast.14), calls=%async_computation.5 | async-start | bytes 1048576 | tf_op jit(solution)/shard_map/all_to_all | solution.py:582
  177.7 17.9 %all-to-all-start.6 = ((bf16[8,96,256]{2,1,0:T(8,128)(2,1)}), bf16[8,96,256]{2,1,0:T(8,128)(2,1)S(1)}, u32[]{:S(2)}, u32[]{:S(2)}) async-start(bf16[8,96,256]{2,1,0:T(8,128)(2,1)} %get-tuple-element.81), calls=%async_computation.6 | async-start | bytes 786432 | tf_op jit(solution)/shard_map/all_to_all | solution.py:582
  202.1 0.7 copy-start.4
  202.1 0.7 copy-start.6
Sparse Core Ops, SparseCore 0:
  10.2 63.0 all-gather.1

commit v10 on v8

--- a/solution.py
+++ b/solution.py
@@ -406,7 +406,8 @@
     unit = key_float * lax.rsqrt(jnp.sum(key_float * key_float, axis=1, keepdims=True) + 1e-06)
     high = unit.astype(BF16)
     low = (unit - high.astype(F32)).astype(BF16)
-    return (dot(member, high) + dot(member, low)).astype(BF16)
+    halves = dot(member, jnp.concatenate([high, low], axis=1))
+    return (halves[:, 0 : high.shape[1]] + halves[:, high.shape[1] :]).astype(BF16)
 
 
 def fill(query_ref, key_ref, member_ref, x_ref, query_scr, key_scr, value_scr):

time: 210 us -> 211 us (level)
  no operation moved by 1% of the time
where the time goes in v10:
time: 211 us; the launch traced here: 210 us
  waiting for transfers between devices  121 us (57%)
  starting transfers between devices  45.4 us (22%)
  Pallas kernels  20.6 us (10%)
  between operations  14.9 us (7%)
  matrix products  4.87 us (2%)
  other arithmetic  2.47 us (1%)
    all_to_all x4, waiting for transfers between devices, exchange(): return lax.all_to_all(rows, axis, split_axis=0, concat_axis=0, tiled=True)  121 us
    all_to_all x4, starting transfers between devices, exchange(): return lax.all_to_all(rows, axis, split_axis=0, concat_axis=0, tiled=True)  45.4 us
    pallas_call x1, Pallas kernels, make_plan(): pl.pallas_call(functools.partial(plan_kernel, room), out_shape=(jax.Shape...  5.26 us
    pallas_call x1, Pallas kernels, attend(): pl.pallas_call(attend_kernel, out_shape=shape, scratch_shapes=filled, com...  4.96 us
    dot_general x1, matrix products, project(): total = jnp.einsum('gtd,gdn->tn', parts, weight, preferred_element_type=F32)  4.87 us
  transfers between devices with their start and end apart: 5, of which 4 were waited for; matrix products, arithmetic and copies ran while one was open for 1% of the time, Pallas kernels for 9%

profile of v10, /device:TPU:1, one launch (start us, length us, event | category | flops | bytes accessed | tf_op | source)
XLA Modules:
  0.0 210.3 jit_solution(8300245505763276922)
XLA Ops:
  7.2 0.0 copy-start.7
  7.2 0.0 copy-start.8
  7.2 0.0 copy-start.10
  7.2 0.0 all-gather.2.cloned.1.call-start
  7.2 2.0 shard_map.68
  9.2 0.0 all-gather.2.cloned.1.call-update
  9.2 19.3 %all-to-all-start.3 = ((bf16[64,8,128]{2,1,0:T(8,128)(2,1)}), bf16[64,8,128]{2,1,0:T(8,128)(2,1)S(1)}, u32[]{:S(2)}, u32[]{:S(2)}) async-start(bf16[64,8,128]{2,1,0:T(8,128)(2,1)} %get-tuple-element.68), calls=%async_computation.3 | async-start | bytes 262144 | tf_op jit(solution)/shard_map/all_to_all | solution.py:583
  28.5 0.2 iota_compare_fusion
  28.7 1.6 convert_reduce_fusion.rank_ref
  30.4 13.1 %all-to-all-done.3 = bf16[64,8,128]{2,1,0:T(8,128)(2,1)S(1)} async-done(((bf16[64,8,128]{2,1,0:T(8,128)(2,1)}), bf16[64,8,128]{2,1,0:T(8,128)(2,1)S(1)}, u32[]{:S(2)}, u32[]{:S(2)}) %all-to-all-start.3) | async-done | bytes 131104 | tf_op jit(solution)/shard_map/all_to_all | solution.py:583
  43.5 5.3 %shard_map.69 = (s32[2,768]{1,0:T(2,128)S(1)}, s32[8,512]{1,0:T(8,128)S(1)}, s32[512,128]{1,0:T(8,128)S(1)}, f32[8,128]{1,0:T(8,128)S(1)}, f32[8,128]{1,0:T(8,128)S(1)}) custom-call(bf16[64,1024]{1,0:T(8,128)(2,1)S(1)} %bitcast.40, f32[2,512]{1,0:T(2,128)S(1)} %get-tuple-element.70.own_ref, s32[2,768]{1,0:T(2,128)} %ids_ref.3, ...), custom_call_target="tpu_custom_call" | custom-call | flops 1000000000 | bytes 1000000 | tf_op jit(solution)/shard_map/pallas_call | solution.py:291
  48.7 0.0 copy-done.7
  48.7 0.0 copy-done.8
  48.8 0.0 copy-done.10
  48.8 4.1 %shard_map.71 = bf16[2048,384]{1,0:T(8,128)(2,1)} custom-call(s32[2,768]{1,0:T(2,128)S(1)} %get-tuple-element.71.place_ref, f32[8,128]{1,0:T(8,128)S(1)} %get-tuple-element.75.first_ref, bf16[768,256]{1,0:T(8,128)(2,1)S(1)} %copy-done.7, bf16[768,256]{1,0:T(8,128)(2,1)S(1)} %copy-done.8, bf16[768,256]{1,0:T(8,128)(2,1)S(1)} %copy-done.10), custom_call_target="tpu_custom_call" | custom-call | flops 2415919104 | bytes 1572864 | tf_op jit(solution)/shard_map/pallas_call | solution.py:364
  52.9 6.6 %all-to-all-start.4 = ((bf16[64,32,384]{2,1,0:T(8,128)(2,1)}), bf16[64,32,384]{2,1,0:T(8,128)(2,1)S(1)}, u32[]{:S(2)}, u32[]{:S(2)}) async-start(bf16[64,32,384]{2,1,0:T(8,128)(2,1)} %bitcast.12), calls=%async_computation.4 | async-start | bytes 3145728 | tf_op jit(solution)/shard_map/all_to_all | solution.py:583
  59.5 1.5 shard_map.70
  61.0 0.0 copy-start.5
  61.0 70.9 %all-to-all-done.4 = bf16[64,32,384]{2,1,0:T(8,128)(2,1)S(1)} async-done(((bf16[64,32,384]{2,1,0:T(8,128)(2,1)}), bf16[64,32,384]{2,1,0:T(8,128)(2,1)S(1)}, u32[]{:S(2)}, u32[]{:S(2)}) %all-to-all-start.4) | async-done | bytes 1572896 | tf_op jit(solution)/shard_map/all_to_all | solution.py:583
  131.9 5.0 %shard_map.72 = bf16[2048,128]{1,0:T(8,128)(2,1)} custom-call(bf16[2048,128]{1,0:T(8,128)(2,1)S(1)} %get-tuple-element.77.query_ref, bf16[2048,128]{1,0:T(8,128)(2,1)S(1)} %get-tuple-element.78.key_ref, bf16[16,2048]{1,0:T(8,128)(2,1)S(1)} %get-tuple-element.79.member_ref, s32[8,128]{1,0:T(8,128)S(1)} %get-tuple-element.80.sums_row_ref, ...), custom_call_target="tpu_custom_call" | custom-call | flops 1073741824 | bytes 2097152 | tf_op jit(solution)/shard_map/pallas_call | solution.py:503
  136.9 0.0 copy-start.9
  136.9 0.0 copy-start.11
  136.9 10.0 %all-to-all-start.5 = ((bf16[64,32,128]{2,1,0:T(8,128)(2,1)}), bf16[64,32,128]{2,1,0:T(8,128)(2,1)S(1)}, u32[]{:S(2)}, u32[]{:S(2)}) async-start(bf16[64,32,128]{2,1,0:T(8,128)(2,1)} %bitcast.14), calls=%async_computation.5 | async-start | bytes 1048576 | tf_op jit(solution)/shard_map/all_to_all | solution.py:583
  146.8 0.2 copy.10
  147.0 28.7 %all-to-all-done.5 = bf16[64,32,128]{2,1,0:T(8,128)(2,1)S(1)} async-done(((bf16[64,32,128]{2,1,0:T(8,128)(2,1)}), bf16[64,32,128]{2,1,0:T(8,128)(2,1)S(1)}, u32[]{:S(2)}, u32[]{:S(2)}) %all-to-all-start.5) | async-done | bytes 524320 | tf_op jit(solution)/shard_map/all_to_all | solution.py:583
  175.7 2.9 %shard_map.73 = (bf16[8,96,256]{2,1,0:T(8,128)(2,1)}, f32[16,128]{1,0:T(8,128)S(1)}) custom-call(s32[768,2]{1,0:T(8,128)S(1)} %bitcast.35, s32[16,128]{1,0:T(8,128)S(1)} %get-tuple-element.74.sums_col_ref, f32[8,128]{1,0:T(8,128)S(1)} %get-tuple-element.75.first_ref, f32[8,128]{1,0:T(8,128)S(1)} %get-tuple-element.76.over_ref, bf16[2048,128]{1,0:T(8,128)(2,1)S(1)} %bitcast.34), custom_call_target="tpu_custom_call" | custom-call | flops 805306368 | bytes 524288 | tf_op jit(solution)/shard_map/pallas_call | solution.py:554
  178.6 9.6 %all-to-all-start.6 = ((bf16[8,96,256]{2,1,0:T(8,128)(2,1)}), bf16[8,96,256]{2,1,0:T(8,128)(2,1)S(1)}, u32[]{:S(2)}, u32[]{:S(2)}) async-start(bf16[8,96,256]{2,1,0:T(8,128)(2,1)} %get-tuple-element.81), calls=%async_computation.6 | async-start | bytes 786432 | tf_op jit(solution)/shard_map/all_to_all | solution.py:583
  188.2 8.1 %all-to-all-done.6 = bf16[8,96,256]{2,1,0:T(8,128)(2,1)S(1)} async-done(((bf16[8,96,256]{2,1,0:T(8,128)(2,1)}), bf16[8,96,256]{2,1,0:T(8,128)(2,1)S(1)}, u32[]{:S(2)}, u32[]{:S(2)}) %all-to-all-start.6) | async-done | bytes 393248 | tf_op jit(solution)/shard_map/all_to_all | solution.py:583
  196.2 0.6 compare_reduce_fusion
  197.5 0.0 all-gather.2.cloned.1.call-done
  197.6 0.0 copy-done.5
  197.6 0.0 copy-done.9
  197.6 0.0 copy-done.11
  197.6 5.2 %conditional.2 = (f32[8,256]{1,0:T(8,128)S(1)}, bf16[96,2048]{1,0:T(8,128)(2,1)S(1)}) conditional(s32[]{:T(128)} %convert_element_type.12, (bf16[2048,2048]{1,0:T(8,128)(2,1)}, bf16[8,96,256]{2,1,0:T(8,128)(2,1)S(1)}, f32[8,256]{1,0:T(8,128)S(1)}) %tuple.21, (bf16[64,1024]{1,0:T(8,128)(2,1)S(1)}, f32[2,512]{1,0:T(2,128)S(1)}, s32[2,768]{1,0:T(2,128)S(1)}, ...), branch_computations={%region_2.0_spmd, %region_3.0_spmd} | conditional | flops 32870275072 | bytes 104674680
  197.6 4.9 %fusion = bf16[96,2048]{1,0:T(8,128)(2,1)S(1)} fusion(bf16[8,96,256]{2,1,0:T(8,128)(2,1)S(1)} %get-tuple-element.25, bf16[8,256,2048]{2,1,0:T(8,128)(2,1)} %bitcast.37), kind=kOutput, calls=%fused_computation.1 | convolution fusion | flops 805502976 | bytes 9175040 | tf_op jit(solution)/shard_map/cond/branch_0_fun/gtd,gdn->tn/dot_general | solution.py:603
  202.7 0.0 copy-start.4
  202.8 0.0 copy-start.6
  202.8 0.7 copy-done.4
  203.5 0.0 copy-done.6
  (3 shorter events, 0.0 us)
Async XLA Ops:
  7.2 41.6 %copy-start.7 = (bf16[768,256]{1,0:T(8,128)(2,1)S(1)}, bf16[768,256]{1,0:T(8,128)(2,1)}, u32[]{:S(2)}) copy-start(bf16[768,256]{1,0:T(8,128)(2,1)} %q_ref.1) | copy-start | bytes 1179652
  7.2 41.6 %copy-start.8 = (bf16[768,256]{1,0:T(8,128)(2,1)S(1)}, bf16[768,256]{1,0:T(8,128)(2,1)}, u32[]{:S(2)}) copy-start(bf16[768,256]{1,0:T(8,128)(2,1)} %k_ref.1) | copy-start | bytes 1179652
  7.2 41.6 %copy-start.10 = (bf16[768,256]{1,0:T(8,128)(2,1)S(1)}, bf16[768,256]{1,0:T(8,128)(2,1)}, u32[]{:S(2)}) copy-start(bf16[768,256]{1,0:T(8,128)(2,1)} %v_ref.1) | copy-start | bytes 1179652
  7.2 190.4 %all-gather.2.cloned.1.call-start = ((), (), s32[]{:S(2)}) async-start(), calls=%async_computation.7 | async-start | bytes 9437184 | tf_op jit(solution)/shard_map/all_gather | solution.py:638
  9.2 34.2 %all-to-all-start.3 = ((bf16[64,8,128]{2,1,0:T(8,128)(2,1)}), bf16[64,8,128]{2,1,0:T(8,128)(2,1)S(1)}, u32[]{:S(2)}, u32[]{:S(2)}) async-start(bf16[64,8,128]{2,1,0:T(8,128)(2,1)} %get-tuple-element.68), calls=%async_computation.3 | async-start | bytes 262144 | tf_op jit(solution)/shard_map/all_to_all | solution.py:583
  52.9 79.0 %all-to-all-start.4 = ((bf16[64,32,384]{2,1,0:T(8,128)(2,1)}), bf16[64,32,384]{2,1,0:T(8,128)(2,1)S(1)}, u32[]{:S(2)}, u32[]{:S(2)}) async-start(bf16[64,32,384]{2,1,0:T(8,128)(2,1)} %bitcast.12), calls=%async_computation.4 | async-start | bytes 3145728 | tf_op jit(solution)/shard_map/all_to_all | solution.py:583
  61.0 136.6 %copy-start.5 = (s32[2,768]{1,0:T(2,128)S(1)}, s32[2,768]{1,0:T(2,128)}, u32[]{:S(2)}) copy-start(s32[2,768]{1,0:T(2,128)} %ids_ref.3) | copy-start | bytes 18436
  136.9 60.7 %copy-start.9 = (bf16[768,256]{1,0:T(8,128)(2,1)S(1)}, bf16[768,256]{1,0:T(8,128)(2,1)}, u32[]{:S(2)}) copy-start(bf16[768,256]{1,0:T(8,128)(2,1)} %k_ref.1) | copy-start | bytes 1179652
  136.9 60.7 %copy-start.11 = (bf16[768,256]{1,0:T(8,128)(2,1)S(1)}, bf16[768,256]{1,0:T(8,128)(2,1)}, u32[]{:S(2)}) copy-start(bf16[768,256]{1,0:T(8,128)(2,1)} %v_ref.1) | copy-start | bytes 1179652
  136.9 38.9 %all-to-all-start.5 = ((bf16[64,32,128]{2,1,0:T(8,128)(2,1)}), bf16[64,32,128]{2,1,0:T(8,128)(2,1)S(1)}, u32[]{:S(2)}, u32[]{:S(2)}) async-start(bf16[64,32,128]{2,1,0:T(8,128)(2,1)} %bitcast.14), calls=%async_computation.5 | async-start | bytes 1048576 | tf_op jit(solution)/shard_map/all_to_all | solution.py:583
  178.6 17.6 %all-to-all-start.6 = ((bf16[8,96,256]{2,1,0:T(8,128)(2,1)}), bf16[8,96,256]{2,1,0:T(8,128)(2,1)S(1)}, u32[]{:S(2)}, u32[]{:S(2)}) async-start(bf16[8,96,256]{2,1,0:T(8,128)(2,1)} %get-tuple-element.81), calls=%async_computation.6 | async-start | bytes 786432 | tf_op jit(solution)/shard_map/all_to_all | solution.py:583
  202.7 0.7 copy-start.4
  202.8 0.7 copy-start.6
Sparse Core Ops, SparseCore 0:
  10.2 63.0 all-gather.1
